TPU v7x, 32 devices: a whole 2x2x4 slice. The times are simulated.
32 devices in a mesh: dp: 2 (over core), fsdp: 16 (over z, y, x).
Axes of the slice: x: 2, y: 2, z: 4, core: 2. Of those that a mesh axis runs over, the one named last changes fastest.
Arguments:
- tokens: bfloat16 [65536, 768], P(('dp', 'fsdp')), may hold values from -6 to 6
- sensor_tag: int32 [64], P(('dp', 'fsdp')), may hold values from 0 to 1
- owner_order: int32 [32, 2048], P(('dp', 'fsdp')), may hold values from 0 to 2047, each once within a row
- ln1_gain: bfloat16 [768], P('fsdp'), may hold values from 0.25 to 1.75
- ln1_bias: bfloat16 [768], P('fsdp'), may hold values from -3 to 3
- w_qkv: bfloat16 [768, 2304], P('fsdp'), may hold values from -0.21875 to 0.21875
- b_query: bfloat16 [768], P('fsdp'), may hold values from -4 to 4
- b_value: bfloat16 [768], P('fsdp'), may hold values from -4 to 4
- w_out: bfloat16 [768, 768], P('fsdp'), may hold values from -0.625 to 0.625
- b_out: bfloat16 [768], P('fsdp'), may hold values from -3 to 3
- ln2_gain: bfloat16 [768], P('fsdp'), may hold values from 0.25 to 1.75
- ln2_bias: bfloat16 [768], P('fsdp'), may hold values from -3 to 3
- w_up: bfloat16 [768, 3072], P('fsdp'), may hold values from -0.21875 to 0.21875
- b_up: bfloat16 [3072], P('fsdp'), may hold values from -4 to 4
- w_down: bfloat16 [3072, 768], P('fsdp'), may hold values from -0.109375 to 0.109375
- b_down: bfloat16 [768], P('fsdp'), may hold values from -3 to 3
- out_grad: float32 [65536, 768], P(('dp', 'fsdp')), may hold values from -6 to 6
Outputs:
- encoded: float32 [65536, 768], P(('dp', 'fsdp'))
- tokens_grad: float32 [65536, 768], P(('dp', 'fsdp'))
- grad_ln1_gain: float32 [768], P('fsdp')
- grad_ln1_bias: float32 [768], P('fsdp')
- grad_w_qkv: float32 [768, 2304], P('fsdp')
- grad_b_query: float32 [768], P('fsdp')
- grad_b_value: float32 [768], P('fsdp')
- grad_w_out: float32 [768, 768], P('fsdp')
- grad_b_out: float32 [768], P('fsdp')
- grad_ln2_gain: float32 [768], P('fsdp')
- grad_ln2_bias: float32 [768], P('fsdp')
- grad_w_up: float32 [768, 3072], P('fsdp')
- grad_b_up: float32 [3072], P('fsdp')
- grad_w_down: float32 [3072, 768], P('fsdp')
- grad_b_down: float32 [768], P('fsdp')
Inputs may be any that keep to these rules, and one draw needn't show every extreme that they name: `sensor_tag`: 0 marks a row holding one chip of 1024 tokens, 1 a row of four chips of 256 tokens. `owner_order`: each row is a permutation of 0 to 2047.
All inputs are finite; a program needn't handle non-finite values.
Results may differ from a plain program's by a relative error of at most 0.025.
Values may be sent and summed in bfloat16 or wider, within the bound.
No kernel may reach another device: no remote copies, remote signals or barrier semaphores. Data moves between devices by JAX's collectives and lax.ppermute only.
A program may use at most 320 MiB of HBM per device.

v0:
```python
import jax
import jax.numpy as jnp
from jax import lax
from jax.sharding import PartitionSpec as P

HEADS = 12
HEAD_DIM = 64
ROW_LEN = 1024


norm_eps = 1e-06
masked_score = -1e30


def norm_rows(values, gain_vec, shift_vec):
    center = values - jnp.mean(values, axis=-1, keepdims=True)
    spread = jnp.mean(center * center, axis=-1, keepdims=True)
    return center * lax.rsqrt(spread + norm_eps) * gain_vec + shift_vec


def norm_back(values, gain_vec, upstream):
    zero_shift = jnp.zeros_like(gain_vec)
    _, pull_back = jax.vjp(norm_rows, values, gain_vec, zero_shift)
    return pull_back(upstream)


def block_mask(tag_value, block_start, block_len, length):
    chip_len = jnp.where(tag_value == 0, length, length // 4)
    query_pos = block_start + jnp.arange(block_len, dtype=jnp.int32)
    key_pos = jnp.arange(length, dtype=jnp.int32)
    return query_pos[:, None] // chip_len == key_pos[None, :] // chip_len


def attend_forward(queries, key_rows, value_rows, sensor_tag):
    rows_here = sensor_tag.shape[0]
    length = ROW_LEN
    block_len = min(512, length)
    per_row = length // block_len
    shape_four = (rows_here, length, HEADS, HEAD_DIM)
    query_four = queries.reshape(shape_four)
    key_four = key_rows.reshape(shape_four)
    value_four = value_rows.reshape(shape_four)

    def attend_one_block(block_index):
        row_at = block_index // per_row
        block_start = block_index % per_row * block_len
        query_block = lax.dynamic_slice_in_dim(query_four[row_at], block_start, block_len, 0)
        scores = jnp.einsum(
            "qhe,khe->hqk", query_block, key_four[row_at], preferred_element_type=jnp.float32
        )
        allowed = block_mask(sensor_tag[row_at], block_start, block_len, length)
        scores = jnp.where(allowed[None], scores, masked_score)
        row_peak = jnp.max(scores, axis=-1, keepdims=True)
        weights = jnp.exp(scores - row_peak)
        row_total = jnp.sum(weights, axis=-1, keepdims=True)
        soft_weights = (weights / row_total).astype(jnp.bfloat16)
        mixed_block = jnp.einsum(
            "hqk,khe->qhe", soft_weights, value_four[row_at], preferred_element_type=jnp.float32
        )
        return (mixed_block.astype(jnp.bfloat16), (row_peak + jnp.log(row_total))[..., 0])

    mixed_all, log_totals = lax.map(
        attend_one_block, jnp.arange(rows_here * per_row, dtype=jnp.int32)
    )
    return (mixed_all.reshape(rows_here * length, HEADS * HEAD_DIM), log_totals)


def attend_backward(queries, key_rows, value_rows, mixed_grad, log_totals, sensor_tag):
    rows_here = sensor_tag.shape[0]
    length = ROW_LEN
    block_len = min(512, length)
    per_row = length // block_len
    shape_four = (rows_here, length, HEADS, HEAD_DIM)
    query_four = queries.reshape(shape_four)
    key_four = key_rows.reshape(shape_four)
    value_four = value_rows.reshape(shape_four)
    grad_four = mixed_grad.reshape(shape_four)

    def one_row(row_at):

        def one_one_block(carried, block_at):
            block_start = block_at * block_len
            query_block = lax.dynamic_slice_in_dim(query_four[row_at], block_start, block_len, 0)
            grad_block = lax.dynamic_slice_in_dim(grad_four[row_at], block_start, block_len, 0)
            scores = jnp.einsum(
                "qhe,khe->hqk", query_block, key_four[row_at], preferred_element_type=jnp.float32
            )
            allowed = block_mask(sensor_tag[row_at], block_start, block_len, length)
            lse_block = log_totals[row_at * per_row + block_at]
            soft = jnp.where(allowed[None], jnp.exp(scores - lse_block[..., None]), 0.0)
            value_part = jnp.einsum(
                "hqk,qhe->khe",
                soft.astype(jnp.bfloat16),
                grad_block,
                preferred_element_type=jnp.float32,
            )
            prob_grad = jnp.einsum(
                "qhe,khe->hqk", grad_block, value_four[row_at], preferred_element_type=jnp.float32
            )
            inner_sum = jnp.sum(prob_grad * soft, axis=-1, keepdims=True)
            score_grad = (soft * (prob_grad - inner_sum)).astype(jnp.bfloat16)
            query_part = jnp.einsum(
                "hqk,khe->qhe", score_grad, key_four[row_at], preferred_element_type=jnp.float32
            )
            key_part = jnp.einsum(
                "hqk,qhe->khe", score_grad, query_block, preferred_element_type=jnp.float32
            )
            return (
                (carried[0] + key_part, carried[1] + value_part),
                query_part.astype(jnp.bfloat16),
            )

        zero_rows = jnp.zeros((length, HEADS, HEAD_DIM), jnp.float32)
        (key_sum, value_sum), query_parts = lax.scan(
            one_one_block, (zero_rows, zero_rows), jnp.arange(per_row, dtype=jnp.int32)
        )
        return (
            query_parts.reshape(length, HEADS, HEAD_DIM),
            key_sum.astype(jnp.bfloat16),
            value_sum.astype(jnp.bfloat16),
        )

    query_grad, key_grad, value_grad = lax.map(one_row, jnp.arange(rows_here, dtype=jnp.int32))
    flat_shape = (rows_here * length, HEADS * HEAD_DIM)
    return (
        query_grad.reshape(flat_shape),
        key_grad.reshape(flat_shape),
        value_grad.reshape(flat_shape),
    )


def local(
    tokens,
    sensor_tag,
    owner_order,
    ln1_gain,
    ln1_bias,
    w_qkv,
    b_query,
    b_value,
    w_out,
    b_out,
    ln2_gain,
    ln2_bias,
    w_up,
    b_up,
    w_down,
    b_down,
    out_grad,
):
    model_width = HEADS * HEAD_DIM
    score_scale = HEAD_DIM ** (-0.5)
    gathered = (
        lax.all_gather(ln1_gain, "fsdp", axis=0, tiled=True),
        lax.all_gather(ln1_bias, "fsdp", axis=0, tiled=True),
        lax.all_gather(w_qkv, "fsdp", axis=0, tiled=True),
        lax.all_gather(b_query, "fsdp", axis=0, tiled=True),
        lax.all_gather(b_value, "fsdp", axis=0, tiled=True),
        lax.all_gather(w_out, "fsdp", axis=0, tiled=True),
        lax.all_gather(b_out, "fsdp", axis=0, tiled=True),
        lax.all_gather(ln2_gain, "fsdp", axis=0, tiled=True),
        lax.all_gather(ln2_bias, "fsdp", axis=0, tiled=True),
        lax.all_gather(w_up, "fsdp", axis=0, tiled=True),
        lax.all_gather(b_up, "fsdp", axis=0, tiled=True),
        lax.all_gather(w_down, "fsdp", axis=0, tiled=True),
        lax.all_gather(b_down, "fsdp", axis=0, tiled=True),
    )
    (
        gain_one,
        shift_one,
        full_qkv,
        query_bias,
        value_bias,
        full_out,
        out_bias,
        gain_two,
        shift_two,
        full_up,
        up_bias,
        full_down,
        down_bias,
    ) = gathered
    stream = tokens.astype(jnp.float32)
    normed = norm_rows(stream, gain_one.astype(jnp.float32), shift_one.astype(jnp.float32)).astype(
        jnp.bfloat16
    )
    joined = jnp.dot(normed, full_qkv, preferred_element_type=jnp.float32)
    queries = ((joined[:, :model_width] + query_bias.astype(jnp.float32)) * score_scale).astype(
        jnp.bfloat16
    )
    key_rows = joined[:, model_width : 2 * model_width].astype(jnp.bfloat16)
    value_rows = (joined[:, 2 * model_width :] + value_bias.astype(jnp.float32)).astype(
        jnp.bfloat16
    )
    mixed_heads, log_totals = attend_forward(queries, key_rows, value_rows, sensor_tag)
    middle = (
        stream
        + jnp.dot(mixed_heads, full_out, preferred_element_type=jnp.float32)
        + out_bias.astype(jnp.float32)
    )
    normed_two = norm_rows(
        middle, gain_two.astype(jnp.float32), shift_two.astype(jnp.float32)
    ).astype(jnp.bfloat16)
    hidden = jnp.dot(normed_two, full_up, preferred_element_type=jnp.float32) + up_bias.astype(
        jnp.float32
    )
    active = jax.nn.gelu(hidden, approximate=False).astype(jnp.bfloat16)
    encoded_rows = (
        middle
        + jnp.dot(active, full_down, preferred_element_type=jnp.float32)
        + down_bias.astype(jnp.float32)
    )
    slot_order = owner_order[0]
    encoded = lax.all_to_all(
        encoded_rows[slot_order].astype(jnp.bfloat16),
        "fsdp",
        split_axis=0,
        concat_axis=0,
        tiled=True,
    ).astype(jnp.float32)
    back_qkv, back_out, back_up, back_down, back_gain_one, back_gain_two = (
        lax.all_gather(w_qkv, "fsdp", axis=0, tiled=True),
        lax.all_gather(w_out, "fsdp", axis=0, tiled=True),
        lax.all_gather(w_up, "fsdp", axis=0, tiled=True),
        lax.all_gather(w_down, "fsdp", axis=0, tiled=True),
        lax.all_gather(ln1_gain, "fsdp", axis=0, tiled=True),
        lax.all_gather(ln2_gain, "fsdp", axis=0, tiled=True),
    )
    returned = lax.all_to_all(
        out_grad.astype(jnp.bfloat16), "fsdp", split_axis=0, concat_axis=0, tiled=True
    ).astype(out_grad.dtype)
    layer_grad = jnp.zeros_like(returned).at[slot_order].set(returned)
    down_in = layer_grad.astype(jnp.bfloat16)
    grad_down = jnp.einsum("tf,td->fd", active, down_in, preferred_element_type=jnp.float32)
    grad_down_bias = jnp.sum(down_in.astype(jnp.float32), axis=0)
    active_grad = jnp.einsum("td,fd->tf", down_in, back_down, preferred_element_type=jnp.float32)
    _, gelu_pull = jax.vjp(lambda inner_rows: jax.nn.gelu(inner_rows, approximate=False), hidden)
    hidden_grad = gelu_pull(active_grad)[0].astype(jnp.bfloat16)
    grad_up = jnp.einsum("td,tf->df", normed_two, hidden_grad, preferred_element_type=jnp.float32)
    grad_up_bias = jnp.sum(hidden_grad.astype(jnp.float32), axis=0)
    normed_two_grad = jnp.einsum(
        "tf,df->td", hidden_grad, back_up, preferred_element_type=jnp.float32
    )
    middle_part, grad_gain_two, grad_shift_two = norm_back(
        middle, back_gain_two.astype(jnp.float32), normed_two_grad
    )
    middle_grad = layer_grad + middle_part
    branch_in = middle_grad.astype(jnp.bfloat16)
    grad_out = jnp.einsum("td,te->de", mixed_heads, branch_in, preferred_element_type=jnp.float32)
    grad_out_bias = jnp.sum(branch_in.astype(jnp.float32), axis=0)
    mixed_grad = jnp.einsum(
        "te,de->td", branch_in, back_out, preferred_element_type=jnp.float32
    ).astype(jnp.bfloat16)
    query_grad, key_grad, value_grad = attend_backward(
        queries, key_rows, value_rows, mixed_grad, log_totals, sensor_tag
    )
    query_scaled = query_grad * jnp.asarray(score_scale, jnp.bfloat16)
    joined_grad = jnp.concatenate([query_scaled, key_grad, value_grad], axis=1)
    grad_qkv = jnp.einsum("td,te->de", normed, joined_grad, preferred_element_type=jnp.float32)
    grad_query_bias = jnp.sum(query_scaled.astype(jnp.float32), axis=0)
    grad_value_bias = jnp.sum(value_grad.astype(jnp.float32), axis=0)
    normed_grad = jnp.einsum("te,de->td", joined_grad, back_qkv, preferred_element_type=jnp.float32)
    stream_part, grad_gain_one, grad_shift_one = norm_back(
        stream, back_gain_one.astype(jnp.float32), normed_grad
    )
    tokens_grad = middle_grad + stream_part
    all_shares = (
        lax.psum_scatter(
            grad_gain_one.astype(jnp.bfloat16), "fsdp", scatter_dimension=0, tiled=True
        ).astype(jnp.float32),
        lax.psum_scatter(
            grad_shift_one.astype(jnp.bfloat16), "fsdp", scatter_dimension=0, tiled=True
        ).astype(jnp.float32),
        lax.psum_scatter(
            grad_qkv.astype(jnp.bfloat16), "fsdp", scatter_dimension=0, tiled=True
        ).astype(jnp.float32),
        lax.psum_scatter(
            grad_query_bias.astype(jnp.bfloat16), "fsdp", scatter_dimension=0, tiled=True
        ).astype(jnp.float32),
        lax.psum_scatter(
            grad_value_bias.astype(jnp.bfloat16), "fsdp", scatter_dimension=0, tiled=True
        ).astype(jnp.float32),
        lax.psum_scatter(
            grad_out.astype(jnp.bfloat16), "fsdp", scatter_dimension=0, tiled=True
        ).astype(jnp.float32),
        lax.psum_scatter(
            grad_out_bias.astype(jnp.bfloat16), "fsdp", scatter_dimension=0, tiled=True
        ).astype(jnp.float32),
        lax.psum_scatter(
            grad_gain_two.astype(jnp.bfloat16), "fsdp", scatter_dimension=0, tiled=True
        ).astype(jnp.float32),
        lax.psum_scatter(
            grad_shift_two.astype(jnp.bfloat16), "fsdp", scatter_dimension=0, tiled=True
        ).astype(jnp.float32),
        lax.psum_scatter(
            grad_up.astype(jnp.bfloat16), "fsdp", scatter_dimension=0, tiled=True
        ).astype(jnp.float32),
        lax.psum_scatter(
            grad_up_bias.astype(jnp.bfloat16), "fsdp", scatter_dimension=0, tiled=True
        ).astype(jnp.float32),
        lax.psum_scatter(
            grad_down.astype(jnp.bfloat16), "fsdp", scatter_dimension=0, tiled=True
        ).astype(jnp.float32),
        lax.psum_scatter(
            grad_down_bias.astype(jnp.bfloat16), "fsdp", scatter_dimension=0, tiled=True
        ).astype(jnp.float32),
    )
    totals = tuple(
        (
            lax.psum(all_shares[0].astype(jnp.bfloat16), "dp").astype(jnp.float32),
            lax.psum(all_shares[1].astype(jnp.bfloat16), "dp").astype(jnp.float32),
            lax.psum(all_shares[2].astype(jnp.bfloat16), "dp").astype(jnp.float32),
            lax.psum(all_shares[3].astype(jnp.bfloat16), "dp").astype(jnp.float32),
            lax.psum(all_shares[4].astype(jnp.bfloat16), "dp").astype(jnp.float32),
            lax.psum(all_shares[5].astype(jnp.bfloat16), "dp").astype(jnp.float32),
            lax.psum(all_shares[6].astype(jnp.bfloat16), "dp").astype(jnp.float32),
            lax.psum(all_shares[7].astype(jnp.bfloat16), "dp").astype(jnp.float32),
            lax.psum(all_shares[8].astype(jnp.bfloat16), "dp").astype(jnp.float32),
            lax.psum(all_shares[9].astype(jnp.bfloat16), "dp").astype(jnp.float32),
            lax.psum(all_shares[10].astype(jnp.bfloat16), "dp").astype(jnp.float32),
            lax.psum(all_shares[11].astype(jnp.bfloat16), "dp").astype(jnp.float32),
            lax.psum(all_shares[12].astype(jnp.bfloat16), "dp").astype(jnp.float32),
        )
    )
    return (
        encoded,
        tokens_grad,
        totals[0],
        totals[1],
        totals[2],
        totals[3],
        totals[4],
        totals[5],
        totals[6],
        totals[7],
        totals[8],
        totals[9],
        totals[10],
        totals[11],
        totals[12],
    )


def solution(mesh):
    in_specs = (
        P(("dp", "fsdp"), None),
        P(("dp", "fsdp")),
        P(("dp", "fsdp"), None),
        P("fsdp"),
        P("fsdp"),
        P("fsdp", None),
        P("fsdp"),
        P("fsdp"),
        P("fsdp", None),
        P("fsdp"),
        P("fsdp"),
        P("fsdp"),
        P("fsdp", None),
        P("fsdp"),
        P("fsdp", None),
        P("fsdp"),
        P(("dp", "fsdp"), None),
    )
    out_specs = (
        P(("dp", "fsdp"), None),
        P(("dp", "fsdp"), None),
        P("fsdp"),
        P("fsdp"),
        P("fsdp", None),
        P("fsdp"),
        P("fsdp"),
        P("fsdp", None),
        P("fsdp"),
        P("fsdp"),
        P("fsdp"),
        P("fsdp", None),
        P("fsdp"),
        P("fsdp", None),
        P("fsdp"),
    )
    return jax.shard_map(local, mesh=mesh, in_specs=in_specs, out_specs=out_specs, check_vma=False)
```

profile of v0, /device:TPU:0, one launch (start us, length us, event | category | flops | bytes accessed | tf_op | source)
XLA Modules:
  0.0 1571.3 jit_solution(5706759700797450709)
XLA Ops:
  27.2 147.8 %all-reduce.19 = (bf16[768]{0:T(1024)(128)(2,1)S(1)}, bf16[768]{0:T(1024)(128)(2,1)S(1)}, bf16[768]{0:T(1024)(128)(2,1)S(1)}, bf16[768]{0:T(1024)(128)(2,1)S(1)}...) all-reduce(bf16[768]{0:T(1024)(128)(2,1)S(1)} %dynamic-update-slice, ...), channel_id=1, replica_groups=mesh['dp'=2,'fsdp'=16] {'fsdp'}, use_global_device_ids=true, to_apply=%add.1 | all-reduce | flops 8448 | bytes 33792
  259.2 167.0 %while.66 = (s32[]{:T(128)}, bf16[4,512,12,64]{1,3,2,0:T(8,128)(2,1)}, f32[4,12,512]{2,1,0:T(8,128)}, s32[4]{0:T(128)S(1)}, bf16[2,1024,12,64]{1,3,2,0:T(8,128)(...) while((s32[]{:T(128)}, ...), condition=%wide.region_5.6_spmd, body=%wide.region_2.5_spmd.sunk | while | flops 1668160000 | bytes 82530864 | solution.py:62
  445.3 70.0 %multiply_convert_fusion.1 = (bf16[2048,3072]{1,0:T(8,128)(2,1)}, f32[2048,3072]{1,0:T(8,128)}, f32[2048,3072]{1,0:T(8,128)}) fusion(f32[3072]{0:T(1024)S(1)} %copy-done.39, bf16[768,3072]{1,0:T(8,128)(2,1)} %all-gather.9.cloned.1.call-done, bf16[2048,768]{0,1:T(8,128)(2,1)S(1)} %add_convert_fusion.3.clone.4), kind=kOutput, calls=%fused_computation.82 | convolution fusion | flops 10078912512 | bytes 70791168 | tf_op jit(solution)/shard_map/dot_general | solution.py:204
  515.3 32.3 %fusion.107 = (bf16[3072]{0:T(1024)(128)(2,1)}, bf16[2048,3072]{1,0:T(8,128)(2,1)}) fusion(f32[2048,3072]{1,0:T(8,128)} %get-tuple-element.815, bf16[3072,768]{1,0:T(8,128)(2,1)} %all-gather.11.cloned.1.call-done, f32[2048,768]{1,0:T(8,128)} %scatter_custom_fusion, f32[2048,3072]{1,0:T(8,128)} %get-tuple-element.830, f32[3072]{0:T(1024)S(1)} %copy-done.39), kind=kOutput, calls=%fused_computation.166 | convolution fusion | flops 9765909504 | bytes 73943040 | tf_op jit(solution)/shard_map/td,fd->tf/dot_general | solution.py:236
  547.6 15.8 %fusion.106 = (bf16[768]{0:T(1024)(128)(2,1)}, f32[2048,768]{1,0:T(8,128)}) fusion(bf16[2048,3072]{1,0:T(8,128)(2,1)} %get-tuple-element.836, bf16[768,3072]{1,0:T(8,128)(2,1)S(1)} %copy-done.49), kind=kOutput, calls=%fused_computation.165 | convolution fusion | flops 9665248256 | bytes 23594496 | tf_op jit(solution)/shard_map/tf,df->td/dot_general | solution.py:241
  608.5 411.4 %while.68 = (s32[]{:T(128)}, bf16[2,1024,12,64]{3,2,1,0:T(8,128)(2,1)}, bf16[2,1024,12,64]{1,3,2,0:T(8,128)(2,1)}, bf16[2,1024,12,64]{1,3,2,0:T(8,128)(2,1)}, s3...) while((s32[]{:T(128)}, ...), condition=%wide.region_15.16_spmd, body=%wide.region_11.15_spmd.sunk | while | flops 4107672064 | bytes 327605248 | solution.py:123
  619.9 178.1 %while.69 = (s32[]{:T(128)}, f32[1024,12,64]{0,2,1:T(8,128)}, f32[1024,12,64]{0,2,1:T(8,128)}, bf16[2,512,12,64]{1,3,2,0:T(8,128)(2,1)}, s32[2]{0:T(128)S(1)}, /...) while((s32[]{:T(128)}, f32[1024,12,64]{0,2,1:T(8,128)}, ...), condition=%wide.region_14.14_spmd.clone, body=%wide.region_12.13_spmd.clone.sunk | while | flops 4106099200 | bytes 237427088 | solution.py:114
  650.0 17.6 %multiply_reduce_fusion.5 = (f32[12,512]{1,0:T(8,128)S(1)}, f32[12,512,1024]{2,1,0:T(8,128)}) fusion(f32[12,512,1024]{2,1,0:T(8,128)} %fusion.152, f32[12,512]{1,0:T(8,128)S(1)} %dynamic-slice_bitcast_fusion.2, pred[512,1024]{1,0:T(8,128)(4,1)S(1)} %broadcast_compare_fusion.5, bf16[1,1024,12,64]{1,3,2,0:T(8,128)(2,1)} %get-tuple-element.1136, ...), kind=kOutput, calls=%fused_computation.32.clone.1 | convolution fusion | flops 830466048 | bytes 53264900 | tf_op jit(solution)/shard_map/while/body/eval_jaxpr/while/body/eval_jaxpr/qhe,khe->hqk/dot_general | solution.py:97
  667.7 21.7 %multiply_convert_fusion.3 = bf16[12,512,1024]{2,1,0:T(8,128)(2,1)} fusion(f32[12,512,1024]{2,1,0:T(8,128)} %get-tuple-element.1083, f32[12,512,1024]{2,1,0:T(8,128)} %fusion.152, f32[12,512]{1,0:T(8,128)S(1)} %get-tuple-element.1084, f32[12,512]{1,0:T(8,128)S(1)} %dynamic-slice_bitcast_fusion.2, pred[512,1024]{1,0:T(8,128)(4,1)S(1)} %broadcast_compare_fusion.5), kind=kLoop, calls=%fused_computation.31.clone.1 | loop fusion | flops 31457280 | bytes 63488000 | tf_op jit(solution)/shard_map/while/body/eval_jaxpr/while/body/eval_jaxpr/convert_element_type | solution.py:101
  725.7 13.8 bitcast_add_fusion.5
  739.5 17.6 %multiply_reduce_fusion.5 = (f32[12,512]{1,0:T(8,128)S(1)}, f32[12,512,1024]{2,1,0:T(8,128)}) fusion(f32[12,512,1024]{2,1,0:T(8,128)} %fusion.152, f32[12,512]{1,0:T(8,128)S(1)} %dynamic-slice_bitcast_fusion.2, pred[512,1024]{1,0:T(8,128)(4,1)S(1)} %broadcast_compare_fusion.5, bf16[1,1024,12,64]{1,3,2,0:T(8,128)(2,1)} %get-tuple-element.1136, ...), kind=kOutput, calls=%fused_computation.32.clone.1 | convolution fusion | flops 830466048 | bytes 53264900 | tf_op jit(solution)/shard_map/while/body/eval_jaxpr/while/body/eval_jaxpr/qhe,khe->hqk/dot_general | solution.py:97
  757.1 21.6 %multiply_convert_fusion.3 = bf16[12,512,1024]{2,1,0:T(8,128)(2,1)} fusion(f32[12,512,1024]{2,1,0:T(8,128)} %get-tuple-element.1083, f32[12,512,1024]{2,1,0:T(8,128)} %fusion.152, f32[12,512]{1,0:T(8,128)S(1)} %get-tuple-element.1084, f32[12,512]{1,0:T(8,128)S(1)} %dynamic-slice_bitcast_fusion.2, pred[512,1024]{1,0:T(8,128)(4,1)S(1)} %broadcast_compare_fusion.5), kind=kLoop, calls=%fused_computation.31.clone.1 | loop fusion | flops 31457280 | bytes 63488000 | tf_op jit(solution)/shard_map/while/body/eval_jaxpr/while/body/eval_jaxpr/convert_element_type | solution.py:101
  825.6 177.5 %while.69 = (s32[]{:T(128)}, f32[1024,12,64]{0,2,1:T(8,128)}, f32[1024,12,64]{0,2,1:T(8,128)}, bf16[2,512,12,64]{1,3,2,0:T(8,128)(2,1)}, s32[2]{0:T(128)S(1)}, /...) while((s32[]{:T(128)}, f32[1024,12,64]{0,2,1:T(8,128)}, ...), condition=%wide.region_14.14_spmd.clone, body=%wide.region_12.13_spmd.clone.sunk | while | flops 4106099200 | bytes 237427088 | solution.py:114
  855.5 17.6 %multiply_reduce_fusion.5 = (f32[12,512]{1,0:T(8,128)S(1)}, f32[12,512,1024]{2,1,0:T(8,128)}) fusion(f32[12,512,1024]{2,1,0:T(8,128)} %fusion.152, f32[12,512]{1,0:T(8,128)S(1)} %dynamic-slice_bitcast_fusion.2, pred[512,1024]{1,0:T(8,128)(4,1)S(1)} %broadcast_compare_fusion.5, bf16[1,1024,12,64]{1,3,2,0:T(8,128)(2,1)} %get-tuple-element.1136, ...), kind=kOutput, calls=%fused_computation.32.clone.1 | convolution fusion | flops 830466048 | bytes 53264900 | tf_op jit(solution)/shard_map/while/body/eval_jaxpr/while/body/eval_jaxpr/qhe,khe->hqk/dot_general | solution.py:97
  873.0 21.6 %multiply_convert_fusion.3 = bf16[12,512,1024]{2,1,0:T(8,128)(2,1)} fusion(f32[12,512,1024]{2,1,0:T(8,128)} %get-tuple-element.1083, f32[12,512,1024]{2,1,0:T(8,128)} %fusion.152, f32[12,512]{1,0:T(8,128)S(1)} %get-tuple-element.1084, f32[12,512]{1,0:T(8,128)S(1)} %dynamic-slice_bitcast_fusion.2, pred[512,1024]{1,0:T(8,128)(4,1)S(1)} %broadcast_compare_fusion.5), kind=kLoop, calls=%fused_computation.31.clone.1 | loop fusion | flops 31457280 | bytes 63488000 | tf_op jit(solution)/shard_map/while/body/eval_jaxpr/while/body/eval_jaxpr/convert_element_type | solution.py:101
  930.8 13.8 bitcast_add_fusion.5
  944.6 17.6 %multiply_reduce_fusion.5 = (f32[12,512]{1,0:T(8,128)S(1)}, f32[12,512,1024]{2,1,0:T(8,128)}) fusion(f32[12,512,1024]{2,1,0:T(8,128)} %fusion.152, f32[12,512]{1,0:T(8,128)S(1)} %dynamic-slice_bitcast_fusion.2, pred[512,1024]{1,0:T(8,128)(4,1)S(1)} %broadcast_compare_fusion.5, bf16[1,1024,12,64]{1,3,2,0:T(8,128)(2,1)} %get-tuple-element.1136, ...), kind=kOutput, calls=%fused_computation.32.clone.1 | convolution fusion | flops 830466048 | bytes 53264900 | tf_op jit(solution)/shard_map/while/body/eval_jaxpr/while/body/eval_jaxpr/qhe,khe->hqk/dot_general | solution.py:97
  962.2 21.6 %multiply_convert_fusion.3 = bf16[12,512,1024]{2,1,0:T(8,128)(2,1)} fusion(f32[12,512,1024]{2,1,0:T(8,128)} %get-tuple-element.1083, f32[12,512,1024]{2,1,0:T(8,128)} %fusion.152, f32[12,512]{1,0:T(8,128)S(1)} %get-tuple-element.1084, f32[12,512]{1,0:T(8,128)S(1)} %dynamic-slice_bitcast_fusion.2, pred[512,1024]{1,0:T(8,128)(4,1)S(1)} %broadcast_compare_fusion.5), kind=kLoop, calls=%fused_computation.31.clone.1 | loop fusion | flops 31457280 | bytes 63488000 | tf_op jit(solution)/shard_map/while/body/eval_jaxpr/while/body/eval_jaxpr/convert_element_type | solution.py:101
  1072.4 16.5 %convolution_convert_fusion = bf16[3072,768]{1,0:T(8,128)(2,1)} fusion(bf16[2048,3072]{1,0:T(8,128)(2,1)} %get-tuple-element.814, f32[2048,768]{1,0:T(8,128)} %scatter_custom_fusion), kind=kOutput, calls=%fused_computation.129 | convolution fusion | flops 9667608576 | bytes 23592960 | tf_op jit(solution)/shard_map/tf,td->fd/dot_general | solution.py:234
  1092.8 16.4 %convolution_convert_fusion.1 = bf16[768,3072]{1,0:T(8,128)(2,1)} fusion(bf16[2048,3072]{1,0:T(8,128)(2,1)} %get-tuple-element.836, f32[2048,768]{0,1:T(8,128)} %copy-done.8, f32[768]{0:T(1024)S(1)} %copy-done.38, f32[768]{0:T(1024)S(1)} %copy-done.34, f32[2048]{0:T(1024)S(1)} %copy-done.21, f32[2048]{0:T(1024)S(1)} %copy-done.18), kind=kOutput, calls=%fused_computation.130 | convolution fusion | flops 9673900032 | bytes 23615488 | tf_op jit(solution)/shard_map/td,tf->df/dot_general | solution.py:239
  1139.3 75.1 %all-reduce.18 = (bf16[768]{0:T(1024)(128)(2,1)S(1)}, bf16[768]{0:T(1024)(128)(2,1)S(1)}, bf16[768]{0:T(1024)(128)(2,1)S(1)}, bf16[768]{0:T(1024)(128)(2,1)S(1)}...) all-reduce(bf16[768]{0:T(1024)(128)(2,1)S(1)} %dynamic-update-slice, ...), channel_id=1, replica_groups=mesh['dp'=2,'fsdp'=16] {'fsdp'}, use_global_device_ids=true, to_apply=%add.8 | all-reduce | flops 9984 | bytes 39936
  1214.4 16.7 %add_add_fusion.4 = bf16[2048,768]{0,1:T(8,128)(2,1)} fusion(f32[2048,768]{0,1:T(8,128)} %copy-done.8, bf16[2048,3072]{1,0:T(8,128)(2,1)} %get-tuple-element.814, bf16[3072,768]{1,0:T(8,128)(2,1)} %all-gather.11.cloned.1.call-done, f32[768]{0:T(1024)S(1)} %convert_element_type.247), kind=kOutput, calls=%fused_computation.126 | convolution fusion | flops 9668395008 | bytes 26741760 | tf_op jit(solution)/shard_map/dot_general | solution.py:210
  1249.9 135.1 %reduce-scatter.11.cloned.1.call-done = bf16[192,768]{1,0:T(8,128)(2,1)} async-done(((bf16[3072,768]{1,0:T(8,128)(2,1)}), bf16[192,768]{1,0:T(8,128)(2,1)}) %reduce-scatter.11.cloned.1.call-update) | async-done | bytes 294928 | tf_op jit(solution)/shard_map/reduce_scatter | solution.py:301
  1385.1 142.9 %reduce-scatter.9.cloned.1.call-done = bf16[48,3072]{1,0:T(8,128)(2,1)} async-done(((bf16[768,3072]{1,0:T(8,128)(2,1)}), bf16[48,3072]{1,0:T(8,128)(2,1)}) %reduce-scatter.9.cloned.1.call-update) | async-done | bytes 294928 | tf_op jit(solution)/shard_map/reduce_scatter | solution.py:295
  (394 shorter events, 674.8 us)
Async XLA Ops:
  7.2 195.3 %all-gather.5.cloned.1.call-start = ((), (), s32[]{:S(2)}) async-start(), calls=%async_computation.6 | async-start | bytes 3760128 | tf_op jit(solution)/shard_map/all_gather | solution.py:156
  7.9 426.5 %all-gather.7.cloned.1.call-start = ((), (), s32[]{:S(2)}) async-start(), calls=%async_computation.7 | async-start | bytes 1253376 | tf_op jit(solution)/shard_map/all_gather | solution.py:159
  8.7 436.6 %all-gather.9.cloned.1.call-start = ((), (), s32[]{:S(2)}) async-start(), calls=%async_computation.8 | async-start | bytes 5013504 | tf_op jit(solution)/shard_map/all_gather | solution.py:163
  9.5 17.0 %copy-start.55 = (bf16[48]{0:T(256)(128)(2,1)S(1)}, bf16[48]{0:T(256)(128)(2,1)}, u32[]{:S(2)}) copy-start(bf16[48]{0:T(256)(128)(2,1)} %param.26) | copy-start | bytes 292
  9.5 17.2 %copy-start.56 = (bf16[48]{0:T(256)(128)(2,1)S(1)}, bf16[48]{0:T(256)(128)(2,1)}, u32[]{:S(2)}) copy-start(bf16[48]{0:T(256)(128)(2,1)} %param.27) | copy-start | bytes 292
  9.5 17.5 %copy-start.57 = (bf16[192]{0:T(256)(128)(2,1)S(1)}, bf16[192]{0:T(256)(128)(2,1)}, u32[]{:S(2)}) copy-start(bf16[192]{0:T(256)(128)(2,1)} %param.36) | copy-start | bytes 1156
  14.3 168.3 %all-to-all-start.1 = ((bf16[16,128,768]{2,1,0:T(8,128)(2,1)}), bf16[16,128,768]{2,1,0:T(8,128)(2,1)}, u32[]{:S(2)}, u32[]{:S(2)}) async-start(bf16[16,128,768]{2,1,0:T(8,128)(2,1)} %bitcast.19), calls=%async_computation.1 | async-start | bytes 6291456 | tf_op jit(solution)/shard_map/all_to_all | solution.py:229
  22.7 492.6 %all-gather.11.cloned.1.call-start = ((), (), s32[]{:S(2)}) async-start(), calls=%async_computation.9 | async-start | bytes 5013504 | tf_op jit(solution)/shard_map/all_gather | solution.py:165
  23.2 1226.6 %reduce-scatter.7.cloned.1.call-start = ((), (), s32[]{:S(2)}) async-start(), calls=%async_computation.11 | async-start | bytes 1253376 | tf_op jit(solution)/shard_map/reduce_scatter | solution.py:283
  175.0 27.5 %copy-start.44 = (f32[768]{0:T(1024)}, f32[768]{0:T(1024)S(1)}, u32[]{:S(2)}) copy-start(f32[768]{0:T(1024)S(1)} %convert_element_type.235) | copy-start | bytes 9220
  175.0 27.5 %copy-start.30 = (f32[768]{0:T(1024)}, f32[768]{0:T(1024)S(1)}, u32[]{:S(2)}) copy-start(f32[768]{0:T(1024)S(1)} %convert_element_type.234) | copy-start | bytes 9220
  180.6 22.0 %copy-start.4 = (bf16[2048,768]{0,1:T(8,128)(2,1)}, bf16[2048,768]{0,1:T(8,128)(2,1)S(1)}, u32[]{:S(2)}) copy-start(bf16[2048,768]{0,1:T(8,128)(2,1)S(1)} %copy.79) | copy-start | bytes 9437188
  181.1 21.4 %copy-start.14 = (f32[2048]{0:T(1024)}, f32[2048]{0:T(1024)S(1)}, u32[]{:S(2)}) copy-start(f32[2048]{0:T(1024)S(1)} %broadcast_multiply_fusion.2) | copy-start | bytes 24580
  182.5 20.0 %copy-start.22 = (f32[2048]{0:T(1024)}, f32[2048]{0:T(1024)S(1)}, u32[]{:S(2)}) copy-start(f32[2048]{0:T(1024)S(1)} %fusion.88) | copy-start | bytes 24580
  182.6 19.9 %copy-start.35 = (s32[2048,1]{0,1:T(1,128)}, s32[2048,1]{0,1:T(1,128)S(1)}, u32[]{:S(2)}) copy-start(s32[2048,1]{0,1:T(1,128)S(1)} %compare_select_fusion) | copy-start | bytes 24580
  515.3 32.3 %copy-start.49 = (bf16[768,3072]{1,0:T(8,128)(2,1)S(1)}, bf16[768,3072]{1,0:T(8,128)(2,1)}, u32[]{:S(2)}) copy-start(bf16[768,3072]{1,0:T(8,128)(2,1)} %all-gather.9.cloned.1.call-done) | copy-start | bytes 14155780
  590.9 659.0 %reduce-scatter.5.cloned.1.call-start = ((), (), s32[]{:S(2)}) async-start(), calls=%async_computation.10 | async-start | bytes 3760128 | tf_op jit(solution)/shard_map/reduce_scatter | solution.py:274
  1072.3 312.8 %reduce-scatter.11.cloned.1.call-start = ((), (), s32[]{:S(2)}) async-start(), calls=%async_computation.13 | async-start | bytes 5013504 | tf_op jit(solution)/shard_map/reduce_scatter | solution.py:301
  1072.4 17.1 %copy-start.36 = (s32[2048,1]{0,1:T(1,128)S(1)}, s32[2048,1]{0,1:T(1,128)}, u32[]{:S(2)}) copy-start(s32[2048,1]{0,1:T(1,128)} %copy-done.35) | copy-start | bytes 24580
  1088.9 439.1 %reduce-scatter.9.cloned.1.call-start = ((), (), s32[]{:S(2)}) async-start(), calls=%async_computation.12 | async-start | bytes 5013504 | tf_op jit(solution)/shard_map/reduce_scatter | solution.py:295
  1243.7 284.3 %copy-start.6 = (bf16[2048,768]{0,1:T(8,128)(2,1)S(1)}, bf16[2048,768]{0,1:T(8,128)(2,1)}, u32[]{:S(2)}) copy-start(bf16[2048,768]{0,1:T(8,128)(2,1)} %copy-done.4) | copy-start | bytes 9437188
  1243.7 284.3 %copy-start.25 = (f32[2048]{0:T(1024)S(1)}, f32[2048]{0:T(1024)}, u32[]{:S(2)}) copy-start(f32[2048]{0:T(1024)} %copy-done.24) | copy-start | bytes 24580
  1243.7 308.6 %all-to-all-start = ((bf16[16,128,768]{2,1,0:T(8,128)(2,1)}), bf16[16,128,768]{2,1,0:T(8,128)(2,1)}, u32[]{:S(2)}, u32[]{:S(2)}) async-start(bf16[16,128,768]{2,1,0:T(8,128)(2,1)} %bitcast.194), calls=%async_computation | async-start | bytes 6291456 | tf_op jit(solution)/shard_map/all_to_all | solution.py:214
  1248.5 308.9 %all-reduce.24.cloned.1.call-start = ((), (), s32[]{:S(2)}) async-start(), calls=%async_computation.14 | async-start | bytes 1769472 | tf_op jit(solution)/shard_map/psum | solution.py:312
  (62 other events, 414.4 us)
Sparse Core Ops, SparseCore 0:
  10.8 117.3 all-gather.4
  131.0 55.9 all-gather.6
  189.8 79.3 all-gather.8
  271.9 79.0 all-gather.10
  591.1 122.4 reduce-scatter.6
  1072.4 132.5 reduce-scatter.4
  1210.2 174.8 reduce-scatter.10
  1391.1 136.9 reduce-scatter.8
  1530.6 18.5 all-reduce.23
where the time goes:
time: 1580 us; the launch traced here: 1570 us
  matrix products  566 us (36%)
  waiting for transfers between devices  281 us (18%)
  other arithmetic  239 us (15%)
  blocking collectives  225 us (14%)
  local copies, waits for them, and re-layouts  203 us (13%)
  loops' own time  25.8 us (2%)
  between operations  17.8 us (1%)
    unnamed x2, blocking collectives  223 us
    reduce_scatter x1, waiting for transfers between devices, local(): lax.psum_scatter(grad_up.astype(jnp.bfloat16), 'fsdp', scatter_dimension=...  143 us
    reduce_scatter x1, waiting for transfers between devices, local(): lax.psum_scatter(grad_down.astype(jnp.bfloat16), 'fsdp', scatter_dimensio...  135 us
    convert_element_type x4, other arithmetic, one_one_block(): score_grad = (soft * (prob_grad - inner_sum)).astype(jnp.bfloat16)  86.6 us
    dot_general x4, matrix products, one_one_block(): jnp.einsum('qhe,khe->hqk', grad_block, value_four[row_at], preferred_elem...  70.3 us
    dot_general x1, matrix products, local(): jnp.dot(normed_two, full_up, preferred_element_type=jnp.float32)  70 us
    dot_general x4, matrix products, one_one_block(): jnp.einsum('qhe,khe->hqk', query_block, key_four[row_at], preferred_eleme...  54.4 us
    dot_general x4, matrix products, one_one_block(): jnp.einsum('hqk,qhe->khe', soft.astype(jnp.bfloat16), grad_block, preferr...  53.6 us
  transfers between devices with their start and end apart: 11, of which 2 were waited for; matrix products, arithmetic and copies ran while one was open for 58% of the time, Pallas kernels for 0%

commit v1 on v0

v1 whole, which is shorter than its diff:
```python
import functools
import math

import jax
import jax.numpy as jnp
from jax import lax
from jax.experimental import pallas as pl
from jax.experimental.pallas import tpu as pltpu
from jax.sharding import PartitionSpec as P

F32 = jnp.float32
BF = jnp.bfloat16
EPS = 1e-6
LOG2E = math.log2(math.e)
LN2 = math.log(2.0)
NT = (((1,), (1,)), ((), ()))
TN = (((0,), (0,)), ((), ()))
NN = (((1,), (0,)), ((), ()))
ANY = pl.BlockSpec(memory_space=pl.ANY)
VECS = 16
SDS = jax.ShapeDtypeStruct


def dg(a, b, dims):
    return lax.dot_general(a, b, dims, preferred_element_type=F32)


def params(axes=1):
    return pltpu.CompilerParams(
        vmem_limit_bytes=58 * 2**20, dimension_semantics=("arbitrary",) * axes
    )


def cost(flops, nbytes, trans=0):
    return pl.CostEstimate(flops=int(flops), bytes_accessed=int(nbytes), transcendentals=int(trans))


def rows_of(height, width):
    return pl.BlockSpec((height, width), lambda i, *_: (i, 0))


def whole(shape):
    zeros = (0,) * len(shape)
    return pl.BlockSpec(shape, lambda *_: zeros, pipeline_mode=pl.Buffered(1))


def fixed(shape):
    zeros = (0,) * len(shape)
    return pl.BlockSpec(shape, lambda *_: zeros)


def norm_stats(x):
    n = x.shape[-1]
    c = x - jnp.sum(x, axis=-1, keepdims=True) * (1.0 / n)
    var = jnp.sum(c * c, axis=-1, keepdims=True) * (1.0 / n)
    return c, lax.rsqrt(var + EPS)


def xor_pp(x, b, n):
    return lax.ppermute(x, "fsdp", [(i, i ^ b) for i in range(n)])


def core_swap(x, m):
    return lax.ppermute(x, "dp", [(i, i ^ 1) for i in range(m)])


def gather_near(x, n):
    q = n // 4
    return jnp.stack([x] + [xor_pp(x, d * q, n) for d in (1, 2, 3)])


def gather_far(s, n, m):
    own = [s] + [xor_pp(s, e, n) for e in range(1, n // 4)]
    return own + [core_swap(t, m) for t in own]


def settle(pieces, f, c, n, rep=1):
    q = n // 4
    rows = pieces[0].shape[1]
    if rows % 16 == 0 and q == 4:
        return pieces
    order = f ^ jnp.arange(n)
    halves = []
    for side in (pieces[:q], pieces[q:]):
        rel = jnp.stack(side, axis=1).reshape((n,) + side[0].shape[1:])
        halves.append(jnp.take(rel, order, axis=0))
    left = jnp.where(c == 0, halves[0], halves[1])
    right = jnp.where(c == 0, halves[1], halves[0])
    out = []
    for side in (left, right):
        four = side.reshape(4, 4, n * rows // 16, side.shape[-1])
        out += [four[:, e] for e in range(4)]
    return out


def load_pieces(idx_ref, pieces, dst, sem, width):
    f = idx_ref[0]
    c = idx_ref[1]
    rows = pieces[0].shape[1]
    started = []
    for e in range(4):
        for d in range(4):
            s = lax.bitwise_xor(f, jnp.int32(d * 4 + e))
            at = pl.ds(pl.multiple_of(s * rows, 16), rows)
            for h, src in ((c, pieces[e]), (1 - c, pieces[4 + e])):
                cols = pl.ds(pl.multiple_of(h * width, 128), width)
                cp = pltpu.make_async_copy(src.at[d, :, pl.ds(0, width)], dst.at[at, cols], sem)
                cp.start()
                started.append(cp)
    return started


def load_vecs(idx_ref, pieces, dst, sem, width):
    f = idx_ref[0]
    rows = pieces[0].shape[1]
    started = []
    for e in range(4):
        for d in range(4):
            s = lax.bitwise_xor(f, jnp.int32(d * 4 + e))
            at = pl.ds(pl.multiple_of(s * rows, 16), rows)
            cp = pltpu.make_async_copy(pieces[e].at[d, :, pl.ds(width, 128)], dst.at[at, :], sem)
            cp.start()
            started.append(cp)
    return started


def qkv_kernel(idx_ref, x_ref, *refs):
    pieces = refs[:8]
    q_ref, k_ref, v_ref, vt_ref, w_ref, vec_ref, sem = refs[8:]
    d = x_ref.shape[1]

    @pl.when(pl.program_id(0) == 0)
    def _():
        going = load_pieces(idx_ref, pieces, w_ref, sem.at[0], 3 * d // 2)
        vecs = load_vecs(idx_ref, pieces, vec_ref, sem.at[1], 3 * d // 2)
        for cp in vecs:
            cp.wait()
        vt_ref[...] = vec_ref[...].astype(F32).T[:VECS]
        for cp in going:
            cp.wait()

    c, r = norm_stats(x_ref[...].astype(F32))
    h = (c * r * vt_ref[0:1, :] + vt_ref[1:2, :]).astype(BF)
    q = dg(h, w_ref[:, :d], NN)
    q_ref[...] = ((q + vt_ref[2:3, :]) * (0.125 * LOG2E)).astype(BF)
    k_ref[...] = dg(h, w_ref[:, d : 2 * d], NN).astype(BF)
    v_ref[...] = (dg(h, w_ref[:, 2 * d :], NN) + vt_ref[3:4, :]).astype(BF)


def qkv(idx, x, pieces, tb=512):
    t, d = x.shape
    return pl.pallas_call(
        qkv_kernel,
        grid_spec=pltpu.PrefetchScalarGridSpec(
            num_scalar_prefetch=1,
            grid=(t // tb,),
            in_specs=[rows_of(tb, d)] + [ANY] * 8,
            out_specs=[rows_of(tb, d)] * 3 + [fixed((VECS, d))],
            scratch_shapes=[
                pltpu.VMEM((d, 3 * d), BF),
                pltpu.VMEM((d, 128), BF),
                pltpu.SemaphoreType.DMA((2,)),
            ],
        ),
        out_shape=[SDS((t, d), BF)] * 3 + [SDS((VECS, d), F32)],
        compiler_params=params(),
        cost_estimate=cost(6 * t * d * d, t * d * 8 + d * d * 6),
        name="qkv",
    )(idx, x, *pieces)


def attend_kernel(tag_ref, q_ref, k_ref, v_ref, o_ref, l_ref, *, qb):
    r = pl.program_id(0)
    length = q_ref.shape[0]
    low = lax.broadcasted_iota(jnp.int32, (1, 128), 1) < 64

    def block(qs, qn, ks, kn):
        q = q_ref[pl.ds(qs, qn), :]
        k = k_ref[pl.ds(ks, kn), :]
        v = v_ref[pl.ds(ks, kn), :]
        outs = []
        for h in range(2):
            sel = low if h == 0 else jnp.logical_not(low)
            qm = jnp.where(sel, q, jnp.asarray(0, BF))
            vm = jnp.where(sel, v, jnp.asarray(1, BF))
            s = dg(qm, k, NT)
            m = jnp.max(s, axis=1, keepdims=True)
            outs.append((dg(jnp.exp2(s - m).astype(BF), vm, NN), m))
        (a, ma), (b, mb) = outs
        acc = jnp.where(low, a, b)
        total = pltpu.roll(jnp.where(low, b, a), 64, 1)
        o_ref[pl.ds(qs, qn), :] = (acc / total).astype(o_ref.dtype)
        lse = (jnp.where(low, ma, mb) + jnp.log2(total)).T
        l_ref[0, 0, 0:1, pl.ds(qs, qn)] = lse[0:1]
        l_ref[0, 0, 1:2, pl.ds(qs, qn)] = lse[64:65]

    @pl.when(tag_ref[r] == 0)
    def _():
        for i in range(length // qb):
            block(i * qb, qb, 0, length)

    @pl.when(tag_ref[r] != 0)
    def _():
        c = length // 4
        for i in range(4):
            block(i * c, c, i * c, c)


def attend(tag, q, k, v, qb=512):
    t, d = q.shape
    rows = tag.shape[0]
    length = t // rows
    pairs = d // 128
    blk = pl.BlockSpec((length, 128), lambda r, p, _: (r, p))
    lse = pl.BlockSpec((1, 1, 2, length), lambda r, p, _: (r, p, 0, 0))
    return pl.pallas_call(
        functools.partial(attend_kernel, qb=qb),
        grid_spec=pltpu.PrefetchScalarGridSpec(
            num_scalar_prefetch=1, grid=(rows, pairs), in_specs=[blk] * 3, out_specs=[blk, lse]
        ),
        out_shape=[SDS((t, d), BF), SDS((rows, pairs, 2, length), F32)],
        compiler_params=params(2),
        cost_estimate=cost(16 * t * length * d, t * d * 8, t * length * 12),
        name="attend",
    )(tag, q, k, v)


def gelu_both(u):
    t = 1.0 + jnp.abs(u) * (0.3275911 / math.sqrt(2.0))
    r = pl.reciprocal(t, approx=True)
    r = r * (2.0 - t * r)
    e = jnp.exp2(u * u * (-0.5 * LOG2E))
    p = -0.5 * 1.453152027 + r * (0.5 * 1.061405429)
    p = 0.5 * 1.421413741 + r * p
    p = -0.5 * 0.284496736 + r * p
    p = 0.5 * 0.254829592 + r * p
    tail = r * p * e
    phi = jnp.where(u >= 0.0, 1.0 - tail, tail)
    return u * phi, phi + u * e * (1.0 / math.sqrt(2.0 * math.pi))


def mlp_kernel(idx_ref, x_ref, o_ref, vt_ref, bu_ref, *refs, fc):
    p1 = refs[:8]
    p2 = refs[8:16]
    x2_ref, gl_ref, gp_ref, y_ref, w1_ref, w2_ref, sem = refs[16:]
    d = x_ref.shape[1]
    ff = w2_ref.shape[0]

    @pl.when(pl.program_id(0) == 0)
    def _():
        going = load_pieces(idx_ref, p1, w1_ref, sem.at[0], w1_ref.shape[1] // 2)
        going += load_pieces(idx_ref, p2, w2_ref, sem.at[1], d // 2)
        for cp in going:
            cp.wait()

    x2 = x_ref[...].astype(F32) + dg(o_ref[...], w1_ref[:, :d], NN) + vt_ref[4:5, :]
    x2_ref[...] = x2
    c, r = norm_stats(x2)
    h = (c * r * vt_ref[5:6, :] + vt_ref[6:7, :]).astype(BF)
    y = x2 + vt_ref[7:8, :]
    for f in range(0, ff, fc):
        u = dg(h, w1_ref[:, d + f : d + f + fc], NN) + bu_ref[:, f : f + fc]
        g, gp = gelu_both(u)
        g = g.astype(BF)
        gl_ref[:, f : f + fc] = g
        gp_ref[:, f : f + fc] = gp.astype(BF)
        y = y + dg(g, w2_ref[f : f + fc, :], NN)
    y_ref[...] = y.astype(BF)


def mlp(idx, x, o, vt, bu, p1, p2, tb=256, fc=768):
    t, d = x.shape
    ff = bu.shape[1]
    return pl.pallas_call(
        functools.partial(mlp_kernel, fc=fc),
        grid_spec=pltpu.PrefetchScalarGridSpec(
            num_scalar_prefetch=1,
            grid=(t // tb,),
            in_specs=[rows_of(tb, d)] * 2 + [whole(vt.shape), whole(bu.shape)] + [ANY] * 16,
            out_specs=[rows_of(tb, d), rows_of(tb, ff), rows_of(tb, ff), rows_of(tb, d)],
            scratch_shapes=[
                pltpu.VMEM((d, d + ff), BF),
                pltpu.VMEM((ff, d), BF),
                pltpu.SemaphoreType.DMA((2,)),
            ],
        ),
        out_shape=[SDS((t, d), F32), SDS((t, ff), BF), SDS((t, ff), BF), SDS((t, d), BF)],
        compiler_params=params(),
        cost_estimate=cost(4 * t * d * (d + 2 * ff), t * (10 * d + 4 * ff) + 4 * d * ff, 2 * t * ff),
        name="mlp",
    )(idx, x, o, vt, bu, *p1, *p2)


def permute_kernel(ord_ref, y_ref, o_ref):
    jb = o_ref.shape[0]
    t = y_ref.shape[0]
    hot = jnp.where(ord_ref[...] == lax.broadcasted_iota(jnp.int32, (jb, t), 1), 1.0, 0.0)
    o_ref[...] = dg(hot.astype(BF), y_ref[...], NN).astype(BF)


def permute(order_col, y, jb=512):
    t, d = y.shape
    return pl.pallas_call(
        permute_kernel,
        grid=(t // jb,),
        in_specs=[rows_of(jb, 1), whole((t, d))],
        out_specs=rows_of(jb, d),
        out_shape=SDS((t, d), BF),
        compiler_params=params(),
        cost_estimate=cost(2 * t * t * d, t * d * 4),
        name="permute",
    )(order_col, y)


def mlp_back_kernel(idx_ref, ord_ref, ret_ref, gp_ref, x2_ref, vt_ref, *refs, fc):
    p1 = refs[:8]
    p2 = refs[8:16]
    (dm_ref, du_ref, dx2_ref, da_ref, do_ref, h2_ref, sums_ref, gbu_ref, w1_ref, w2_ref, sem) = refs[16:]
    i = pl.program_id(0)
    tb, ff = gp_ref.shape
    t, d = ret_ref.shape

    @pl.when(i == 0)
    def _():
        going = load_pieces(idx_ref, p1, w1_ref, sem.at[0], w1_ref.shape[1] // 2)
        going += load_pieces(idx_ref, p2, w2_ref, sem.at[1], d // 2)
        sums_ref[...] = jnp.zeros_like(sums_ref)
        gbu_ref[...] = jnp.zeros_like(gbu_ref)
        for cp in going:
            cp.wait()

    at = lax.broadcasted_iota(jnp.int32, (tb, t), 0) + i * tb
    hot = jnp.where(ord_ref[...] == at, 1.0, 0.0).astype(BF)
    dy = dg(hot, ret_ref[...], NN)
    dm = dy.astype(BF)
    dm_ref[...] = dm
    sums_ref[0:1, :] += jnp.sum(dy, axis=0, keepdims=True)
    dh = jnp.zeros((tb, d), F32)
    for f in range(0, ff, fc):
        du = (dg(dm, w2_ref[f : f + fc, :], NT) * gp_ref[:, f : f + fc].astype(F32)).astype(BF)
        du_ref[:, f : f + fc] = du
        gbu_ref[:, f : f + fc] += jnp.sum(du.astype(F32), axis=0, keepdims=True)
        dh = dh + dg(du, w1_ref[:, d + f : d + f + fc], NT)
    c, r = norm_stats(x2_ref[...])
    xh = c * r
    gain = vt_ref[5:6, :]
    h2_ref[...] = (xh * gain + vt_ref[6:7, :]).astype(BF)
    sums_ref[1:2, :] += jnp.sum(dh * xh, axis=0, keepdims=True)
    sums_ref[2:3, :] += jnp.sum(dh, axis=0, keepdims=True)
    dz = dh * gain
    m1 = jnp.sum(dz, axis=-1, keepdims=True) * (1.0 / d)
    m2 = jnp.sum(dz * xh, axis=-1, keepdims=True) * (1.0 / d)
    dx2 = dy + r * (dz - m1 - xh * m2)
    dx2_ref[...] = dx2
    da = dx2.astype(BF)
    da_ref[...] = da
    sums_ref[3:4, :] += jnp.sum(da.astype(F32), axis=0, keepdims=True)
    do_ref[...] = dg(da, w1_ref[:, :d], NT).astype(BF)


def mlp_back(idx, order_row, ret, gp, x2, vt, p1, p2, tb=256, fc=768):
    t, d = x2.shape
    ff = gp.shape[1]
    return pl.pallas_call(
        functools.partial(mlp_back_kernel, fc=fc),
        grid_spec=pltpu.PrefetchScalarGridSpec(
            num_scalar_prefetch=1,
            grid=(t // tb,),
            in_specs=[whole((1, t)), whole((t, d)), rows_of(tb, ff), rows_of(tb, d), whole(vt.shape)]
            + [ANY] * 16,
            out_specs=[
                rows_of(tb, d),
                rows_of(tb, ff),
                rows_of(tb, d),
                rows_of(tb, d),
                rows_of(tb, d),
                rows_of(tb, d),
                fixed((8, d)),
                fixed((1, ff)),
            ],
            scratch_shapes=[
                pltpu.VMEM((d, d + ff), BF),
                pltpu.VMEM((ff, d), BF),
                pltpu.SemaphoreType.DMA((2,)),
            ],
        ),
        out_shape=[
            SDS((t, d), BF),
            SDS((t, ff), BF),
            SDS((t, d), F32),
            SDS((t, d), BF),
            SDS((t, d), BF),
            SDS((t, d), BF),
            SDS((8, d), F32),
            SDS((1, ff), F32),
        ],
        compiler_params=params(),
        cost_estimate=cost(2 * t * d * (d + 2 * ff + t) * 1.5, t * (20 * d + 4 * ff)),
        name="mlp_back",
    )(idx, order_row, ret, gp, x2, vt, *p1, *p2)


def split_halves(c, r, mine_ref, theirs_ref):
    h = r.shape[1] // 2
    left, right = r[:, :h], r[:, h:]
    mine_ref[...] = jnp.where(c == 0, left, right)
    theirs_ref[...] = jnp.where(c == 0, right, left)


def grad_down_kernel(idx_ref, g_ref, dm_ref, mine_ref, theirs_ref):
    split_halves(idx_ref[1], dg(g_ref[...], dm_ref[...], TN).astype(BF), mine_ref, theirs_ref)


def grad_down(idx, g, dm, mb=768):
    t, ff = g.shape
    d = dm.shape[1]
    return pl.pallas_call(
        grad_down_kernel,
        grid_spec=pltpu.PrefetchScalarGridSpec(
            num_scalar_prefetch=1,
            grid=(ff // mb,),
            in_specs=[pl.BlockSpec((t, mb), lambda i, _: (0, i)), whole((t, d))],
            out_specs=[rows_of(mb, d // 2)] * 2,
        ),
        out_shape=[SDS((ff, d // 2), BF)] * 2,
        compiler_params=params(),
        cost_estimate=cost(3 * t * ff * d, 2 * t * (ff + d) + 2 * ff * d),
        name="grad_down",
    )(idx, g, dm)


def grad_up_kernel(idx_ref, h2_ref, o_ref, du_ref, da_ref, mine_ref, theirs_ref, *, steps):
    i = pl.program_id(0)

    @pl.when(i < steps)
    def _():
        split_halves(idx_ref[1], dg(h2_ref[...], du_ref[...], TN).astype(BF), mine_ref, theirs_ref)

    @pl.when(i == steps)
    def _():
        split_halves(idx_ref[1], dg(o_ref[...], da_ref[...], TN).astype(BF), mine_ref, theirs_ref)


def grad_up(idx, h2, o, du, da):
    t, d = h2.shape
    ff = du.shape[1]
    steps = ff // d
    return pl.pallas_call(
        functools.partial(grad_up_kernel, steps=steps),
        grid_spec=pltpu.PrefetchScalarGridSpec(
            num_scalar_prefetch=1,
            grid=(steps + 1,),
            in_specs=[
                whole((t, d)),
                whole((t, d)),
                pl.BlockSpec((t, d), lambda i, _: (0, jnp.minimum(i, steps - 1))),
                whole((t, d)),
            ],
            out_specs=[pl.BlockSpec((d, d // 2), lambda i, _: (0, i))] * 2,
        ),
        out_shape=[SDS((d, (d + ff) // 2), BF)] * 2,
        compiler_params=params(),
        cost_estimate=cost(3 * t * (ff + d) * d, 2 * t * (ff + 3 * d) + 2 * ff * d),
        name="grad_up",
    )(idx, h2, o, du, da)


def attend_back_kernel(
    tag_ref, q_ref, k_ref, v_ref, do_ref, o_ref, l_ref, dq_ref, dk_ref, dv_ref, dl_ref, dqt_ref, *, kb, qb
):
    r = pl.program_id(0)
    length = q_ref.shape[0]
    low = lax.broadcasted_iota(jnp.int32, (1, 128), 1) < 64
    prod = (do_ref[...].astype(F32) * o_ref[...].astype(F32)).T
    dl_ref[0:1, :] = jnp.sum(prod[0:64], axis=0, keepdims=True)
    dl_ref[1:2, :] = jnp.sum(prod[64:128], axis=0, keepdims=True)

    def block(ks, kn, qs, qn):
        k = k_ref[pl.ds(ks, kn), :]
        v = v_ref[pl.ds(ks, kn), :]
        q = q_ref[pl.ds(qs, qn), :]
        do = do_ref[pl.ds(qs, qn), :]
        dks = []
        dvs = []
        dqs = []
        for h in range(2):
            sel = low if h == 0 else jnp.logical_not(low)
            km = jnp.where(sel, k, jnp.asarray(0, BF))
            vm = jnp.where(sel, v, jnp.asarray(0, BF))
            pt = jnp.exp2(dg(km, q, NT) - l_ref[0, 0, h : h + 1, pl.ds(qs, qn)])
            dst = (pt * (dg(vm, do, NT) - dl_ref[h : h + 1, pl.ds(qs, qn)])).astype(BF)
            dvs.append(dg(pt.astype(BF), do, NN))
            dks.append(dg(dst, q, NN))
            dqs.append(dg(km.T, dst, NN))
        return jnp.where(low, dks[0], dks[1]), jnp.where(low, dvs[0], dvs[1]), dqs[0] + dqs[1]

    def run(kn, qn, plan):
        seen = set()
        for ks, starts in plan:
            dk = dv = None
            for qs in starts:
                a, b, dq = block(ks, kn, qs, qn)
                dk = a if dk is None else dk + a
                dv = b if dv is None else dv + b
                if qs in seen:
                    dqt_ref[:, pl.ds(qs, qn)] += dq
                else:
                    dqt_ref[:, pl.ds(qs, qn)] = dq
                seen.add(qs)
            dk_ref[pl.ds(ks, kn), :] = (dk * LN2).astype(BF)
            dv_ref[pl.ds(ks, kn), :] = dv.astype(BF)
        dq_ref[...] = (dqt_ref[...].T * 0.125).astype(BF)

    @pl.when(tag_ref[r] == 0)
    def _():
        run(kb, qb, [(ks, range(0, length, qb)) for ks in range(0, length, kb)])

    @pl.when(tag_ref[r] != 0)
    def _():
        c = length // 4
        run(c, c, [(ks, [ks]) for ks in range(0, length, c)])


def attend_back(tag, q, k, v, do, o, lse, kb=512, qb=512):
    t, d = q.shape
    rows = tag.shape[0]
    length = t // rows
    pairs = d // 128
    blk = pl.BlockSpec((length, 128), lambda r, p, _: (r, p))
    lse_spec = pl.BlockSpec((1, 1, 2, length), lambda r, p, _: (r, p, 0, 0))
    return pl.pallas_call(
        functools.partial(attend_back_kernel, kb=kb, qb=qb),
        grid_spec=pltpu.PrefetchScalarGridSpec(
            num_scalar_prefetch=1,
            grid=(rows, pairs),
            in_specs=[blk] * 5 + [lse_spec],
            out_specs=[blk] * 3,
            scratch_shapes=[pltpu.VMEM((2, length), F32), pltpu.VMEM((128, length), F32)],
        ),
        out_shape=[SDS((t, d), BF)] * 3,
        compiler_params=params(2),
        cost_estimate=cost(40 * t * length * d, t * d * 16, t * length * 12),
        name="attend_back",
    )(tag, q, k, v, do, o, lse)


def grad_qkv_kernel(idx_ref, x_ref, vt_ref, dq_ref, dk_ref, dv_ref, mine_ref, theirs_ref, s_ref, h_ref):
    i = pl.program_id(0)

    @pl.when(i == 0)
    def _():
        c, r = norm_stats(x_ref[...].astype(F32))
        h_ref[...] = (c * r * vt_ref[0:1, :] + vt_ref[1:2, :]).astype(BF)
        s_ref[...] = jnp.zeros_like(s_ref)

    for m, ref in enumerate((dq_ref, dk_ref, dv_ref)):

        @pl.when(i == m)
        def _(m=m, ref=ref):
            dj = ref[...]
            split_halves(idx_ref[1], dg(h_ref[...], dj, TN).astype(BF), mine_ref, theirs_ref)
            if m != 1:
                s_ref[m // 2 : m // 2 + 1, :] = jnp.sum(dj.astype(F32), axis=0, keepdims=True)


def grad_qkv(idx, x, vt, dq, dk, dv):
    t, d = x.shape
    return pl.pallas_call(
        grad_qkv_kernel,
        grid_spec=pltpu.PrefetchScalarGridSpec(
            num_scalar_prefetch=1,
            grid=(3,),
            in_specs=[whole((t, d)), whole(vt.shape)] + [whole((t, d))] * 3,
            out_specs=[pl.BlockSpec((d, d // 2), lambda i, _: (0, i))] * 2 + [fixed((8, d))],
            scratch_shapes=[pltpu.VMEM((t, d), BF)],
        ),
        out_shape=[SDS((d, 3 * d // 2), BF)] * 2 + [SDS((8, d), F32)],
        compiler_params=params(),
        cost_estimate=cost(9 * t * d * d, t * d * 10),
        name="grad_qkv",
    )(idx, x, vt, dq, dk, dv)


def tokens_back_kernel(idx_ref, dq_ref, dk_ref, dv_ref, x_ref, vt_ref, dx2_ref, *refs):
    pieces = refs[:8]
    tg_ref, s_ref, w_ref, sem = refs[8:]
    d = x_ref.shape[1]

    @pl.when(pl.program_id(0) == 0)
    def _():
        going = load_pieces(idx_ref, pieces, w_ref, sem, 3 * d // 2)
        s_ref[...] = jnp.zeros_like(s_ref)
        for cp in going:
            cp.wait()

    dh = dg(dq_ref[...], w_ref[:, :d], NT)
    dh = dh + dg(dk_ref[...], w_ref[:, d : 2 * d], NT)
    dh = dh + dg(dv_ref[...], w_ref[:, 2 * d :], NT)
    c, r = norm_stats(x_ref[...].astype(F32))
    xh = c * r
    s_ref[0:1, :] += jnp.sum(dh * xh, axis=0, keepdims=True)
    s_ref[1:2, :] += jnp.sum(dh, axis=0, keepdims=True)
    dz = dh * vt_ref[0:1, :]
    m1 = jnp.sum(dz, axis=-1, keepdims=True) * (1.0 / d)
    m2 = jnp.sum(dz * xh, axis=-1, keepdims=True) * (1.0 / d)
    tg_ref[...] = dx2_ref[...] + r * (dz - m1 - xh * m2)


def tokens_back(idx, dq, dk, dv, x, vt, dx2, pieces, tb=512):
    t, d = x.shape
    return pl.pallas_call(
        tokens_back_kernel,
        grid_spec=pltpu.PrefetchScalarGridSpec(
            num_scalar_prefetch=1,
            grid=(t // tb,),
            in_specs=[rows_of(tb, d)] * 4 + [whole(vt.shape), rows_of(tb, d)] + [ANY] * 8,
            out_specs=[rows_of(tb, d), fixed((8, d))],
            scratch_shapes=[pltpu.VMEM((d, 3 * d), BF), pltpu.SemaphoreType.DMA],
        ),
        out_shape=[SDS((t, d), F32), SDS((8, d), F32)],
        compiler_params=params(),
        cost_estimate=cost(9 * t * d * d, t * d * 16 + d * d * 6),
        name="tokens_back",
    )(idx, dq, dk, dv, x, vt, dx2, *pieces)


def sum_far_kernel(idx_ref, *refs, q):
    for e in range(q):
        a, b, o = refs[e], refs[q + e], refs[2 * q + e]
        o[...] = (a[...].astype(F32) + b[...].astype(F32)).astype(BF)


def sum_far(idx, mine, recv, n):
    q = n // 4
    _, rows, ch = mine.shape

    def spec(e):
        return pl.BlockSpec((1, rows, ch), lambda z, ix: (z * q + lax.bitwise_xor(ix[0] % q, jnp.int32(e)), 0, 0))

    specs = [spec(e) for e in range(q)]
    return pl.pallas_call(
        functools.partial(sum_far_kernel, q=q),
        grid_spec=pltpu.PrefetchScalarGridSpec(
            num_scalar_prefetch=1,
            grid=(4,),
            in_specs=specs * 2,
            out_specs=[pl.BlockSpec((1, rows, ch), lambda z, ix: (z, 0, 0))] * q,
        ),
        out_shape=[SDS((4, rows, ch), BF)] * q,
        compiler_params=params(),
        cost_estimate=cost(n * rows * ch, n * rows * ch * 6),
        name="sum_far",
    )(idx, *([mine] * q), *([recv] * q))


def sum_near_kernel(idx_ref, *refs, q):
    for d in range(4):
        total = refs[d * q][...].astype(F32)
        for e in range(1, q):
            total = total + refs[d * q + e][...].astype(F32)
        refs[4 * q + d][...] = total[0].astype(BF)


def sum_near(idx, parts, n):
    q = n // 4
    _, rows, ch = parts[0].shape

    def spec(d):
        return pl.BlockSpec((1, rows, ch), lambda i, ix: (lax.bitwise_xor(ix[0] // q, jnp.int32(d)), 0, 0))

    return pl.pallas_call(
        functools.partial(sum_near_kernel, q=q),
        grid_spec=pltpu.PrefetchScalarGridSpec(
            num_scalar_prefetch=1,
            grid=(1,),
            in_specs=[spec(d) for d in range(4) for _ in range(q)],
            out_specs=[fixed((rows, ch))] * 4,
        ),
        out_shape=[SDS((rows, ch), BF)] * 4,
        compiler_params=params(),
        cost_estimate=cost(n * rows * ch, n * rows * ch * 3),
        name="sum_near",
    )(idx, *(list(parts) * 4))


def reduce_steps(idx, mine, recv, n, m):
    q = n // 4
    outs = sum_far(idx, mine, recv, n)
    parts = [outs[0]] + [xor_pp(outs[e], e, n) for e in range(1, q)]
    near = sum_near(idx, parts, n)
    total = near[0].astype(F32)
    for d in range(1, 4):
        total = total + xor_pp(near[d], d * q, n).astype(F32)
    b = 2
    while b < m:
        total = total + lax.ppermute(total.astype(BF), "dp", [(i, i ^ b) for i in range(m)]).astype(F32)
        b *= 2
    return total


def reduce_grad(idx, mine, theirs, n, m):
    rows, ch = mine.shape[0] // n, mine.shape[1]
    recv = core_swap(theirs, m)
    low = reduce_steps(idx, mine.reshape(n, rows, ch), recv.reshape(n, rows, ch), n, m).astype(BF)
    other = core_swap(low, m)
    first = idx[1] == 0
    return (
        jnp.where(first, low, other).astype(F32),
        jnp.where(first, other, low).astype(F32),
    )


def vec_table_kernel(*refs):
    a, b, c, u, o = refs
    d = a.shape[1]
    rows = jnp.concatenate(
        [c[0:2, :], b[0:2, :], a[3:4, :], a[1:3, :], a[0:1, :], u[...], jnp.zeros((116, d), F32)], axis=0
    )
    o[...] = rows.T.astype(BF)


def vec_table(s_mlp, s_qkv, s_tok, gbu):
    d = s_mlp.shape[1]
    return pl.pallas_call(
        vec_table_kernel, out_shape=SDS((d, 128), BF), compiler_params=params(0), name="vec_table"
    )(s_mlp, s_qkv, s_tok, gbu)


def local(
    tokens,
    sensor_tag,
    owner_order,
    ln1_gain,
    ln1_bias,
    w_qkv,
    b_query,
    b_value,
    w_out,
    b_out,
    ln2_gain,
    ln2_bias,
    w_up,
    b_up,
    w_down,
    b_down,
    out_grad,
    *,
    n,
    m,
):
    t, d = tokens.shape
    ff = w_up.shape[1]
    rows = d // n
    wide = ff // d
    f = lax.axis_index("fsdp")
    c = lax.axis_index("dp") % 2
    idx = jnp.stack([f, c]).astype(jnp.int32)
    use = idx if rows % 16 == 0 and n == 16 else jnp.zeros_like(idx)

    def core_half(x):
        h = x.shape[1] // 2
        return jnp.where(c == 0, x[:, :h], x[:, h:])

    vec = jnp.stack([ln1_gain, ln1_bias, b_query, b_value, b_out, ln2_gain, ln2_bias, b_down], axis=1)
    vec = jnp.concatenate([vec, b_up.reshape(wide, rows).T], axis=1)
    vec = jnp.pad(vec, ((0, 0), (0, 128 - vec.shape[1])))
    shard_a = jnp.concatenate([core_half(w_qkv), vec], axis=1)
    shard_b = core_half(jnp.concatenate([w_out, w_up], axis=1))
    shard_c = core_half(w_down)
    near_a = gather_near(shard_a, n)
    pieces_a = settle(gather_far(near_a, n, m), f, c, n)
    near_b = gather_near(shard_b, n)
    near_c = gather_near(shard_c, n)
    pieces_b = settle(gather_far(near_b, n, m), f, c, n)
    pieces_c = settle(gather_far(near_c, n, m), f, c, n)

    returned = lax.all_to_all(out_grad.astype(BF), "fsdp", split_axis=0, concat_axis=0, tiled=True)

    q, k, v, vt = qkv(use, tokens, pieces_a)
    mixed, lse = attend(sensor_tag, q, k, v)
    bu = vt[8 : 8 + wide].reshape(wide, n, rows).transpose(1, 0, 2).reshape(1, ff)
    x2, active, slope, y = mlp(use, tokens, mixed, vt, bu, pieces_b, pieces_c)
    sent = permute(owner_order.reshape(t, 1), y)
    encoded = lax.all_to_all(sent, "fsdp", split_axis=0, concat_axis=0, tiled=True).astype(F32)

    dm, du, dx2, da, do, h2, s_mlp, gbu = mlp_back(
        use, owner_order, returned, slope, x2, vt, pieces_b, pieces_c
    )
    down_mine, down_theirs = grad_down(idx, active, dm)
    g_down = reduce_grad(idx, down_mine, down_theirs, n, m)
    up_mine, up_theirs = grad_up(idx, h2, mixed, du, da)
    g_up = reduce_grad(idx, up_mine, up_theirs, n, m)
    dq, dk, dv = attend_back(sensor_tag, q, k, v, do, mixed, lse)
    qkv_mine, qkv_theirs, s_qkv = grad_qkv(idx, tokens, vt, dq, dk, dv)
    g_qkv = reduce_grad(idx, qkv_mine, qkv_theirs, n, m)
    tokens_grad, s_tok = tokens_back(use, dq, dk, dv, tokens, vt, dx2, pieces_a)

    gbu = gbu.reshape(n, wide, rows).transpose(1, 0, 2).reshape(wide, d)
    table = vec_table(s_mlp, s_qkv, s_tok, gbu)
    table_swap = core_swap(table, m)
    vecs = reduce_steps(idx, table.reshape(n, rows, 128), table_swap.reshape(n, rows, 128), n, m)
    vecs = vecs.T

    def join(pair, parts, width):
        out = []
        for p in range(parts):
            out += [pair[0][:, p * width : (p + 1) * width], pair[1][:, p * width : (p + 1) * width]]
        return jnp.concatenate(out, axis=1)

    h = d // 2
    grad_qkv_out = join(g_qkv, 3, h)
    grad_up_out = join((g_up[0][:, : ff // 2], g_up[1][:, : ff // 2]), wide, h)
    grad_out_out = join((g_up[0][:, ff // 2 :], g_up[1][:, ff // 2 :]), 1, h)
    grad_down_out = join(g_down, 1, h)
    return (
        encoded,
        tokens_grad,
        vecs[0],
        vecs[1],
        grad_qkv_out,
        vecs[2],
        vecs[3],
        grad_out_out,
        vecs[4],
        vecs[5],
        vecs[6],
        grad_up_out,
        vecs[8 : 8 + wide].reshape(ff // n),
        grad_down_out,
        vecs[7],
    )


def solution(mesh):
    n = mesh.shape["fsdp"]
    m = mesh.shape["dp"]
    both = P(("dp", "fsdp"), None)
    vec = P("fsdp")
    mat = P("fsdp", None)
    in_specs = (both, P(("dp", "fsdp")), both, vec, vec, mat, vec, vec, mat, vec, vec, vec, mat, vec, mat, vec, both)
    out_specs = (both, both, vec, vec, mat, vec, vec, mat, vec, vec, vec, mat, vec, mat, vec)
    return jax.shard_map(
        functools.partial(local, n=n, m=m), mesh=mesh, in_specs=in_specs, out_specs=out_specs, check_vma=False
    )
```

time: 1580 us -> 649 us (0.41)
  matrix products: 566 us -> 0 us
  Pallas kernels: 0 us -> 311 us
  blocking collectives: 225 us -> 0 us
  other arithmetic: 239 us -> 20 us
  local copies, waits for them, and re-layouts: 203 us -> 16.8 us
  waiting for transfers between devices: 281 us -> 196 us
  starting transfers between devices: 13.5 us -> 94.9 us
  loops' own time: 25.8 us -> 0 us
  between operations: 17.8 us -> 1.67 us
    dot_general x40 -> x0, matrix products: 566 us -> none  [the longest x4 70.3 us: one_one_block(): jnp.einsum('qhe,khe->hqk', grad_block, value_four[row_at], preferred_elem...]
    pallas_call x0 -> x19, Pallas kernels: none -> 311 us  [the longest x1 51 us: mlp(): pl.pallas_call(functools.partial(mlp_kernel, fc=fc), grid_spec=pltpu.Pref...]
    reduce_scatter x4 -> x0, waiting for transfers between devices: 278 us -> none  [the longest x1 143 us: local(): lax.psum_scatter(grad_up.astype(jnp.bfloat16), 'fsdp', scatter_dimension=...]
    unnamed x2 -> x0, blocking collectives: 223 us -> none
    ppermute x0 -> x61, waiting for transfers between devices: none -> 196 us  [the longest x42 194 us: xor_pp(): return lax.ppermute(x, 'fsdp', [(i, i ^ b) for i in range(n)])]
    convert_element_type x30 -> x7, other arithmetic: 115 us -> 12 us  [the longest x1 5.08 us: local(): lax.all_to_all(sent, 'fsdp', split_axis=0, concat_axis=0, tiled=True)]
    reduce_sum x15 -> x0, other arithmetic: 88.6 us -> none  [the longest x4 46.6 us: attend_one_block(): row_total = jnp.sum(weights, axis=-1, keepdims=True)]
    ppermute x0 -> x61, starting transfers between devices: none -> 79.8 us  [the longest x42 56.1 us: xor_pp(): return lax.ppermute(x, 'fsdp', [(i, i ^ b) for i in range(n)])]
  transfers between devices with their start and end apart: 11 -> 63, of which waited for: 2 -> 26; matrix products, arithmetic and copies ran while one was open for 58% -> 4% of each run, Pallas kernels for 0% -> 49%
where the time goes in v1:
time: 649 us; the launch traced here: 640 us
  Pallas kernels  311 us (48%)
  waiting for transfers between devices  196 us (30%)
  starting transfers between devices  94.9 us (15%)
  other arithmetic  20 us (3%)
  local copies, waits for them, and re-layouts  16.8 us (3%)
    ppermute x42, waiting for transfers between devices, xor_pp(): return lax.ppermute(x, 'fsdp', [(i, i ^ b) for i in range(n)])  194 us
    ppermute x42, starting transfers between devices, xor_pp(): return lax.ppermute(x, 'fsdp', [(i, i ^ b) for i in range(n)])  56.1 us
    pallas_call x1, Pallas kernels, mlp(): pl.pallas_call(functools.partial(mlp_kernel, fc=fc), grid_spec=pltpu.Pref...  51 us
    pallas_call x1, Pallas kernels, attend_back(): pl.pallas_call(functools.partial(attend_back_kernel, kb=kb, qb=qb), grid_...  50 us
    pallas_call x1, Pallas kernels, mlp_back(): pl.pallas_call(functools.partial(mlp_back_kernel, fc=fc), grid_spec=pltpu...  47.8 us
    pallas_call x1, Pallas kernels, attend(): pl.pallas_call(functools.partial(attend_kernel, qb=qb), grid_spec=pltpu.P...  34 us
    ppermute x19, starting transfers between devices, core_swap(): return lax.ppermute(x, 'dp', [(i, i ^ 1) for i in range(m)])  23.8 us
    pallas_call x1, Pallas kernels, grad_up(): pl.pallas_call(functools.partial(grad_up_kernel, steps=steps), grid_spec=...  20.2 us
  transfers between devices with their start and end apart: 63, of which 26 were waited for; matrix products, arithmetic and copies ran while one was open for 4% of the time, Pallas kernels for 49%

profile of v1, /device:TPU:0, one launch (start us, length us, event | category | flops | bytes accessed | tf_op | source)
XLA Modules:
  0.0 639.5 jit_solution(12905988201197116866)
XLA Ops:
  11.1 7.7 %collective-permute-done.1 = bf16[48,1280]{1,0:T(8,128)(2,1)S(1)} collective-permute-done((bf16[48,1280]{1,0:T(8,128)(2,1)S(1)}, bf16[48,1280]{1,0:T(8,128)(2,1)S(1)}, u32[]{:S(2)}, u32[]{:S(2)}) %collective-permute-start.1) | collective-permute-done | bytes 122912 | tf_op jit(solution)/shard_map/ppermute | solution.py:60
  28.9 15.8 %collective-permute-done.21 = bf16[192,384]{1,0:T(8,128)(2,1)S(1)} collective-permute-done((bf16[192,384]{1,0:T(8,128)(2,1)S(1)}, bf16[192,384]{1,0:T(8,128)(2,1)S(1)}, u32[]{:S(2)}, u32[]{:S(2)}) %collective-permute-start.21) | collective-permute-done | bytes 147488 | tf_op jit(solution)/shard_map/ppermute | solution.py:60
  53.7 16.5 %collective-permute-done.4.refs_2_ = bf16[4,48,1280]{2,1,0:T(8,128)(2,1)} collective-permute-done((bf16[4,48,1280]{2,1,0:T(8,128)(2,1)S(1)}, bf16[4,48,1280]{2,1,0:T(8,128)(2,1)}, u32[]{:S(2)}, u32[]{:S(2)}) %collective-permute-start.4) | collective-permute-done | bytes 491552 | tf_op jit(solution)/shard_map/ppermute | solution.py:60
  71.2 21.5 %collective-permute-done.24.refs_10_ = bf16[4,192,384]{2,1,0:T(8,128)(2,1)} collective-permute-done((bf16[4,192,384]{2,1,0:T(8,128)(2,1)}, bf16[4,192,384]{2,1,0:T(8,128)(2,1)}, u32[]{:S(2)}, u32[]{:S(2)}) %collective-permute-start.24) | collective-permute-done | bytes 589856 | tf_op jit(solution)/shard_map/ppermute | solution.py:60
  109.5 14.2 %qkv.1 = (bf16[2048,768]{1,0:T(8,128)(2,1)}, bf16[2048,768]{1,0:T(8,128)(2,1)}, bf16[2048,768]{1,0:T(8,128)(2,1)}, f32[16,768]{1,0:T(8,128)}) custom-call(s32[2]{0:T(128)} %pad_add_fusion.idx_ref, bf16[2048,768]{1,0:T(8,128)(2,1)} %x_ref.7, bf16[4,48,1280]{2,1,0:T(8,128)(2,1)} %copy-done.13, bf16[4,48,1280]{2,1,0:T(8,128)(2,1)} %collective-permute-done.3.refs_1_, ...), custom_call_target="tpu_custom_call" | custom-call | flops 7247757312 | bytes 16121856 | tf_op jit(solution)/shard_map/qkv/pallas_call | solution.py:152
  123.8 9.5 %collective-permute-done.13.refs_1_ = bf16[4,48,1920]{2,1,0:T(8,128)(2,1)} collective-permute-done((bf16[4,48,1920]{2,1,0:T(8,128)(2,1)S(1)}, bf16[4,48,1920]{2,1,0:T(8,128)(2,1)}, u32[]{:S(2)}, u32[]{:S(2)}) %collective-permute-start.13) | collective-permute-done | bytes 737312 | tf_op jit(solution)/shard_map/ppermute | solution.py:60
  133.3 31.0 %collective-permute-done.14.refs_2_ = bf16[4,48,1920]{2,1,0:T(8,128)(2,1)} collective-permute-done((bf16[4,48,1920]{2,1,0:T(8,128)(2,1)S(1)}, bf16[4,48,1920]{2,1,0:T(8,128)(2,1)}, u32[]{:S(2)}, u32[]{:S(2)}) %collective-permute-start.14) | collective-permute-done | bytes 737312 | tf_op jit(solution)/shard_map/ppermute | solution.py:60
  164.2 13.5 %collective-permute-done.15.refs_3_ = bf16[4,48,1920]{2,1,0:T(8,128)(2,1)} collective-permute-done((bf16[4,48,1920]{2,1,0:T(8,128)(2,1)S(1)}, bf16[4,48,1920]{2,1,0:T(8,128)(2,1)}, u32[]{:S(2)}, u32[]{:S(2)}) %collective-permute-start.15) | collective-permute-done | bytes 737312 | tf_op jit(solution)/shard_map/ppermute | solution.py:60
  178.4 34.0 %attend.1 = (bf16[2048,768]{1,0:T(8,128)(2,1)}, f32[2,6,2,1024]{3,2,1,0:T(2,128)}) custom-call(s32[2]{0:T(128)} %tag_ref.3, bf16[2048,768]{1,0:T(8,128)(2,1)} %get-tuple-element.77.q_ref, bf16[2048,768]{1,0:T(8,128)(2,1)} %get-tuple-element.78.k_ref, bf16[2048,768]{1,0:T(8,128)(2,1)} %get-tuple-element.79.v_ref), custom_call_target="tpu_custom_call" | custom-call | flops 25769803776 | bytes 12582912 | tf_op jit(solution)/shard_map/attend/pallas_call | solution.py:216
  213.9 51.0 %mlp.1 = (f32[2048,768]{1,0:T(8,128)}, bf16[2048,3072]{1,0:T(8,128)(2,1)}, bf16[2048,3072]{1,0:T(8,128)(2,1)}, bf16[2048,768]{1,0:T(8,128)(2,1)}) custom-call(s32[2]{0:T(128)} %pad_add_fusion.idx_ref, bf16[2048,768]{1,0:T(8,128)(2,1)} %x_ref.7, bf16[2048,768]{1,0:T(8,128)(2,1)} %get-tuple-element.80.o_ref, f32[16,768]{1,0:T(8,128)} %get-tuple-element.81.vt_ref, ...), custom_call_target="tpu_custom_call" | custom-call | flops 43486543872 | bytes 50331648 | tf_op jit(solution)/shard_map/mlp/pallas_call | solution.py:274
  264.9 10.3 %permute.1 = bf16[2048,768]{1,0:T(8,128)(2,1)} custom-call(s32[2048,1]{1,0:T(8,128)} %copy.57.ord_ref, bf16[2048,768]{1,0:T(8,128)(2,1)} %get-tuple-element.82.y_ref), custom_call_target="tpu_custom_call" | custom-call | flops 6442450944 | bytes 6291456 | tf_op jit(solution)/shard_map/permute/pallas_call | solution.py:303
  276.9 10.2 %all-to-all-start = ((bf16[16,128,768]{2,1,0:T(8,128)(2,1)}), bf16[16,128,768]{2,1,0:T(8,128)(2,1)}, u32[]{:S(2)}, u32[]{:S(2)}) async-start(bf16[16,128,768]{2,1,0:T(8,128)(2,1)} %bitcast.68), calls=%async_computation | async-start | bytes 6291456 | tf_op jit(solution)/shard_map/all_to_all | solution.py:784
  287.1 47.8 %mlp_back.1 = (bf16[2048,768]{1,0:T(8,128)(2,1)}, bf16[2048,3072]{1,0:T(8,128)(2,1)}, f32[2048,768]{1,0:T(8,128)}, bf16[2048,768]{1,0:T(8,128)(2,1)}, bf16[2048,...) custom-call(s32[2]{0:T(128)} %pad_add_fusion.idx_ref, s32[1,2048]{1,0:T(1,128)} %ord_ref.1, ...), custom_call_target="tpu_custom_call" | custom-call | flops 42278584320 | bytes 56623104 | tf_op jit(solution)/shard_map/mlp_back/pallas_call | solution.py:364
  334.9 15.5 %grad_down.1 = (bf16[3072,384]{1,0:T(8,128)(2,1)}, bf16[3072,384]{1,0:T(8,128)(2,1)}) custom-call(s32[2]{0:T(128)} %pad_add_fusion.idx_ref, bf16[2048,3072]{1,0:T(8,128)(2,1)} %get-tuple-element.127.g_ref, bf16[2048,768]{1,0:T(8,128)(2,1)} %get-tuple-element.128.dm_ref), custom_call_target="tpu_custom_call" | custom-call | flops 14495514624 | bytes 20447232 | tf_op jit(solution)/shard_map/grad_down/pallas_call | solution.py:417
  352.9 50.0 %attend_back.1 = (bf16[2048,768]{1,0:T(8,128)(2,1)}, bf16[2048,768]{1,0:T(8,128)(2,1)}, bf16[2048,768]{1,0:T(8,128)(2,1)}) custom-call(s32[2]{0:T(128)} %tag_ref.3, bf16[2048,768]{1,0:T(8,128)(2,1)} %get-tuple-element.77.q_ref, bf16[2048,768]{1,0:T(8,128)(2,1)} %get-tuple-element.78.k_ref, bf16[2048,768]{1,0:T(8,128)(2,1)} %get-tuple-element.79.v_ref, ...), custom_call_target="tpu_custom_call" | custom-call | flops 64424509440 | bytes 25165824 | tf_op jit(solution)/shard_map/attend_back/pallas_call | solution.py:531
  402.9 16.7 %grad_qkv.1 = (bf16[768,1152]{1,0:T(8,128)(2,1)}, bf16[768,1152]{1,0:T(8,128)(2,1)}, f32[8,768]{1,0:T(8,128)}) custom-call(s32[2]{0:T(128)} %pad_add_fusion.idx_ref, bf16[2048,768]{1,0:T(8,128)(2,1)} %x_ref.7, f32[16,768]{1,0:T(8,128)} %get-tuple-element.81.vt_ref, bf16[2048,768]{1,0:T(8,128)(2,1)} %get-tuple-element.87.dq_ref, ...), custom_call_target="tpu_custom_call" | custom-call | flops 10871635968 | bytes 15728640 | tf_op jit(solution)/shard_map/grad_qkv/pallas_call | solution.py:568
  419.6 18.8 %collective-permute-start.37 = (bf16[768,1152]{1,0:T(8,128)(2,1)}, bf16[768,1152]{1,0:T(8,128)(2,1)}, u32[]{:S(2)}, u32[]{:S(2)}) collective-permute-start(bf16[768,1152]{1,0:T(8,128)(2,1)} %get-tuple-element.105), channel_id=1, source_target_pairs={{0,16},{16,0},{1,17},{17,1},{2,18},{18,2},{3,19},{19,3},{4,20},{20... | collective-permute-start | bytes 5308424 | tf_op jit(solution)/shard_map/ppermute | solution.py:64
  438.4 20.2 %grad_up.1 = (bf16[768,1920]{1,0:T(8,128)(2,1)}, bf16[768,1920]{1,0:T(8,128)(2,1)}) custom-call(s32[2]{0:T(128)} %pad_add_fusion.idx_ref, bf16[2048,768]{1,0:T(8,128)(2,1)} %get-tuple-element.114.h2_ref, bf16[2048,768]{1,0:T(8,128)(2,1)} %get-tuple-element.80.o_ref, bf16[2048,3072]{1,0:T(8,128)(2,1)} %get-tuple-element.115.du_ref, ...), custom_call_target="tpu_custom_call" | custom-call | flops 18119393280 | bytes 26738688 | tf_op jit(solution)/shard_map/grad_up/pallas_call | solution.py:448
  458.7 17.9 %tokens_back.1 = (f32[2048,768]{1,0:T(8,128)}, f32[8,768]{1,0:T(8,128)}) custom-call(s32[2]{0:T(128)} %pad_add_fusion.idx_ref, bf16[2048,768]{1,0:T(8,128)(2,1)} %get-tuple-element.87.dq_ref, bf16[2048,768]{1,0:T(8,128)(2,1)} %get-tuple-element.88.dk_ref, bf16[2048,768]{1,0:T(8,128)(2,1)} %get-tuple-element.89.dv_ref, bf16[2048,768]{1,0:T(8,128)(2,1)} %x_ref.7, ...), custom_call_target="tpu_custom_call" | custom-call | flops 10871635968 | bytes 28704768 | tf_op jit(solution)/shard_map/tokens_back/pallas_call | solution.py:611
  512.4 8.9 %collective-permute-done.38.refs_1_.refs_5_.refs_9_.refs_13_ = bf16[4,48,1152]{2,1,0:T(8,128)(2,1)S(1)} collective-permute-done((bf16[4,48,1152]{2,1,0:T(8,128)(2,1)}, bf16[4,48,1152]{2,1,0:T(8,128)(2,1)S(1)}, u32[]{:S(2)}, u32[]{:S(2)}) %collective-permute-start.38) | collective-permute-done | bytes 442400 | tf_op jit(solution)/shard_map/ppermute | solution.py:60
  573.1 10.1 %collective-permute-done.55.refs_2_.refs_6_.refs_10_.refs_14_ = bf16[4,192,384]{2,1,0:T(8,128)(2,1)} collective-permute-done((bf16[4,192,384]{2,1,0:T(8,128)(2,1)}, bf16[4,192,384]{2,1,0:T(8,128)(2,1)}, u32[]{:S(2)}, u32[]{:S(2)}) %collective-permute-start.55) | collective-permute-done | bytes 589856 | tf_op jit(solution)/shard_map/ppermute | solution.py:60
  588.4 10.1 %collective-permute-done.46.refs_1_.refs_5_.refs_9_.refs_13_ = bf16[4,48,1920]{2,1,0:T(8,128)(2,1)S(1)} collective-permute-done((bf16[4,48,1920]{2,1,0:T(8,128)(2,1)}, bf16[4,48,1920]{2,1,0:T(8,128)(2,1)S(1)}, u32[]{:S(2)}, u32[]{:S(2)}) %collective-permute-start.46) | collective-permute-done | bytes 737312 | tf_op jit(solution)/shard_map/ppermute | solution.py:60
  600.4 13.6 %collective-permute-done.47.refs_2_.refs_6_.refs_10_.refs_14_ = bf16[4,48,1920]{2,1,0:T(8,128)(2,1)S(1)} collective-permute-done((bf16[4,48,1920]{2,1,0:T(8,128)(2,1)}, bf16[4,48,1920]{2,1,0:T(8,128)(2,1)S(1)}, u32[]{:S(2)}, u32[]{:S(2)}) %collective-permute-start.47) | collective-permute-done | bytes 737312 | tf_op jit(solution)/shard_map/ppermute | solution.py:60
  627.7 7.8 %collective-permute-done.50 = bf16[48,1920]{1,0:T(8,128)(2,1)S(1)} collective-permute-done((bf16[48,1920]{1,0:T(8,128)(2,1)}, bf16[48,1920]{1,0:T(8,128)(2,1)S(1)}, u32[]{:S(2)}, u32[]{:S(2)}) %collective-permute-start.50) | collective-permute-done | bytes 184352 | tf_op jit(solution)/shard_map/ppermute | solution.py:60
  (224 shorter events, 165.4 us)
Async XLA Ops:
  52.1 40.5 %collective-permute-start.24 = (bf16[4,192,384]{2,1,0:T(8,128)(2,1)}, bf16[4,192,384]{2,1,0:T(8,128)(2,1)}, u32[]{:S(2)}, u32[]{:S(2)}) collective-permute-start(bf16[4,192,384]{2,1,0:T(8,128)(2,1)} %pad_maximum_fusion.1.refs_8_), channel_id=1, source_target_pairs={{0,2},{1,3},{2,0},{3,1},{4,6},{5,7},{6,4},{7,5},{8,10},{9,11},{10,... | collective-permute-start | bytes 1769480 | tf_op jit(solution)/shard_map/ppermute | solution.py:60
  70.3 34.5 %collective-permute-start.25 = (bf16[4,192,384]{2,1,0:T(8,128)(2,1)}, bf16[4,192,384]{2,1,0:T(8,128)(2,1)}, u32[]{:S(2)}, u32[]{:S(2)}) collective-permute-start(bf16[4,192,384]{2,1,0:T(8,128)(2,1)} %pad_maximum_fusion.1.refs_8_), channel_id=1, source_target_pairs={{0,3},{1,2},{2,1},{3,0},{4,7},{5,6},{6,5},{7,4},{8,11},{9,10},{10,... | collective-permute-start | bytes 1769480 | tf_op jit(solution)/shard_map/ppermute | solution.py:60
  70.3 36.5 %collective-permute-start.26 = (bf16[4,192,384]{2,1,0:T(8,128)(2,1)}, bf16[4,192,384]{2,1,0:T(8,128)(2,1)}, u32[]{:S(2)}, u32[]{:S(2)}) collective-permute-start(bf16[4,192,384]{2,1,0:T(8,128)(2,1)} %pad_maximum_fusion.1.refs_8_), channel_id=1, source_target_pairs={{0,16},{16,0},{1,17},{17,1},{2,18},{18,2},{3,19},{19,3},{4,20},{20... | collective-permute-start | bytes 1769480 | tf_op jit(solution)/shard_map/ppermute | solution.py:64
  70.3 38.0 %collective-permute-start.7 = (bf16[4,48,1280]{2,1,0:T(8,128)(2,1)}, bf16[4,48,1280]{2,1,0:T(8,128)(2,1)}, u32[]{:S(2)}, u32[]{:S(2)}) collective-permute-start(bf16[4,48,1280]{2,1,0:T(8,128)(2,1)} %collective-permute-done.3.refs_1_), channel_id=1, source_target_pairs={{0,16},{16,0},{1,17},{17,1},{2,18},{18,2},{3,19},{19,3},{4,20},{20... | collective-permute-start | bytes 1474568 | tf_op jit(solution)/shard_map/ppermute | solution.py:64
  71.2 37.2 %collective-permute-start.8 = (bf16[4,48,1280]{2,1,0:T(8,128)(2,1)}, bf16[4,48,1280]{2,1,0:T(8,128)(2,1)}, u32[]{:S(2)}, u32[]{:S(2)}) collective-permute-start(bf16[4,48,1280]{2,1,0:T(8,128)(2,1)} %collective-permute-done.4.refs_2_), channel_id=1, source_target_pairs={{0,16},{16,0},{1,17},{17,1},{2,18},{18,2},{3,19},{19,3},{4,20},{20... | collective-permute-start | bytes 1474568 | tf_op jit(solution)/shard_map/ppermute | solution.py:64
  97.4 177.8 %all-to-all-start.1 = ((bf16[16,128,768]{2,1,0:T(8,128)(2,1)}), bf16[16,128,768]{2,1,0:T(8,128)(2,1)S(1)}, u32[]{:S(2)}, u32[]{:S(2)}) async-start(bf16[16,128,768]{2,1,0:T(8,128)(2,1)} %bitcast.27), calls=%async_computation.1 | async-start | bytes 6291456 | tf_op jit(solution)/shard_map/all_to_all | solution.py:777
  106.8 57.4 %collective-permute-start.14 = (bf16[4,48,1920]{2,1,0:T(8,128)(2,1)S(1)}, bf16[4,48,1920]{2,1,0:T(8,128)(2,1)}, u32[]{:S(2)}, u32[]{:S(2)}) collective-permute-start(bf16[4,48,1920]{2,1,0:T(8,128)(2,1)S(1)} %pad_maximum_fusion.refs_0_), channel_id=1, source_target_pairs={{0,2},{1,3},{2,0},{3,1},{4,6},{5,7},{6,4},{7,5},{8,10},{9,11},{10,... | collective-permute-start | bytes 2211848 | tf_op jit(solution)/shard_map/ppermute | solution.py:60
  108.3 69.5 %collective-permute-start.15 = (bf16[4,48,1920]{2,1,0:T(8,128)(2,1)S(1)}, bf16[4,48,1920]{2,1,0:T(8,128)(2,1)}, u32[]{:S(2)}, u32[]{:S(2)}) collective-permute-start(bf16[4,48,1920]{2,1,0:T(8,128)(2,1)S(1)} %pad_maximum_fusion.refs_0_), channel_id=1, source_target_pairs={{0,3},{1,2},{2,1},{3,0},{4,7},{5,6},{6,5},{7,4},{8,11},{9,10},{10,... | collective-permute-start | bytes 2211848 | tf_op jit(solution)/shard_map/ppermute | solution.py:60
  108.4 69.4 %collective-permute-start.16 = (bf16[4,48,1920]{2,1,0:T(8,128)(2,1)S(1)}, bf16[4,48,1920]{2,1,0:T(8,128)(2,1)S(1)}, u32[]{:S(2)}, u32[]{:S(2)}) collective-permute-start(bf16[4,48,1920]{2,1,0:T(8,128)(2,1)S(1)} %pad_maximum_fusion.refs_0_), channel_id=1, source_target_pairs={{0,16},{16,0},{1,17},{17,1},{2,18},{18,2},{3,19},{19,3},{4,20},{20... | collective-permute-start | bytes 2211848 | tf_op jit(solution)/shard_map/ppermute | solution.py:64
  109.0 69.3 %collective-permute-start.27 = (bf16[4,192,384]{2,1,0:T(8,128)(2,1)}, bf16[4,192,384]{2,1,0:T(8,128)(2,1)S(1)}, u32[]{:S(2)}, u32[]{:S(2)}) collective-permute-start(bf16[4,192,384]{2,1,0:T(8,128)(2,1)} %copy-done.23), channel_id=1, source_target_pairs={{0,16},{16,0},{1,17},{17,1},{2,18},{18,2},{3,19},{19,3},{4,20},{20... | collective-permute-start | bytes 1769480 | tf_op jit(solution)/shard_map/ppermute | solution.py:64
  133.2 80.6 %collective-permute-start.28 = (bf16[4,192,384]{2,1,0:T(8,128)(2,1)}, bf16[4,192,384]{2,1,0:T(8,128)(2,1)}, u32[]{:S(2)}, u32[]{:S(2)}) collective-permute-start(bf16[4,192,384]{2,1,0:T(8,128)(2,1)} %collective-permute-done.24.refs_10_), channel_id=1, source_target_pairs={{0,16},{16,0},{1,17},{17,1},{2,18},{18,2},{3,19},{19,3},{4,20},{20... | collective-permute-start | bytes 1769480 | tf_op jit(solution)/shard_map/ppermute | solution.py:64
  164.2 49.7 %collective-permute-start.29 = (bf16[4,192,384]{2,1,0:T(8,128)(2,1)}, bf16[4,192,384]{2,1,0:T(8,128)(2,1)}, u32[]{:S(2)}, u32[]{:S(2)}) collective-permute-start(bf16[4,192,384]{2,1,0:T(8,128)(2,1)} %collective-permute-done.25.refs_11_), channel_id=1, source_target_pairs={{0,16},{16,0},{1,17},{17,1},{2,18},{18,2},{3,19},{19,3},{4,20},{20... | collective-permute-start | bytes 1769480 | tf_op jit(solution)/shard_map/ppermute | solution.py:64
  177.8 36.1 %collective-permute-start.17 = (bf16[4,48,1920]{2,1,0:T(8,128)(2,1)}, bf16[4,48,1920]{2,1,0:T(8,128)(2,1)}, u32[]{:S(2)}, u32[]{:S(2)}) collective-permute-start(bf16[4,48,1920]{2,1,0:T(8,128)(2,1)} %collective-permute-done.13.refs_1_), channel_id=1, source_target_pairs={{0,16},{16,0},{1,17},{17,1},{2,18},{18,2},{3,19},{19,3},{4,20},{20... | collective-permute-start | bytes 2211848 | tf_op jit(solution)/shard_map/ppermute | solution.py:64
  177.8 36.1 %collective-permute-start.18 = (bf16[4,48,1920]{2,1,0:T(8,128)(2,1)}, bf16[4,48,1920]{2,1,0:T(8,128)(2,1)}, u32[]{:S(2)}, u32[]{:S(2)}) collective-permute-start(bf16[4,48,1920]{2,1,0:T(8,128)(2,1)} %collective-permute-done.14.refs_2_), channel_id=1, source_target_pairs={{0,16},{16,0},{1,17},{17,1},{2,18},{18,2},{3,19},{19,3},{4,20},{20... | collective-permute-start | bytes 2211848 | tf_op jit(solution)/shard_map/ppermute | solution.py:64
  178.3 35.6 %collective-permute-start.19 = (bf16[4,48,1920]{2,1,0:T(8,128)(2,1)}, bf16[4,48,1920]{2,1,0:T(8,128)(2,1)}, u32[]{:S(2)}, u32[]{:S(2)}) collective-permute-start(bf16[4,48,1920]{2,1,0:T(8,128)(2,1)} %collective-permute-done.15.refs_3_), channel_id=1, source_target_pairs={{0,16},{16,0},{1,17},{17,1},{2,18},{18,2},{3,19},{19,3},{4,20},{20... | collective-permute-start | bytes 2211848 | tf_op jit(solution)/shard_map/ppermute | solution.py:64
  276.9 266.5 %all-to-all-start = ((bf16[16,128,768]{2,1,0:T(8,128)(2,1)}), bf16[16,128,768]{2,1,0:T(8,128)(2,1)}, u32[]{:S(2)}, u32[]{:S(2)}) async-start(bf16[16,128,768]{2,1,0:T(8,128)(2,1)} %bitcast.68), calls=%async_computation | async-start | bytes 6291456 | tf_op jit(solution)/shard_map/all_to_all | solution.py:784
  350.3 198.2 %collective-permute-start.53 = (bf16[3072,384]{1,0:T(8,128)(2,1)}, bf16[3072,384]{1,0:T(8,128)(2,1)}, u32[]{:S(2)}, u32[]{:S(2)}) collective-permute-start(bf16[3072,384]{1,0:T(8,128)(2,1)} %get-tuple-element.130), channel_id=1, source_target_pairs={{0,16},{16,0},{1,17},{17,1},{2,18},{18,2},{3,19},{19,3},{4,20},{20... | collective-permute-start | bytes 7077896 | tf_op jit(solution)/shard_map/ppermute | solution.py:64
  419.6 83.1 %collective-permute-start.37 = (bf16[768,1152]{1,0:T(8,128)(2,1)}, bf16[768,1152]{1,0:T(8,128)(2,1)}, u32[]{:S(2)}, u32[]{:S(2)}) collective-permute-start(bf16[768,1152]{1,0:T(8,128)(2,1)} %get-tuple-element.105), channel_id=1, source_target_pairs={{0,16},{16,0},{1,17},{17,1},{2,18},{18,2},{3,19},{19,3},{4,20},{20... | collective-permute-start | bytes 5308424 | tf_op jit(solution)/shard_map/ppermute | solution.py:64
  458.6 98.6 %collective-permute-start.45 = (bf16[768,1920]{1,0:T(8,128)(2,1)}, bf16[768,1920]{1,0:T(8,128)(2,1)S(1)}, u32[]{:S(2)}, u32[]{:S(2)}) collective-permute-start(bf16[768,1920]{1,0:T(8,128)(2,1)} %get-tuple-element.118), channel_id=1, source_target_pairs={{0,16},{16,0},{1,17},{17,1},{2,18},{18,2},{3,19},{19,3},{4,20},{20... | collective-permute-start | bytes 8847368 | tf_op jit(solution)/shard_map/ppermute | solution.py:64
  564.4 34.1 %collective-permute-start.46 = (bf16[4,48,1920]{2,1,0:T(8,128)(2,1)}, bf16[4,48,1920]{2,1,0:T(8,128)(2,1)S(1)}, u32[]{:S(2)}, u32[]{:S(2)}) collective-permute-start(bf16[4,48,1920]{2,1,0:T(8,128)(2,1)} %get-tuple-element.120), channel_id=1, source_target_pairs={{0,1},{1,0},{2,3},{3,2},{4,5},{5,4},{6,7},{7,6},{8,9},{9,8},{10,11... | collective-permute-start | bytes 2211848 | tf_op jit(solution)/shard_map/ppermute | solution.py:60
  565.7 48.3 %collective-permute-start.47 = (bf16[4,48,1920]{2,1,0:T(8,128)(2,1)}, bf16[4,48,1920]{2,1,0:T(8,128)(2,1)S(1)}, u32[]{:S(2)}, u32[]{:S(2)}) collective-permute-start(bf16[4,48,1920]{2,1,0:T(8,128)(2,1)} %get-tuple-element.121), channel_id=1, source_target_pairs={{0,2},{1,3},{2,0},{3,1},{4,6},{5,7},{6,4},{7,5},{8,10},{9,11},{10,... | collective-permute-start | bytes 2211848 | tf_op jit(solution)/shard_map/ppermute | solution.py:60
  570.0 44.0 %collective-permute-start.48 = (bf16[4,48,1920]{2,1,0:T(8,128)(2,1)}, bf16[4,48,1920]{2,1,0:T(8,128)(2,1)S(1)}, u32[]{:S(2)}, u32[]{:S(2)}) collective-permute-start(bf16[4,48,1920]{2,1,0:T(8,128)(2,1)} %get-tuple-element.122), channel_id=1, source_target_pairs={{0,3},{1,2},{2,1},{3,0},{4,7},{5,6},{6,5},{7,4},{8,11},{9,10},{10,... | collective-permute-start | bytes 2211848 | tf_op jit(solution)/shard_map/ppermute | solution.py:60
  586.6 34.1 %collective-permute-start.57 = (bf16[192,384]{1,0:T(8,128)(2,1)}, bf16[192,384]{1,0:T(8,128)(2,1)S(1)}, u32[]{:S(2)}, u32[]{:S(2)}) collective-permute-start(bf16[192,384]{1,0:T(8,128)(2,1)} %get-tuple-element.136), channel_id=1, source_target_pairs={{0,4},{1,5},{2,6},{3,7},{4,0},{5,1},{6,2},{7,3},{8,12},{9,13},{10,... | collective-permute-start | bytes 442376 | tf_op jit(solution)/shard_map/ppermute | solution.py:60
  586.6 36.6 %collective-permute-start.58 = (bf16[192,384]{1,0:T(8,128)(2,1)}, bf16[192,384]{1,0:T(8,128)(2,1)S(1)}, u32[]{:S(2)}, u32[]{:S(2)}) collective-permute-start(bf16[192,384]{1,0:T(8,128)(2,1)} %get-tuple-element.137), channel_id=1, source_target_pairs={{0,8},{1,9},{2,10},{3,11},{4,12},{5,13},{6,14},{7,15},{8,0},{9,1},... | collective-permute-start | bytes 442376 | tf_op jit(solution)/shard_map/ppermute | solution.py:60
  (65 other events, 1024.7 us)

commit v2 on v1

--- a/solution.py
+++ b/solution.py
@@ -32,7 +32,7 @@
 
 
 def cost(flops, nbytes, trans=0):
-    return pl.CostEstimate(flops=int(flops), bytes_accessed=int(nbytes), transcendentals=int(trans))
+    return pl.CostEstimate(flops=int(flops) >> 10, bytes_accessed=int(nbytes) >> 10, transcendentals=int(trans) >> 10)
 
 
 def rows_of(height, width):
@@ -56,6 +56,10 @@
     return c, lax.rsqrt(var + EPS)
 
 
+def after(x, *deps):
+    return lax.optimization_barrier((x,) + deps)[0]
+
+
 def xor_pp(x, b, n):
     return lax.ppermute(x, "fsdp", [(i, i ^ b) for i in range(n)])
 
@@ -69,17 +73,21 @@
     return jnp.stack([x] + [xor_pp(x, d * q, n) for d in (1, 2, 3)])
 
 
-def gather_far(s, n, m):
-    own = [s] + [xor_pp(s, e, n) for e in range(1, n // 4)]
-    return own + [core_swap(t, m) for t in own]
-
-
-def settle(pieces, f, c, n, rep=1):
+def tops(n):
+    q = n // 4
+    return [[low + z * q for z in range(4)] for low in range(q)]
+
+
+def gather_far(s, n):
+    return [s] + [xor_pp(s, e, n) for e in range(1, n // 4)]
+
+
+def settle(pieces, order, c, n, tall=None):
     q = n // 4
     rows = pieces[0].shape[1]
     if rows % 16 == 0 and q == 4:
         return pieces
-    order = f ^ jnp.arange(n)
+    height = n * rows // 16
     halves = []
     for side in (pieces[:q], pieces[q:]):
         rel = jnp.stack(side, axis=1).reshape((n,) + side[0].shape[1:])
@@ -88,51 +96,64 @@
     right = jnp.where(c == 0, halves[1], halves[0])
     out = []
     for side in (left, right):
-        four = side.reshape(4, 4, n * rows // 16, side.shape[-1])
+        cut = side.shape[-1] if tall is None else tall
+        flat = side[..., :cut].reshape(16, height, cut)
+        if tall is not None:
+            w = (side.shape[-1] - cut) // 4
+            low = side[..., cut:].reshape(n, rows, 4, w).transpose(0, 2, 1, 3)
+            low = low.reshape(16, 4, height, w).transpose(0, 2, 1, 3).reshape(16, height, 4 * w)
+            flat = jnp.concatenate([flat, low], axis=2)
+        four = flat.reshape(4, 4, height, side.shape[-1])
         out += [four[:, e] for e in range(4)]
     return out
 
 
-def load_pieces(idx_ref, pieces, dst, sem, width):
+def piece(pieces, side, e, d):
+    return pieces[side].at[e, d] if len(pieces) == 2 else pieces[4 * side + e].at[d]
+
+
+def load_pieces(idx_ref, pieces, plan, sem, relative=False):
     f = idx_ref[0]
     c = idx_ref[1]
-    rows = pieces[0].shape[1]
+    rows = pieces[0].shape[-2]
     started = []
-    for e in range(4):
-        for d in range(4):
-            s = lax.bitwise_xor(f, jnp.int32(d * 4 + e))
-            at = pl.ds(pl.multiple_of(s * rows, 16), rows)
-            for h, src in ((c, pieces[e]), (1 - c, pieces[4 + e])):
-                cols = pl.ds(pl.multiple_of(h * width, 128), width)
-                cp = pltpu.make_async_copy(src.at[d, :, pl.ds(0, width)], dst.at[at, cols], sem)
-                cp.start()
-                started.append(cp)
+    for start, width, dst, height, first, two in plan:
+        for e in range(4):
+            for d in range(4):
+                s = lax.bitwise_xor(f if relative else f % 4 + d * 4, jnp.int32(d * 4 + e if relative else e))
+                at = pl.ds(pl.multiple_of(s * height + first, 16), rows)
+                src = pl.ds(start, width)
+                if two:
+                    for side, h in ((0, c), (1, 1 - c)):
+                        cols = pl.ds(pl.multiple_of(h * width, 128), width)
+                        block = piece(pieces, side, e, d)
+                        started.append(pltpu.make_async_copy(block.at[:, src], dst.at[at, cols], sem))
+                else:
+                    block = piece(pieces, 0, e, d)
+                    started.append(pltpu.make_async_copy(block.at[:, src], dst.at[at, :], sem))
+    for cp in started:
+        cp.start()
     return started
 
 
-def load_vecs(idx_ref, pieces, dst, sem, width):
-    f = idx_ref[0]
-    rows = pieces[0].shape[1]
-    started = []
-    for e in range(4):
-        for d in range(4):
-            s = lax.bitwise_xor(f, jnp.int32(d * 4 + e))
-            at = pl.ds(pl.multiple_of(s * rows, 16), rows)
-            cp = pltpu.make_async_copy(pieces[e].at[d, :, pl.ds(width, 128)], dst.at[at, :], sem)
-            cp.start()
-            started.append(cp)
-    return started
+def plan_mlp(rows, w1_ref, w2_ref):
+    half = w1_ref.shape[1] // 2
+    w = w2_ref.shape[1] // 2
+    return [(0, half, w1_ref, rows, 0, True)], [
+        (half + j * w, w, w2_ref, 4 * rows, j * rows, True) for j in range(4)
+    ]
 
 
 def qkv_kernel(idx_ref, x_ref, *refs):
-    pieces = refs[:8]
-    q_ref, k_ref, v_ref, vt_ref, w_ref, vec_ref, sem = refs[8:]
+    pieces = refs[:2]
+    q_ref, k_ref, v_ref, h_ref, vt_ref, w_ref, vec_ref, sem = refs[2:]
     d = x_ref.shape[1]
 
     @pl.when(pl.program_id(0) == 0)
     def _():
-        going = load_pieces(idx_ref, pieces, w_ref, sem.at[0], 3 * d // 2)
-        vecs = load_vecs(idx_ref, pieces, vec_ref, sem.at[1], 3 * d // 2)
+        rows = pieces[0].shape[-2]
+        vecs = load_pieces(idx_ref, pieces, [(3 * d // 2, 128, vec_ref, rows, 0, False)], sem.at[1], True)
+        going = load_pieces(idx_ref, pieces, [(0, 3 * d // 2, w_ref, rows, 0, True)], sem.at[0], True)
         for cp in vecs:
             cp.wait()
         vt_ref[...] = vec_ref[...].astype(F32).T[:VECS]
@@ -141,6 +162,7 @@
 
     c, r = norm_stats(x_ref[...].astype(F32))
     h = (c * r * vt_ref[0:1, :] + vt_ref[1:2, :]).astype(BF)
+    h_ref[...] = h
     q = dg(h, w_ref[:, :d], NN)
     q_ref[...] = ((q + vt_ref[2:3, :]) * (0.125 * LOG2E)).astype(BF)
     k_ref[...] = dg(h, w_ref[:, d : 2 * d], NN).astype(BF)
@@ -154,15 +176,15 @@
         grid_spec=pltpu.PrefetchScalarGridSpec(
             num_scalar_prefetch=1,
             grid=(t // tb,),
-            in_specs=[rows_of(tb, d)] + [ANY] * 8,
-            out_specs=[rows_of(tb, d)] * 3 + [fixed((VECS, d))],
+            in_specs=[rows_of(tb, d)] + [ANY] * 2,
+            out_specs=[rows_of(tb, d)] * 4 + [fixed((VECS, d))],
             scratch_shapes=[
                 pltpu.VMEM((d, 3 * d), BF),
                 pltpu.VMEM((d, 128), BF),
                 pltpu.SemaphoreType.DMA((2,)),
             ],
         ),
-        out_shape=[SDS((t, d), BF)] * 3 + [SDS((VECS, d), F32)],
+        out_shape=[SDS((t, d), BF)] * 4 + [SDS((VECS, d), F32)],
         compiler_params=params(),
         cost_estimate=cost(6 * t * d * d, t * d * 8 + d * d * 6),
         name="qkv",
@@ -240,16 +262,16 @@
 
 
 def mlp_kernel(idx_ref, x_ref, o_ref, vt_ref, bu_ref, *refs, fc):
-    p1 = refs[:8]
-    p2 = refs[8:16]
-    x2_ref, gl_ref, gp_ref, y_ref, w1_ref, w2_ref, sem = refs[16:]
+    pieces = refs[:8]
+    x2_ref, gl_ref, gp_ref, y_ref, w1_ref, w2_ref, sem = refs[8:]
     d = x_ref.shape[1]
     ff = w2_ref.shape[0]
 
     @pl.when(pl.program_id(0) == 0)
     def _():
-        going = load_pieces(idx_ref, p1, w1_ref, sem.at[0], w1_ref.shape[1] // 2)
-        going += load_pieces(idx_ref, p2, w2_ref, sem.at[1], d // 2)
+        first, second = plan_mlp(pieces[0].shape[1], w1_ref, w2_ref)
+        going = load_pieces(idx_ref, pieces, first, sem.at[0])
+        going += load_pieces(idx_ref, pieces, second, sem.at[1])
         for cp in going:
             cp.wait()
 
@@ -268,7 +290,7 @@
     y_ref[...] = y.astype(BF)
 
 
-def mlp(idx, x, o, vt, bu, p1, p2, tb=256, fc=768):
+def mlp(idx, x, o, vt, bu, pieces, tb=256, fc=768):
     t, d = x.shape
     ff = bu.shape[1]
     return pl.pallas_call(
@@ -276,7 +298,7 @@
         grid_spec=pltpu.PrefetchScalarGridSpec(
             num_scalar_prefetch=1,
             grid=(t // tb,),
-            in_specs=[rows_of(tb, d)] * 2 + [whole(vt.shape), whole(bu.shape)] + [ANY] * 16,
+            in_specs=[rows_of(tb, d)] * 2 + [whole(vt.shape), whole(bu.shape)] + [ANY] * 8,
             out_specs=[rows_of(tb, d), rows_of(tb, ff), rows_of(tb, ff), rows_of(tb, d)],
             scratch_shapes=[
                 pltpu.VMEM((d, d + ff), BF),
@@ -288,7 +310,7 @@
         compiler_params=params(),
         cost_estimate=cost(4 * t * d * (d + 2 * ff), t * (10 * d + 4 * ff) + 4 * d * ff, 2 * t * ff),
         name="mlp",
-    )(idx, x, o, vt, bu, *p1, *p2)
+    )(idx, x, o, vt, bu, *pieces)
 
 
 def permute_kernel(ord_ref, y_ref, o_ref):
@@ -313,17 +335,17 @@
 
 
 def mlp_back_kernel(idx_ref, ord_ref, ret_ref, gp_ref, x2_ref, vt_ref, *refs, fc):
-    p1 = refs[:8]
-    p2 = refs[8:16]
-    (dm_ref, du_ref, dx2_ref, da_ref, do_ref, h2_ref, sums_ref, gbu_ref, w1_ref, w2_ref, sem) = refs[16:]
+    pieces = refs[:8]
+    (dm_ref, du_ref, dx2_ref, da_ref, do_ref, h2_ref, sums_ref, gbu_ref, w1_ref, w2_ref, sem) = refs[8:]
     i = pl.program_id(0)
     tb, ff = gp_ref.shape
     t, d = ret_ref.shape
 
     @pl.when(i == 0)
     def _():
-        going = load_pieces(idx_ref, p1, w1_ref, sem.at[0], w1_ref.shape[1] // 2)
-        going += load_pieces(idx_ref, p2, w2_ref, sem.at[1], d // 2)
+        first, second = plan_mlp(pieces[0].shape[1], w1_ref, w2_ref)
+        going = load_pieces(idx_ref, pieces, first, sem.at[0])
+        going += load_pieces(idx_ref, pieces, second, sem.at[1])
         sums_ref[...] = jnp.zeros_like(sums_ref)
         gbu_ref[...] = jnp.zeros_like(gbu_ref)
         for cp in going:
@@ -358,7 +380,7 @@
     do_ref[...] = dg(da, w1_ref[:, :d], NT).astype(BF)
 
 
-def mlp_back(idx, order_row, ret, gp, x2, vt, p1, p2, tb=256, fc=768):
+def mlp_back(idx, order_row, ret, gp, x2, vt, pieces, tb=256, fc=768):
     t, d = x2.shape
     ff = gp.shape[1]
     return pl.pallas_call(
@@ -367,7 +389,7 @@
             num_scalar_prefetch=1,
             grid=(t // tb,),
             in_specs=[whole((1, t)), whole((t, d)), rows_of(tb, ff), rows_of(tb, d), whole(vt.shape)]
-            + [ANY] * 16,
+            + [ANY] * 8,
             out_specs=[
                 rows_of(tb, d),
                 rows_of(tb, ff),
@@ -397,7 +419,7 @@
         compiler_params=params(),
         cost_estimate=cost(2 * t * d * (d + 2 * ff + t) * 1.5, t * (20 * d + 4 * ff)),
         name="mlp_back",
-    )(idx, order_row, ret, gp, x2, vt, *p1, *p2)
+    )(idx, order_row, ret, gp, x2, vt, *pieces)
 
 
 def split_halves(c, r, mine_ref, theirs_ref):
@@ -521,20 +543,21 @@
         run(c, c, [(ks, [ks]) for ks in range(0, length, c)])
 
 
-def attend_back(tag, q, k, v, do, o, lse, kb=512, qb=512):
-    t, d = q.shape
+def attend_back(tag, q, k, v, do, o, lse, first, pairs, kb=512, qb=512):
+    t = q.shape[0]
+    d = pairs * 128
     rows = tag.shape[0]
     length = t // rows
-    pairs = d // 128
-    blk = pl.BlockSpec((length, 128), lambda r, p, _: (r, p))
-    lse_spec = pl.BlockSpec((1, 1, 2, length), lambda r, p, _: (r, p, 0, 0))
+    blk = pl.BlockSpec((length, 128), lambda r, p, _: (r, p + first))
+    out = pl.BlockSpec((length, 128), lambda r, p, _: (r, p))
+    lse_spec = pl.BlockSpec((1, 1, 2, length), lambda r, p, _: (r, p + first, 0, 0))
     return pl.pallas_call(
         functools.partial(attend_back_kernel, kb=kb, qb=qb),
         grid_spec=pltpu.PrefetchScalarGridSpec(
             num_scalar_prefetch=1,
             grid=(rows, pairs),
             in_specs=[blk] * 5 + [lse_spec],
-            out_specs=[blk] * 3,
+            out_specs=[out] * 3,
             scratch_shapes=[pltpu.VMEM((2, length), F32), pltpu.VMEM((128, length), F32)],
         ),
         out_shape=[SDS((t, d), BF)] * 3,
@@ -544,51 +567,40 @@
     )(tag, q, k, v, do, o, lse)
 
 
-def grad_qkv_kernel(idx_ref, x_ref, vt_ref, dq_ref, dk_ref, dv_ref, mine_ref, theirs_ref, s_ref, h_ref):
-    i = pl.program_id(0)
-
-    @pl.when(i == 0)
-    def _():
-        c, r = norm_stats(x_ref[...].astype(F32))
-        h_ref[...] = (c * r * vt_ref[0:1, :] + vt_ref[1:2, :]).astype(BF)
-        s_ref[...] = jnp.zeros_like(s_ref)
-
+def grad_qkv_kernel(idx_ref, h_ref, dq_ref, dk_ref, dv_ref, o_ref):
+    w = dq_ref.shape[1]
     for m, ref in enumerate((dq_ref, dk_ref, dv_ref)):
-
-        @pl.when(i == m)
-        def _(m=m, ref=ref):
-            dj = ref[...]
-            split_halves(idx_ref[1], dg(h_ref[...], dj, TN).astype(BF), mine_ref, theirs_ref)
-            if m != 1:
-                s_ref[m // 2 : m // 2 + 1, :] = jnp.sum(dj.astype(F32), axis=0, keepdims=True)
-
-
-def grad_qkv(idx, x, vt, dq, dk, dv):
-    t, d = x.shape
+        o_ref[:, m * w : (m + 1) * w] = dg(h_ref[...], ref[...], TN).astype(BF)
+
+
+def grad_qkv(idx, h1, dq, dk, dv, other):
+    t, d = h1.shape
+    w = d // 2
+    half = pl.BlockSpec((t, w), lambda i, ix: (0, lax.bitwise_xor(ix[1], jnp.int32(other))))
     return pl.pallas_call(
         grad_qkv_kernel,
         grid_spec=pltpu.PrefetchScalarGridSpec(
             num_scalar_prefetch=1,
-            grid=(3,),
-            in_specs=[whole((t, d)), whole(vt.shape)] + [whole((t, d))] * 3,
-            out_specs=[pl.BlockSpec((d, d // 2), lambda i, _: (0, i))] * 2 + [fixed((8, d))],
-            scratch_shapes=[pltpu.VMEM((t, d), BF)],
-        ),
-        out_shape=[SDS((d, 3 * d // 2), BF)] * 2 + [SDS((8, d), F32)],
-        compiler_params=params(),
-        cost_estimate=cost(9 * t * d * d, t * d * 10),
-        name="grad_qkv",
-    )(idx, x, vt, dq, dk, dv)
-
-
-def tokens_back_kernel(idx_ref, dq_ref, dk_ref, dv_ref, x_ref, vt_ref, dx2_ref, *refs):
-    pieces = refs[:8]
-    tg_ref, s_ref, w_ref, sem = refs[8:]
+            grid=(1,),
+            in_specs=[whole((t, d)), half, half, half],
+            out_specs=fixed((d, 3 * w)),
+        ),
+        out_shape=SDS((d, 3 * w), BF),
+        compiler_params=params(),
+        cost_estimate=cost(6 * t * d * w, t * d * 6),
+        name="grad_qkv_other" if other else "grad_qkv_own",
+    )(idx, h1, dq, dk, dv)
+
+
+def tokens_back_kernel(idx_ref, x_ref, vt_ref, dx2_ref, dq_ref, dk_ref, dv_ref, *refs):
+    pieces = refs[:2]
+    tg_ref, s_ref, w_ref, sem = refs[2:]
     d = x_ref.shape[1]
 
     @pl.when(pl.program_id(0) == 0)
     def _():
-        going = load_pieces(idx_ref, pieces, w_ref, sem, 3 * d // 2)
+        plan = [(0, 3 * d // 2, w_ref, pieces[0].shape[-2], 0, True)]
+        going = load_pieces(idx_ref, pieces, plan, sem, True)
         s_ref[...] = jnp.zeros_like(s_ref)
         for cp in going:
             cp.wait()
@@ -596,6 +608,8 @@
     dh = dg(dq_ref[...], w_ref[:, :d], NT)
     dh = dh + dg(dk_ref[...], w_ref[:, d : 2 * d], NT)
     dh = dh + dg(dv_ref[...], w_ref[:, 2 * d :], NT)
+    s_ref[2:3, :] += jnp.sum(dq_ref[...].astype(F32), axis=0, keepdims=True)
+    s_ref[3:4, :] += jnp.sum(dv_ref[...].astype(F32), axis=0, keepdims=True)
     c, r = norm_stats(x_ref[...].astype(F32))
     xh = c * r
     s_ref[0:1, :] += jnp.sum(dh * xh, axis=0, keepdims=True)
@@ -613,7 +627,7 @@
         grid_spec=pltpu.PrefetchScalarGridSpec(
             num_scalar_prefetch=1,
             grid=(t // tb,),
-            in_specs=[rows_of(tb, d)] * 4 + [whole(vt.shape), rows_of(tb, d)] + [ANY] * 8,
+            in_specs=[rows_of(tb, d), whole(vt.shape)] + [rows_of(tb, d)] * 4 + [ANY] * 2,
             out_specs=[rows_of(tb, d), fixed((8, d))],
             scratch_shapes=[pltpu.VMEM((d, 3 * d), BF), pltpu.SemaphoreType.DMA],
         ),
@@ -621,76 +635,127 @@
         compiler_params=params(),
         cost_estimate=cost(9 * t * d * d, t * d * 16 + d * d * 6),
         name="tokens_back",
-    )(idx, dq, dk, dv, x, vt, dx2, *pieces)
-
-
-def sum_far_kernel(idx_ref, *refs, q):
+    )(idx, x, vt, dx2, dq, dk, dv, *pieces)
+
+
+def sum_far_kernel(idx_ref, *refs, q, groups):
+    outs = refs[2 * groups * q :]
     for e in range(q):
-        a, b, o = refs[e], refs[q + e], refs[2 * q + e]
-        o[...] = (a[...].astype(F32) + b[...].astype(F32)).astype(BF)
-
-
-def sum_far(idx, mine, recv, n):
+        start = 0
+        for g in range(groups):
+            a, b = refs[2 * g * q + e], refs[(2 * g + 1) * q + e]
+            total = (a[0].astype(F32) + b[0].astype(F32)).astype(BF)
+            rows = outs[e].shape[1]
+            w = total.shape[1]
+            for j in range(total.shape[0] // rows):
+                outs[e][0, :, start : start + w] = total[j * rows : (j + 1) * rows]
+                start += w
+
+
+def reduce_far(idx, pairs, rows, n):
     q = n // 4
-    _, rows, ch = mine.shape
-
-    def spec(e):
-        return pl.BlockSpec((1, rows, ch), lambda z, ix: (z * q + lax.bitwise_xor(ix[0] % q, jnp.int32(e)), 0, 0))
-
-    specs = [spec(e) for e in range(q)]
-    return pl.pallas_call(
-        functools.partial(sum_far_kernel, q=q),
+    ops, specs, width = [], [], 0
+
+    def spec(e, shape):
+        return pl.BlockSpec(
+            (1,) + shape, lambda z, ix: (z * q + lax.bitwise_xor(ix[0] % q, jnp.int32(e)), 0, 0)
+        )
+
+    for pair in pairs:
+        shape = (pair[0].shape[0] // n, pair[0].shape[1])
+        width += shape[0] // rows * shape[1]
+        for x in pair:
+            ops += [x.reshape((n,) + shape)] * q
+            specs += [spec(e, shape) for e in range(q)]
+    outs = pl.pallas_call(
+        functools.partial(sum_far_kernel, q=q, groups=len(pairs)),
         grid_spec=pltpu.PrefetchScalarGridSpec(
             num_scalar_prefetch=1,
             grid=(4,),
-            in_specs=specs * 2,
-            out_specs=[pl.BlockSpec((1, rows, ch), lambda z, ix: (z, 0, 0))] * q,
-        ),
-        out_shape=[SDS((4, rows, ch), BF)] * q,
-        compiler_params=params(),
-        cost_estimate=cost(n * rows * ch, n * rows * ch * 6),
+            in_specs=specs,
+            out_specs=[pl.BlockSpec((1, rows, width), lambda z, ix: (z, 0, 0))] * q,
+        ),
+        out_shape=[SDS((4, rows, width), BF)] * q,
+        compiler_params=params(),
+        cost_estimate=cost(n * rows * width, n * rows * width * 6),
         name="sum_far",
-    )(idx, *([mine] * q), *([recv] * q))
-
-
-def sum_near_kernel(idx_ref, *refs, q):
+    )(idx, *ops)
+    return [outs[0]] + [xor_pp(outs[e], e, n) for e in range(1, q)]
+
+
+def sum_parts_kernel(*refs):
+    total = refs[0][...].astype(F32)
+    for x in refs[1:-1]:
+        total = total + x[...].astype(F32)
+    refs[-1][...] = total.astype(BF)
+
+
+def sum_parts(parts):
+    shape = (1,) + parts[0].shape[1:]
+    spec = pl.BlockSpec(shape, lambda i: (i, 0, 0))
+    return pl.pallas_call(
+        sum_parts_kernel,
+        grid=(4,),
+        in_specs=[spec] * len(parts),
+        out_specs=spec,
+        out_shape=SDS(parts[0].shape, BF),
+        compiler_params=params(),
+        cost_estimate=cost(4 * len(parts) * math.prod(shape), 8 * len(parts) * math.prod(shape)),
+        name="sum_parts",
+    )(*parts)
+
+
+def sum_near_kernel(idx_ref, *refs, q, groups):
+    outs = refs[4 * q * groups :]
     for d in range(4):
-        total = refs[d * q][...].astype(F32)
-        for e in range(1, q):
-            total = total + refs[d * q + e][...].astype(F32)
-        refs[4 * q + d][...] = total[0].astype(BF)
-
-
-def sum_near(idx, parts, n):
+        start = 0
+        for g in range(groups):
+            at = (g * 4 + d) * q
+            total = refs[at][0].astype(F32)
+            for e in range(1, q):
+                total = total + refs[at + e][0].astype(F32)
+            w = total.shape[1]
+            outs[d][:, start : start + w] = total.astype(BF)
+            start += w
+
+
+def reduce_near(idx, groups, n):
     q = n // 4
-    _, rows, ch = parts[0].shape
-
-    def spec(d):
-        return pl.BlockSpec((1, rows, ch), lambda i, ix: (lax.bitwise_xor(ix[0] // q, jnp.int32(d)), 0, 0))
-
-    return pl.pallas_call(
-        functools.partial(sum_near_kernel, q=q),
+    ops, specs, width = [], [], 0
+
+    def spec(d, shape):
+        return pl.BlockSpec((1,) + shape, lambda i, ix: (lax.bitwise_xor(ix[0] // q, jnp.int32(d)), 0, 0))
+
+    for parts in groups:
+        shape = parts[0].shape[1:]
+        rows = shape[0]
+        width += shape[1]
+        ops += list(parts) * 4
+        specs += [spec(d, shape) for d in range(4) for _ in range(q)]
+    near = pl.pallas_call(
+        functools.partial(sum_near_kernel, q=q, groups=len(groups)),
         grid_spec=pltpu.PrefetchScalarGridSpec(
             num_scalar_prefetch=1,
             grid=(1,),
-            in_specs=[spec(d) for d in range(4) for _ in range(q)],
-            out_specs=[fixed((rows, ch))] * 4,
-        ),
-        out_shape=[SDS((rows, ch), BF)] * 4,
-        compiler_params=params(),
-        cost_estimate=cost(n * rows * ch, n * rows * ch * 3),
+            in_specs=specs,
+            out_specs=[fixed((rows, width))] * 4,
+        ),
+        out_shape=[SDS((rows, width), BF)] * 4,
+        compiler_params=params(),
+        cost_estimate=cost(n * rows * width, n * rows * width * 3),
         name="sum_near",
-    )(idx, *(list(parts) * 4))
-
-
-def reduce_steps(idx, mine, recv, n, m):
-    q = n // 4
-    outs = sum_far(idx, mine, recv, n)
-    parts = [outs[0]] + [xor_pp(outs[e], e, n) for e in range(1, q)]
-    near = sum_near(idx, parts, n)
+    )(idx, *ops)
+    return [near[0]] + [xor_pp(near[d], d * q, n) for d in range(1, 4)]
+
+
+def reduce_last(near, n, m):
     total = near[0].astype(F32)
-    for d in range(1, 4):
-        total = total + xor_pp(near[d], d * q, n).astype(F32)
+    for x in near[1:]:
+        total = total + x.astype(F32)
+    return over_pairs(total, m)
+
+
+def over_pairs(total, m):
     b = 2
     while b < m:
         total = total + lax.ppermute(total.astype(BF), "dp", [(i, i ^ b) for i in range(m)]).astype(F32)
@@ -698,32 +763,20 @@
     return total
 
 
-def reduce_grad(idx, mine, theirs, n, m):
-    rows, ch = mine.shape[0] // n, mine.shape[1]
-    recv = core_swap(theirs, m)
-    low = reduce_steps(idx, mine.reshape(n, rows, ch), recv.reshape(n, rows, ch), n, m).astype(BF)
-    other = core_swap(low, m)
-    first = idx[1] == 0
-    return (
-        jnp.where(first, low, other).astype(F32),
-        jnp.where(first, other, low).astype(F32),
-    )
-
-
 def vec_table_kernel(*refs):
-    a, b, c, u, o = refs
+    a, c, u, o = refs
     d = a.shape[1]
     rows = jnp.concatenate(
-        [c[0:2, :], b[0:2, :], a[3:4, :], a[1:3, :], a[0:1, :], u[...], jnp.zeros((116, d), F32)], axis=0
+        [c[0:4, :], a[3:4, :], a[1:3, :], a[0:1, :], u[...], jnp.zeros((116, d), F32)], axis=0
     )
     o[...] = rows.T.astype(BF)
 
 
-def vec_table(s_mlp, s_qkv, s_tok, gbu):
+def vec_table(s_mlp, s_tok, gbu):
     d = s_mlp.shape[1]
     return pl.pallas_call(
         vec_table_kernel, out_shape=SDS((d, 128), BF), compiler_params=params(0), name="vec_table"
-    )(s_mlp, s_qkv, s_tok, gbu)
+    )(s_mlp, s_tok, gbu)
 
 
 def local(
@@ -765,53 +818,96 @@
     vec = jnp.concatenate([vec, b_up.reshape(wide, rows).T], axis=1)
     vec = jnp.pad(vec, ((0, 0), (0, 128 - vec.shape[1])))
     shard_a = jnp.concatenate([core_half(w_qkv), vec], axis=1)
-    shard_b = core_half(jnp.concatenate([w_out, w_up], axis=1))
-    shard_c = core_half(w_down)
+    shard_b = jnp.concatenate(
+        [core_half(jnp.concatenate([w_out, w_up], axis=1))]
+        + [core_half(w_down[j * rows : (j + 1) * rows]) for j in range(wide)],
+        axis=1,
+    )
+    q = n // 4
     near_a = gather_near(shard_a, n)
-    pieces_a = settle(gather_far(near_a, n, m), f, c, n)
-    near_b = gather_near(shard_b, n)
-    near_c = gather_near(shard_c, n)
-    pieces_b = settle(gather_far(near_b, n, m), f, c, n)
-    pieces_c = settle(gather_far(near_c, n, m), f, c, n)
-
-    returned = lax.all_to_all(out_grad.astype(BF), "fsdp", split_axis=0, concat_axis=0, tiled=True)
-
-    q, k, v, vt = qkv(use, tokens, pieces_a)
-    mixed, lse = attend(sensor_tag, q, k, v)
+    near_b = lax.all_to_all(
+        jnp.broadcast_to(after(shard_b, near_a)[None], (4,) + shard_b.shape),
+        "fsdp",
+        split_axis=0,
+        concat_axis=0,
+        tiled=True,
+        axis_index_groups=tops(n),
+    )
+    own_a = gather_far(near_a, n)
+    everyone = jnp.arange(n)
+    own_a = jnp.stack(own_a)
+    pieces_a = [own_a, core_swap(own_a, m)]
+    if use is not idx:
+        pieces_a = settle([x[e] for x in pieces_a for e in range(q)], f ^ everyone, c, n)
+        pieces_a = [jnp.stack(pieces_a[:4]), jnp.stack(pieces_a[4:])]
+    own_b = gather_far(near_b, n)
+    swap_b = [core_swap(near_b, m)]
+
+    qh, kh, vh, h1, vt = qkv(use, after(tokens, near_b), pieces_a)
+    mixed, lse = attend(sensor_tag, qh, kh, vh)
     bu = vt[8 : 8 + wide].reshape(wide, n, rows).transpose(1, 0, 2).reshape(1, ff)
-    x2, active, slope, y = mlp(use, tokens, mixed, vt, bu, pieces_b, pieces_c)
+    own_b = [after(x, mixed) for x in own_b]
+    cast = after(out_grad.astype(BF), own_b)
+    returned = lax.all_to_all(cast, "fsdp", split_axis=0, concat_axis=0, tiled=True)
+    swap_b += [core_swap(x, m) for x in own_b[1:]]
+    pieces_b = settle(own_b + swap_b, everyone // q * q + (everyone ^ f) % q, c, n, (d + ff) // 2)
+
+    x2, active, slope, y = mlp(use, tokens, mixed, vt, bu, pieces_b)
     sent = permute(owner_order.reshape(t, 1), y)
-    encoded = lax.all_to_all(sent, "fsdp", split_axis=0, concat_axis=0, tiled=True).astype(F32)
-
-    dm, du, dx2, da, do, h2, s_mlp, gbu = mlp_back(
-        use, owner_order, returned, slope, x2, vt, pieces_b, pieces_c
+    encoded = lax.all_to_all(sent, "fsdp", split_axis=0, concat_axis=0, tiled=True)
+
+    returned = after(returned, sent)
+    dm, du, dx2, da, do, h2, s_mlp, gbu = mlp_back(use, owner_order, returned, slope, x2, vt, pieces_b)
+    gbu = gbu.reshape(n, wide, rows).transpose(1, 0, 2).reshape(wide, d)
+    up_own, up_other = grad_up(idx, h2, mixed, du, da)
+    up_recv = core_swap(up_other, m)
+    down_own, down_other = grad_down(idx, *after((active, dm), up_own))
+    down_recv = core_swap(down_other, m)
+    encoded = after(encoded, down_own).astype(F32)
+    up_recv, down_recv = after((up_recv, down_recv), encoded)
+    far_b = reduce_far(idx, [(up_own, up_recv), (down_own, down_recv)], rows, n)
+    do, gbu = after((do, gbu), far_b[0])
+    dj = attend_back(sensor_tag, qh, kh, vh, do, mixed, lse, 0, d // 128)
+    far_b = sum_parts(after(far_b, dj))
+    total_b = lax.all_to_all(
+        far_b, "fsdp", split_axis=0, concat_axis=0, tiled=True, axis_index_groups=tops(n)
     )
-    down_mine, down_theirs = grad_down(idx, active, dm)
-    g_down = reduce_grad(idx, down_mine, down_theirs, n, m)
-    up_mine, up_theirs = grad_up(idx, h2, mixed, du, da)
-    g_up = reduce_grad(idx, up_mine, up_theirs, n, m)
-    dq, dk, dv = attend_back(sensor_tag, q, k, v, do, mixed, lse)
-    qkv_mine, qkv_theirs, s_qkv = grad_qkv(idx, tokens, vt, dq, dk, dv)
-    g_qkv = reduce_grad(idx, qkv_mine, qkv_theirs, n, m)
-    tokens_grad, s_tok = tokens_back(use, dq, dk, dv, tokens, vt, dx2, pieces_a)
-
-    gbu = gbu.reshape(n, wide, rows).transpose(1, 0, 2).reshape(wide, d)
-    table = vec_table(s_mlp, s_qkv, s_tok, gbu)
-    table_swap = core_swap(table, m)
-    vecs = reduce_steps(idx, table.reshape(n, rows, 128), table_swap.reshape(n, rows, 128), n, m)
-    vecs = vecs.T
-
-    def join(pair, parts, width):
+    dj = after(dj, far_b)
+    qkv_other = grad_qkv(idx, h1, *dj, 1)
+    qkv_recv = core_swap(qkv_other, m)
+    qkv_own = grad_qkv(idx, after(h1, qkv_other), *dj, 0)
+    far_a = reduce_far(idx, [(qkv_own, after(qkv_recv, qkv_own))], rows, n)
+    tokens_grad, s_tok = tokens_back(use, *after(dj, far_a[0]), tokens, vt, dx2, pieces_a)
+    table = vec_table(s_mlp, s_tok, gbu).reshape(4, q, rows, 128)
+    far_v = [lax.dynamic_index_in_dim(table, (f % q) ^ e, 1, keepdims=False) for e in range(q)]
+    far_v = [far_v[0]] + [xor_pp(far_v[e], e, n) for e in range(1, q)]
+    total_b = over_pairs(jnp.sum(after(total_b, tokens_grad).astype(F32), axis=0), m).astype(BF)
+    other_b = core_swap(total_b, m)
+
+    near_a = reduce_near(idx, [far_a, far_v], n)
+    total_a = reduce_last(near_a, n, m)
+    other_a = core_swap(total_a.astype(BF), m)
+    cut = 3 * d // 2
+    vecs = (total_a[:, cut:] + other_a[:, cut:].astype(F32)).T
+    total_a, other_a = total_a[:, :cut].astype(BF), other_a[:, :cut]
+
+    def both(mine, other):
+        first = c == 0
+        return jnp.where(first, mine, other).astype(F32), jnp.where(first, other, mine).astype(F32)
+
+    def join(pair, start, width, parts, axis=1):
         out = []
         for p in range(parts):
-            out += [pair[0][:, p * width : (p + 1) * width], pair[1][:, p * width : (p + 1) * width]]
-        return jnp.concatenate(out, axis=1)
+            at = slice(start + p * width, start + (p + 1) * width)
+            out.append(jnp.concatenate([pair[0][:, at], pair[1][:, at]], axis=1))
+        return jnp.concatenate(out, axis=axis)
 
     h = d // 2
-    grad_qkv_out = join(g_qkv, 3, h)
-    grad_up_out = join((g_up[0][:, : ff // 2], g_up[1][:, : ff // 2]), wide, h)
-    grad_out_out = join((g_up[0][:, ff // 2 :], g_up[1][:, ff // 2 :]), 1, h)
-    grad_down_out = join(g_down, 1, h)
+    g_mlp = both(total_b, other_b)
+    grad_qkv_out = join(both(total_a, other_a), 0, h, 3)
+    grad_up_out = join(g_mlp, 0, h, wide)
+    grad_out_out = join(g_mlp, ff // 2, h, 1)
+    grad_down_out = join(g_mlp, (d + ff) // 2, h, wide, 0)
     return (
         encoded,
         tokens_grad,

time: 649 us -> 479 us (0.74)
  waiting for transfers between devices: 196 us -> 61.6 us
  starting transfers between devices: 94.9 us -> 69 us
  Pallas kernels: 311 us -> 302 us
    ppermute x42 -> x21, waiting for transfers between devices: 194 us -> 49.9 us  [xor_pp(): return lax.ppermute(x, 'fsdp', [(i, i ^ b) for i in range(n)])]
    ppermute x42 -> x21, starting transfers between devices: 56.1 us -> 30.3 us  [xor_pp(): return lax.ppermute(x, 'fsdp', [(i, i ^ b) for i in range(n)])]
    all_to_all x1 -> x3, starting transfers between devices: 4.89 us -> 18.1 us  [the longest x1 9.53 us: local(): lax.all_to_all(cast, 'fsdp', split_axis=0, concat_axis=0, tiled=True)]
    pallas_call x8 -> x4, Pallas kernels: 31.5 us -> 20.3 us  [the longest x2 12.7 us: reduce_far(): pl.pallas_call(functools.partial(sum_far_kernel, q=q, groups=len(pairs)),...]
    ppermute x19 -> x10, starting transfers between devices: 23.8 us -> 13.4 us  [core_swap(): return lax.ppermute(x, 'dp', [(i, i ^ 1) for i in range(m)])]
    pallas_call x1 -> x2, Pallas kernels: 16.7 us -> 20.4 us  [grad_qkv(): pl.pallas_call(grad_qkv_kernel, grid_spec=pltpu.PrefetchScalarGridSpec(nu...]
  transfers between devices with their start and end apart: 63 -> 35, of which waited for: 26 -> 16; matrix products, arithmetic and copies ran while one was open for 4% -> 5% of each run, Pallas kernels for 49% -> 61%
where the time goes in v2:
time: 479 us; the launch traced here: 472 us
  Pallas kernels  302 us (63%)
  starting transfers between devices  69 us (14%)
  waiting for transfers between devices  61.6 us (13%)
  other arithmetic  20.6 us (4%)
  local copies, waits for them, and re-layouts  16.8 us (4%)
    pallas_call x1, Pallas kernels, mlp(): pl.pallas_call(functools.partial(mlp_kernel, fc=fc), grid_spec=pltpu.Pref...  50.3 us
    ppermute x21, waiting for transfers between devices, xor_pp(): return lax.ppermute(x, 'fsdp', [(i, i ^ b) for i in range(n)])  49.9 us
    pallas_call x1, Pallas kernels, attend_back(): pl.pallas_call(functools.partial(attend_back_kernel, kb=kb, qb=qb), grid_...  49.8 us
    pallas_call x1, Pallas kernels, mlp_back(): pl.pallas_call(functools.partial(mlp_back_kernel, fc=fc), grid_spec=pltpu...  47.6 us
    pallas_call x1, Pallas kernels, attend(): pl.pallas_call(functools.partial(attend_kernel, qb=qb), grid_spec=pltpu.P...  34 us
    ppermute x21, starting transfers between devices, xor_pp(): return lax.ppermute(x, 'fsdp', [(i, i ^ b) for i in range(n)])  30.3 us
    pallas_call x2, Pallas kernels, grad_qkv(): pl.pallas_call(grad_qkv_kernel, grid_spec=pltpu.PrefetchScalarGridSpec(nu...  20.4 us
    pallas_call x1, Pallas kernels, grad_up(): pl.pallas_call(functools.partial(grad_up_kernel, steps=steps), grid_spec=...  19.9 us
  transfers between devices with their start and end apart: 35, of which 16 were waited for; matrix products, arithmetic and copies ran while one was open for 5% of the time, Pallas kernels for 61%

profile of v2, /device:TPU:0, one launch (start us, length us, event | category | flops | bytes accessed | tf_op | source)
XLA Modules:
  0.0 471.6 jit_solution(2877088426306486872)
XLA Ops:
  3.3 5.1 %collective-permute-start.2 = (bf16[48,1280]{1,0:T(8,128)(2,1)S(1)}, bf16[48,1280]{1,0:T(8,128)(2,1)S(1)}, u32[]{:S(2)}, u32[]{:S(2)}) collective-permute-start(bf16[48,1280]{1,0:T(8,128)(2,1)S(1)} %get-tuple-element.184), channel_id=1, source_target_pairs={{0,12},{1,13},{2,14},{3,15},{4,8},{5,9},{6,10},{7,11},{8,4},{9,5},... | collective-permute-start | bytes 368648 | tf_op jit(solution)/shard_map/ppermute | solution.py:64
  13.4 5.4 %collective-permute-done.1 = bf16[48,1280]{1,0:T(8,128)(2,1)S(1)} collective-permute-done((bf16[48,1280]{1,0:T(8,128)(2,1)S(1)}, bf16[48,1280]{1,0:T(8,128)(2,1)S(1)}, u32[]{:S(2)}, u32[]{:S(2)}) %collective-permute-start.1) | collective-permute-done | bytes 122912 | tf_op jit(solution)/shard_map/ppermute | solution.py:64
  28.1 11.6 %collective-permute-done.5 = bf16[4,48,1280]{2,1,0:T(8,128)(2,1)S(1)} collective-permute-done((bf16[4,48,1280]{2,1,0:T(8,128)(2,1)S(1)}, bf16[4,48,1280]{2,1,0:T(8,128)(2,1)S(1)}, u32[]{:S(2)}, u32[]{:S(2)}) %collective-permute-start.5) | collective-permute-done | bytes 491552 | tf_op jit(solution)/shard_map/ppermute | solution.py:64
  39.7 8.5 %collective-permute-done.4 = bf16[4,48,1280]{2,1,0:T(8,128)(2,1)S(1)} collective-permute-done((bf16[4,48,1280]{2,1,0:T(8,128)(2,1)S(1)}, bf16[4,48,1280]{2,1,0:T(8,128)(2,1)S(1)}, u32[]{:S(2)}, u32[]{:S(2)}) %collective-permute-start.4) | collective-permute-done | bytes 491552 | tf_op jit(solution)/shard_map/ppermute | solution.py:64
  49.6 6.0 %all-to-all-done.refs_0_ = bf16[4,48,3456]{2,1,0:T(8,128)(2,1)S(1)} async-done(((bf16[4,48,3456]{2,1,0:T(8,128)(2,1)}), bf16[4,48,3456]{2,1,0:T(8,128)(2,1)S(1)}, u32[]{:S(2)}, u32[]{:S(2)}) %all-to-all-start) | async-done | bytes 1327136 | tf_op jit(solution)/shard_map/all_to_all | solution.py:828
  59.1 4.8 %convert_element_type.41 = bf16[2048,768]{1,0:T(8,128)(2,1)} convert(f32[2048,768]{1,0:T(8,128)} %param.33) | non-fusion elementwise | flops 1572864 | bytes 9437184 | tf_op jit(solution)/shard_map/convert_element_type | solution.py:850
  64.5 14.5 %qkv.1 = (bf16[2048,768]{1,0:T(8,128)(2,1)}, bf16[2048,768]{1,0:T(8,128)(2,1)}, bf16[2048,768]{1,0:T(8,128)(2,1)}, bf16[2048,768]{1,0:T(8,128)(2,1)}, f32[16,768]{1,0:T(8,128)}) custom-call(s32[2]{0:T(128)} %pad_add_fusion.idx_ref, bf16[2048,768]{1,0:T(8,128)(2,1)} %x_ref.4, bf16[4,4,48,1280]{3,2,1,0:T(8,128)(2,1)} %copy-done.2, ...), custom_call_target="tpu_custom_call" | custom-call | flops 7077888 | bytes 15744 | tf_op jit(solution)/shard_map/qkv/pallas_call | solution.py:174
  79.0 34.0 %attend.1 = (bf16[2048,768]{1,0:T(8,128)(2,1)}, f32[2,6,2,1024]{3,2,1,0:T(2,128)}) custom-call(s32[2]{0:T(128)} %tag_ref.3, bf16[2048,768]{1,0:T(8,128)(2,1)} %get-tuple-element.85.q_ref, bf16[2048,768]{1,0:T(8,128)(2,1)} %get-tuple-element.86.k_ref, bf16[2048,768]{1,0:T(8,128)(2,1)} %get-tuple-element.87.v_ref), custom_call_target="tpu_custom_call" | custom-call | flops 25165824 | bytes 12288 | tf_op jit(solution)/shard_map/attend/pallas_call | solution.py:238
  115.5 9.5 %all-to-all-start.2 = ((bf16[16,128,768]{2,1,0:T(8,128)(2,1)}), bf16[16,128,768]{2,1,0:T(8,128)(2,1)S(1)}, u32[]{:S(2)}, u32[]{:S(2)}) async-start(bf16[16,128,768]{2,1,0:T(8,128)(2,1)} %bitcast.23), calls=%async_computation.2 | async-start | bytes 6291456 | tf_op jit(solution)/shard_map/all_to_all | solution.py:851
  134.2 50.3 %mlp.1 = (f32[2048,768]{1,0:T(8,128)}, bf16[2048,3072]{1,0:T(8,128)(2,1)}, bf16[2048,3072]{1,0:T(8,128)(2,1)}, bf16[2048,768]{1,0:T(8,128)(2,1)}) custom-call(s32[2]{0:T(128)} %pad_add_fusion.idx_ref, bf16[2048,768]{1,0:T(8,128)(2,1)} %x_ref.4, bf16[2048,768]{1,0:T(8,128)(2,1)} %get-tuple-element.88.o_ref, f32[16,768]{1,0:T(8,128)} %get-tuple-element.89.vt_ref, ...), custom_call_target="tpu_custom_call" | custom-call | flops 42467328 | bytes 49152 | tf_op jit(solution)/shard_map/mlp/pallas_call | solution.py:296
  184.5 10.3 %permute.1 = bf16[2048,768]{1,0:T(8,128)(2,1)} custom-call(s32[2048,1]{1,0:T(8,128)} %copy.65.ord_ref, bf16[2048,768]{1,0:T(8,128)(2,1)} %get-tuple-element.94.y_ref), custom_call_target="tpu_custom_call" | custom-call | flops 6291456 | bytes 6144 | tf_op jit(solution)/shard_map/permute/pallas_call | solution.py:325
  196.5 7.3 %all-to-all-start.1 = ((bf16[16,128,768]{2,1,0:T(8,128)(2,1)}), bf16[16,128,768]{2,1,0:T(8,128)(2,1)}, u32[]{:S(2)}, u32[]{:S(2)}) async-start(bf16[16,128,768]{2,1,0:T(8,128)(2,1)} %bitcast.77), calls=%async_computation.1 | async-start | bytes 6291456 | tf_op jit(solution)/shard_map/all_to_all | solution.py:857
  203.8 47.6 %mlp_back.1 = (bf16[2048,768]{1,0:T(8,128)(2,1)}, bf16[2048,3072]{1,0:T(8,128)(2,1)}, f32[2048,768]{1,0:T(8,128)}, bf16[2048,768]{1,0:T(8,128)(2,1)}, bf16[2048,...) custom-call(s32[2]{0:T(128)} %pad_add_fusion.idx_ref, s32[1,2048]{1,0:T(1,128)} %ord_ref.1, ...), custom_call_target="tpu_custom_call" | custom-call | flops 41287680 | bytes 55296 | tf_op jit(solution)/shard_map/mlp_back/pallas_call | solution.py:386
  251.4 19.9 %grad_up.1 = (bf16[768,1920]{1,0:T(8,128)(2,1)}, bf16[768,1920]{1,0:T(8,128)(2,1)}) custom-call(s32[2]{0:T(128)} %pad_add_fusion.idx_ref, bf16[2048,768]{1,0:T(8,128)(2,1)} %get-tuple-element.101.h2_ref, bf16[2048,768]{1,0:T(8,128)(2,1)} %get-tuple-element.88.o_ref, bf16[2048,3072]{1,0:T(8,128)(2,1)} %get-tuple-element.102.du_ref, ...), custom_call_target="tpu_custom_call" | custom-call | flops 17694720 | bytes 26112 | tf_op jit(solution)/shard_map/grad_up/pallas_call | solution.py:470
  271.2 15.2 %grad_down.1 = (bf16[3072,384]{1,0:T(8,128)(2,1)}, bf16[3072,384]{1,0:T(8,128)(2,1)}) custom-call(s32[2]{0:T(128)} %pad_add_fusion.idx_ref, bf16[2048,3072]{1,0:T(8,128)(2,1)} %get-tuple-element.105.g_ref, bf16[2048,768]{1,0:T(8,128)(2,1)} %get-tuple-element.106.dm_ref), custom_call_target="tpu_custom_call" | custom-call | flops 14155776 | bytes 19968 | tf_op jit(solution)/shard_map/grad_down/pallas_call | solution.py:439
  287.0 5.1 %convert_element_type.42 = f32[2048,768]{1,0:T(8,128)} convert(bf16[2048,768]{1,0:T(8,128)(2,1)} %bitcast.22) | non-fusion elementwise | flops 1572864 | bytes 9437184 | tf_op jit(solution)/shard_map/convert_element_type | solution.py:866
  293.6 7.9 %sum_far.2 = (bf16[4,48,3456]{2,1,0:T(8,128)(2,1)}, bf16[4,48,3456]{2,1,0:T(8,128)(2,1)}, bf16[4,48,3456]{2,1,0:T(8,128)(2,1)}, bf16[4,48,3456]{2,1,0:T(8,128)(2,1)}) custom-call(s32[2]{0:T(128)} %pad_add_fusion.idx_ref, bf16[16,48,1920]{2,1,0:T(8,128)(2,1)} %bitcast.57, bf16[16,48,1920]{2,1,0:T(8,128)(2,1)} %bitcast.58, bf16[16,48,1920]{2,1,0:T(8,128)(2,1)} %bitcast.59, ...), custom_call_target="tpu_custom_call" | custom-call | flops 2592 | bytes 15552 | tf_op jit(solution)/shard_map/sum_far/pallas_call | solution.py:670
  307.2 49.8 %attend_back.1 = (bf16[2048,768]{1,0:T(8,128)(2,1)}, bf16[2048,768]{1,0:T(8,128)(2,1)}, bf16[2048,768]{1,0:T(8,128)(2,1)}) custom-call(s32[2]{0:T(128)} %tag_ref.3, bf16[2048,768]{1,0:T(8,128)(2,1)} %get-tuple-element.85.q_ref, bf16[2048,768]{1,0:T(8,128)(2,1)} %get-tuple-element.86.k_ref, bf16[2048,768]{1,0:T(8,128)(2,1)} %get-tuple-element.87.v_ref, ...), custom_call_target="tpu_custom_call" | custom-call | flops 62914560 | bytes 24576 | tf_op jit(solution)/shard_map/attend_back/pallas_call | solution.py:554
  357.0 6.1 %collective-permute-done.17.refs_2_ = bf16[4,48,3456]{2,1,0:T(8,128)(2,1)S(1)} collective-permute-done((bf16[4,48,3456]{2,1,0:T(8,128)(2,1)}, bf16[4,48,3456]{2,1,0:T(8,128)(2,1)S(1)}, u32[]{:S(2)}, u32[]{:S(2)}) %collective-permute-start.17) | collective-permute-done | bytes 1327136 | tf_op jit(solution)/shard_map/ppermute | solution.py:64
  368.6 4.8 %all-to-all-start.3 = ((bf16[4,48,3456]{2,1,0:T(8,128)(2,1)}), bf16[4,48,3456]{2,1,0:T(8,128)(2,1)S(1)}, u32[]{:S(2)}, u32[]{:S(2)}) async-start(bf16[4,48,3456]{2,1,0:T(8,128)(2,1)} %sum_parts.1), calls=%async_computation.3 | async-start | bytes 2654208 | tf_op jit(solution)/shard_map/all_to_all | solution.py:872
  373.4 10.2 %grad_qkv_other.1 = bf16[768,1152]{1,0:T(8,128)(2,1)} custom-call(s32[2]{0:T(128)} %pad_add_fusion.idx_ref, bf16[2048,768]{1,0:T(8,128)(2,1)} %get-tuple-element.133.h_ref, bf16[2048,768]{1,0:T(8,128)(2,1)} %get-tuple-element.136.dq_ref, bf16[2048,768]{1,0:T(8,128)(2,1)} %get-tuple-element.137.dk_ref, bf16[2048,768]{1,0:T(8,128)(2,1)} %get-tuple-element.138.dv_ref), custom_call_target="tpu_custom_call" | custom-call | flops 3538944 | bytes 9216 | tf_op jit(solution)/shard_map/grad_qkv_other/pallas_call | solution.py:580
  383.6 11.7 %collective-permute-start.19 = (bf16[768,1152]{1,0:T(8,128)(2,1)}, bf16[768,1152]{1,0:T(8,128)(2,1)S(1)}, u32[]{:S(2)}, u32[]{:S(2)}) collective-permute-start(bf16[768,1152]{1,0:T(8,128)(2,1)} %grad_qkv_other.1), channel_id=1, source_target_pairs={{0,16},{16,0},{1,17},{17,1},{2,18},{18,2},{3,19},{19,3},{4,20},{20... | collective-permute-start | bytes 5308424 | tf_op jit(solution)/shard_map/ppermute | solution.py:68
  395.3 10.2 %grad_qkv_own.1 = bf16[768,1152]{1,0:T(8,128)(2,1)} custom-call(s32[2]{0:T(128)} %pad_add_fusion.idx_ref, bf16[2048,768]{1,0:T(8,128)(2,1)} %get-tuple-element.133.h_ref, bf16[2048,768]{1,0:T(8,128)(2,1)} %get-tuple-element.136.dq_ref, bf16[2048,768]{1,0:T(8,128)(2,1)} %get-tuple-element.137.dk_ref, bf16[2048,768]{1,0:T(8,128)(2,1)} %get-tuple-element.138.dv_ref), custom_call_target="tpu_custom_call" | custom-call | flops 3538944 | bytes 9216 | tf_op jit(solution)/shard_map/grad_qkv_own/pallas_call | solution.py:580
  416.4 18.1 %tokens_back.1 = (f32[2048,768]{1,0:T(8,128)}, f32[8,768]{1,0:T(8,128)}) custom-call(s32[2]{0:T(128)} %pad_add_fusion.idx_ref, bf16[2048,768]{1,0:T(8,128)(2,1)} %x_ref.4, f32[16,768]{1,0:T(8,128)} %get-tuple-element.89.vt_ref, f32[2048,768]{1,0:T(8,128)} %get-tuple-element.109.dx2_ref, bf16[2048,768]{1,0:T(8,128)(2,1)} %get-tuple-element.136.dq_ref, ...), custom_call_target="tpu_custom_call" | custom-call | flops 10616832 | bytes 28032 | tf_op jit(solution)/shard_map/tokens_back/pallas_call | solution.py:625
  (150 shorter events, 96.2 us)
Async XLA Ops:
  3.3 10.1 %collective-permute-start.2 = (bf16[48,1280]{1,0:T(8,128)(2,1)S(1)}, bf16[48,1280]{1,0:T(8,128)(2,1)S(1)}, u32[]{:S(2)}, u32[]{:S(2)}) collective-permute-start(bf16[48,1280]{1,0:T(8,128)(2,1)S(1)} %get-tuple-element.184), channel_id=1, source_target_pairs={{0,12},{1,13},{2,14},{3,15},{4,8},{5,9},{6,10},{7,11},{8,4},{9,5},... | collective-permute-start | bytes 368648 | tf_op jit(solution)/shard_map/ppermute | solution.py:64
  8.4 10.4 %collective-permute-start.1 = (bf16[48,1280]{1,0:T(8,128)(2,1)S(1)}, bf16[48,1280]{1,0:T(8,128)(2,1)S(1)}, u32[]{:S(2)}, u32[]{:S(2)}) collective-permute-start(bf16[48,1280]{1,0:T(8,128)(2,1)S(1)} %get-tuple-element.184), channel_id=1, source_target_pairs={{0,8},{1,9},{2,10},{3,11},{4,12},{5,13},{6,14},{7,15},{8,0},{9,1},... | collective-permute-start | bytes 368648 | tf_op jit(solution)/shard_map/ppermute | solution.py:64
  8.4 10.4 %collective-permute-start = (bf16[48,1280]{1,0:T(8,128)(2,1)S(1)}, bf16[48,1280]{1,0:T(8,128)(2,1)S(1)}, u32[]{:S(2)}, u32[]{:S(2)}) collective-permute-start(bf16[48,1280]{1,0:T(8,128)(2,1)S(1)} %get-tuple-element.184), channel_id=1, source_target_pairs={{0,4},{1,5},{2,6},{3,7},{4,0},{5,1},{6,2},{7,3},{8,12},{9,13},{10,... | collective-permute-start | bytes 368648 | tf_op jit(solution)/shard_map/ppermute | solution.py:64
  20.8 34.8 %all-to-all-start = ((bf16[4,48,3456]{2,1,0:T(8,128)(2,1)}), bf16[4,48,3456]{2,1,0:T(8,128)(2,1)S(1)}, u32[]{:S(2)}, u32[]{:S(2)}) async-start(bf16[4,48,3456]{2,1,0:T(8,128)(2,1)} %broadcast_in_dim.2), calls=%async_computation | async-start | bytes 2654208 | tf_op jit(solution)/shard_map/all_to_all | solution.py:828
  24.6 15.1 %collective-permute-start.5 = (bf16[4,48,1280]{2,1,0:T(8,128)(2,1)S(1)}, bf16[4,48,1280]{2,1,0:T(8,128)(2,1)S(1)}, u32[]{:S(2)}, u32[]{:S(2)}) collective-permute-start(bf16[4,48,1280]{2,1,0:T(8,128)(2,1)S(1)} %get-tuple-element.176), channel_id=1, source_target_pairs={{0,3},{1,2},{2,1},{3,0},{4,7},{5,6},{6,5},{7,4},{8,11},{9,10},{10,... | collective-permute-start | bytes 1474568 | tf_op jit(solution)/shard_map/ppermute | solution.py:64
  27.0 21.1 %collective-permute-start.4 = (bf16[4,48,1280]{2,1,0:T(8,128)(2,1)S(1)}, bf16[4,48,1280]{2,1,0:T(8,128)(2,1)S(1)}, u32[]{:S(2)}, u32[]{:S(2)}) collective-permute-start(bf16[4,48,1280]{2,1,0:T(8,128)(2,1)S(1)} %get-tuple-element.176), channel_id=1, source_target_pairs={{0,2},{1,3},{2,0},{3,1},{4,6},{5,7},{6,4},{7,5},{8,10},{9,11},{10,... | collective-permute-start | bytes 1474568 | tf_op jit(solution)/shard_map/ppermute | solution.py:64
  27.5 20.7 %collective-permute-start.3 = (bf16[4,48,1280]{2,1,0:T(8,128)(2,1)S(1)}, bf16[4,48,1280]{2,1,0:T(8,128)(2,1)S(1)}, u32[]{:S(2)}, u32[]{:S(2)}) collective-permute-start(bf16[4,48,1280]{2,1,0:T(8,128)(2,1)S(1)} %get-tuple-element.176), channel_id=1, source_target_pairs={{0,1},{1,0},{2,3},{3,2},{4,5},{5,4},{6,7},{7,6},{8,9},{9,8},{10,11... | collective-permute-start | bytes 1474568 | tf_op jit(solution)/shard_map/ppermute | solution.py:64
  49.5 14.9 %collective-permute-start.6 = (bf16[4,4,48,1280]{3,2,1,0:T(8,128)(2,1)S(1)}, bf16[4,4,48,1280]{3,2,1,0:T(8,128)(2,1)}, u32[]{:S(2)}, u32[]{:S(2)}) collective-permute-start(bf16[4,4,48,1280]{3,2,1,0:T(8,128)(2,1)S(1)} %pad_maximum_fusion.refs_0_), channel_id=1, source_target_pairs={{0,16},{16,0},{1,17},{17,1},{2,18},{18,2},{3,19},{19,3},{4,20},{20... | collective-permute-start | bytes 5898248 | tf_op jit(solution)/shard_map/ppermute | solution.py:68
  55.6 57.3 %collective-permute-start.7 = (bf16[4,48,3456]{2,1,0:T(8,128)(2,1)S(1)}, bf16[4,48,3456]{2,1,0:T(8,128)(2,1)}, u32[]{:S(2)}, u32[]{:S(2)}) collective-permute-start(bf16[4,48,3456]{2,1,0:T(8,128)(2,1)S(1)} %all-to-all-done.refs_0_), channel_id=1, source_target_pairs={{0,1},{1,0},{2,3},{3,2},{4,5},{5,4},{6,7},{7,6},{8,9},{9,8},{10,11... | collective-permute-start | bytes 3981320 | tf_op jit(solution)/shard_map/ppermute | solution.py:64
  57.1 58.3 %collective-permute-start.8 = (bf16[4,48,3456]{2,1,0:T(8,128)(2,1)S(1)}, bf16[4,48,3456]{2,1,0:T(8,128)(2,1)}, u32[]{:S(2)}, u32[]{:S(2)}) collective-permute-start(bf16[4,48,3456]{2,1,0:T(8,128)(2,1)S(1)} %all-to-all-done.refs_0_), channel_id=1, source_target_pairs={{0,2},{1,3},{2,0},{3,1},{4,6},{5,7},{6,4},{7,5},{8,10},{9,11},{10,... | collective-permute-start | bytes 3981320 | tf_op jit(solution)/shard_map/ppermute | solution.py:64
  58.6 56.8 %collective-permute-start.9 = (bf16[4,48,3456]{2,1,0:T(8,128)(2,1)S(1)}, bf16[4,48,3456]{2,1,0:T(8,128)(2,1)}, u32[]{:S(2)}, u32[]{:S(2)}) collective-permute-start(bf16[4,48,3456]{2,1,0:T(8,128)(2,1)S(1)} %all-to-all-done.refs_0_), channel_id=1, source_target_pairs={{0,3},{1,2},{2,1},{3,0},{4,7},{5,6},{6,5},{7,4},{8,11},{9,10},{10,... | collective-permute-start | bytes 3981320 | tf_op jit(solution)/shard_map/ppermute | solution.py:64
  115.5 79.4 %all-to-all-start.2 = ((bf16[16,128,768]{2,1,0:T(8,128)(2,1)}), bf16[16,128,768]{2,1,0:T(8,128)(2,1)S(1)}, u32[]{:S(2)}, u32[]{:S(2)}) async-start(bf16[16,128,768]{2,1,0:T(8,128)(2,1)} %bitcast.23), calls=%async_computation.2 | async-start | bytes 6291456 | tf_op jit(solution)/shard_map/all_to_all | solution.py:851
  196.5 90.5 %all-to-all-start.1 = ((bf16[16,128,768]{2,1,0:T(8,128)(2,1)}), bf16[16,128,768]{2,1,0:T(8,128)(2,1)}, u32[]{:S(2)}, u32[]{:S(2)}) async-start(bf16[16,128,768]{2,1,0:T(8,128)(2,1)} %bitcast.77), calls=%async_computation.1 | async-start | bytes 6291456 | tf_op jit(solution)/shard_map/all_to_all | solution.py:857
  271.2 20.8 %collective-permute-start.14 = (bf16[768,1920]{1,0:T(8,128)(2,1)}, bf16[768,1920]{1,0:T(8,128)(2,1)S(1)}, u32[]{:S(2)}, u32[]{:S(2)}) collective-permute-start(bf16[768,1920]{1,0:T(8,128)(2,1)} %get-tuple-element.112), channel_id=1, source_target_pairs={{0,16},{16,0},{1,17},{17,1},{2,18},{18,2},{3,19},{19,3},{4,20},{20... | collective-permute-start | bytes 8847368 | tf_op jit(solution)/shard_map/ppermute | solution.py:68
  301.6 55.4 %collective-permute-start.16 = (bf16[4,48,3456]{2,1,0:T(8,128)(2,1)}, bf16[4,48,3456]{2,1,0:T(8,128)(2,1)S(1)}, u32[]{:S(2)}, u32[]{:S(2)}) collective-permute-start(bf16[4,48,3456]{2,1,0:T(8,128)(2,1)} %get-tuple-element.122), channel_id=1, source_target_pairs={{0,1},{1,0},{2,3},{3,2},{4,5},{5,4},{6,7},{7,6},{8,9},{9,8},{10,11... | collective-permute-start | bytes 3981320 | tf_op jit(solution)/shard_map/ppermute | solution.py:64
  303.7 59.4 %collective-permute-start.17 = (bf16[4,48,3456]{2,1,0:T(8,128)(2,1)}, bf16[4,48,3456]{2,1,0:T(8,128)(2,1)S(1)}, u32[]{:S(2)}, u32[]{:S(2)}) collective-permute-start(bf16[4,48,3456]{2,1,0:T(8,128)(2,1)} %get-tuple-element.123), channel_id=1, source_target_pairs={{0,2},{1,3},{2,0},{3,1},{4,6},{5,7},{6,4},{7,5},{8,10},{9,11},{10,... | collective-permute-start | bytes 3981320 | tf_op jit(solution)/shard_map/ppermute | solution.py:64
  305.1 57.9 %collective-permute-start.18 = (bf16[4,48,3456]{2,1,0:T(8,128)(2,1)}, bf16[4,48,3456]{2,1,0:T(8,128)(2,1)}, u32[]{:S(2)}, u32[]{:S(2)}) collective-permute-start(bf16[4,48,3456]{2,1,0:T(8,128)(2,1)} %get-tuple-element.124), channel_id=1, source_target_pairs={{0,3},{1,2},{2,1},{3,0},{4,7},{5,6},{6,5},{7,4},{8,11},{9,10},{10,... | collective-permute-start | bytes 3981320 | tf_op jit(solution)/shard_map/ppermute | solution.py:64
  368.6 65.9 %all-to-all-start.3 = ((bf16[4,48,3456]{2,1,0:T(8,128)(2,1)}), bf16[4,48,3456]{2,1,0:T(8,128)(2,1)S(1)}, u32[]{:S(2)}, u32[]{:S(2)}) async-start(bf16[4,48,3456]{2,1,0:T(8,128)(2,1)} %sum_parts.1), calls=%async_computation.3 | async-start | bytes 2654208 | tf_op jit(solution)/shard_map/all_to_all | solution.py:872
  383.6 21.9 %collective-permute-start.19 = (bf16[768,1152]{1,0:T(8,128)(2,1)}, bf16[768,1152]{1,0:T(8,128)(2,1)S(1)}, u32[]{:S(2)}, u32[]{:S(2)}) collective-permute-start(bf16[768,1152]{1,0:T(8,128)(2,1)} %grad_qkv_other.1), channel_id=1, source_target_pairs={{0,16},{16,0},{1,17},{17,1},{2,18},{18,2},{3,19},{19,3},{4,20},{20... | collective-permute-start | bytes 5308424 | tf_op jit(solution)/shard_map/ppermute | solution.py:68
  411.4 39.7 %collective-permute-start.20 = (bf16[4,48,1152]{2,1,0:T(8,128)(2,1)}, bf16[4,48,1152]{2,1,0:T(8,128)(2,1)S(1)}, u32[]{:S(2)}, u32[]{:S(2)}) collective-permute-start(bf16[4,48,1152]{2,1,0:T(8,128)(2,1)} %get-tuple-element.140), channel_id=1, source_target_pairs={{0,1},{1,0},{2,3},{3,2},{4,5},{5,4},{6,7},{7,6},{8,9},{9,8},{10,11... | collective-permute-start | bytes 1327112 | tf_op jit(solution)/shard_map/ppermute | solution.py:64
  413.1 38.0 %collective-permute-start.21 = (bf16[4,48,1152]{2,1,0:T(8,128)(2,1)}, bf16[4,48,1152]{2,1,0:T(8,128)(2,1)S(1)}, u32[]{:S(2)}, u32[]{:S(2)}) collective-permute-start(bf16[4,48,1152]{2,1,0:T(8,128)(2,1)} %get-tuple-element.141), channel_id=1, source_target_pairs={{0,2},{1,3},{2,0},{3,1},{4,6},{5,7},{6,4},{7,5},{8,10},{9,11},{10,... | collective-permute-start | bytes 1327112 | tf_op jit(solution)/shard_map/ppermute | solution.py:64
  415.3 35.9 %collective-permute-start.22 = (bf16[4,48,1152]{2,1,0:T(8,128)(2,1)}, bf16[4,48,1152]{2,1,0:T(8,128)(2,1)S(1)}, u32[]{:S(2)}, u32[]{:S(2)}) collective-permute-start(bf16[4,48,1152]{2,1,0:T(8,128)(2,1)} %get-tuple-element.142), channel_id=1, source_target_pairs={{0,3},{1,2},{2,1},{3,0},{4,7},{5,6},{6,5},{7,4},{8,11},{9,10},{10,... | collective-permute-start | bytes 1327112 | tf_op jit(solution)/shard_map/ppermute | solution.py:64
  434.8 25.1 %collective-permute-start.30 = (bf16[48,3456]{1,0:T(8,128)(2,1)S(1)}, bf16[48,3456]{1,0:T(8,128)(2,1)S(1)}, u32[]{:S(2)}, u32[]{:S(2)}) collective-permute-start(bf16[48,3456]{1,0:T(8,128)(2,1)S(1)} %reduce_sum.12), channel_id=1, source_target_pairs={{0,16},{16,0},{1,17},{17,1},{2,18},{18,2},{3,19},{19,3},{4,20},{20... | collective-permute-start | bytes 995336 | tf_op jit(solution)/shard_map/ppermute | solution.py:68
  459.2 8.6 %collective-permute-start.27 = (bf16[48,1280]{1,0:T(8,128)(2,1)}, bf16[48,1280]{1,0:T(8,128)(2,1)S(1)}, u32[]{:S(2)}, u32[]{:S(2)}) collective-permute-start(bf16[48,1280]{1,0:T(8,128)(2,1)} %get-tuple-element.148), channel_id=1, source_target_pairs={{0,8},{1,9},{2,10},{3,11},{4,12},{5,13},{6,14},{7,15},{8,0},{9,1},... | collective-permute-start | bytes 368648 | tf_op jit(solution)/shard_map/ppermute | solution.py:64
  (29 other events, 155.9 us)

commit v3 on v2

v3 whole, which is shorter than its diff:
```python
import functools
import math

import jax
import jax.numpy as jnp
from jax import lax
from jax.experimental import pallas as pl
from jax.experimental.pallas import tpu as pltpu
from jax.sharding import PartitionSpec as P

F32 = jnp.float32
BF = jnp.bfloat16
EPS = 1e-6
LOG2E = math.log2(math.e)
LN2 = math.log(2.0)
NT = (((1,), (1,)), ((), ()))
TN = (((0,), (0,)), ((), ()))
NN = (((1,), (0,)), ((), ()))
ANY = pl.BlockSpec(memory_space=pl.ANY)
VECS = 16
SDS = jax.ShapeDtypeStruct


def dg(a, b, dims):
    return lax.dot_general(a, b, dims, preferred_element_type=F32)


def params(axes=1):
    return pltpu.CompilerParams(
        vmem_limit_bytes=58 * 2**20, dimension_semantics=("arbitrary",) * axes
    )


def cost(flops, nbytes, trans=0):
    return pl.CostEstimate(flops=int(flops) >> 10, bytes_accessed=int(nbytes) >> 10, transcendentals=int(trans) >> 10)


def rows_of(height, width):
    return pl.BlockSpec((height, width), lambda i, *_: (i, 0))


def whole(shape):
    zeros = (0,) * len(shape)
    return pl.BlockSpec(shape, lambda *_: zeros, pipeline_mode=pl.Buffered(1))


def fixed(shape):
    zeros = (0,) * len(shape)
    return pl.BlockSpec(shape, lambda *_: zeros)


def norm_stats(x):
    n = x.shape[-1]
    c = x - jnp.sum(x, axis=-1, keepdims=True) * (1.0 / n)
    var = jnp.sum(c * c, axis=-1, keepdims=True) * (1.0 / n)
    return c, lax.rsqrt(var + EPS)


def after(x, *deps):
    return lax.optimization_barrier((x,) + deps)[0]


def xor_pp(x, b, n):
    return lax.ppermute(x, "fsdp", [(i, i ^ b) for i in range(n)])


def core_swap(x, m):
    return lax.ppermute(x, "dp", [(i, i ^ 1) for i in range(m)])


def gather_near(x, n):
    q = n // 4
    return jnp.stack([x] + [xor_pp(x, d * q, n) for d in (1, 2, 3)])


def tops(n):
    q = n // 4
    return [[low + z * q for z in range(4)] for low in range(q)]


def gather_far(s, n):
    return [s] + [xor_pp(s, e, n) for e in range(1, n // 4)]


def fits(rows, n):
    return rows % 16 == 0 and n == 16


def settle(pieces, order, c, n, wide=None):
    q = n // 4
    rows, width = pieces[0].shape[1:]
    if fits(rows, n):
        return pieces
    height = n * rows // 16
    halves = []
    for side in (pieces[:q], pieces[q:]):
        rel = jnp.stack(side, axis=1).reshape((n, rows, width))
        whole_side = jnp.take(rel, order, axis=0)
        flat = whole_side.reshape(16, height, width)
        if wide is not None:
            cut = width * (wide + 1) // (2 * wide + 1)
            low = whole_side[..., cut:].reshape(n, rows, wide, -1).transpose(0, 2, 1, 3)
            low = low.reshape(16, wide, height, -1).transpose(0, 2, 1, 3).reshape(16, height, -1)
            flat = jnp.concatenate([flat[..., :cut], low], axis=2)
        halves.append(flat.reshape(4, 4, height, width))
    left, right = jnp.where(c == 0, halves[0], halves[1]), jnp.where(c == 0, halves[1], halves[0])
    return [side[:, e] for side in (left, right) for e in range(4)]


def load_pieces(idx_ref, plan, sem):
    c = idx_ref[1]
    started = []
    for find, shard, start, width, dst, height, first in plan:
        for e in range(4):
            for d in range(4):
                for block, h in zip(find(e, d), (c, 1 - c), strict=False):
                    rows = block.shape[0]
                    at = pl.ds(pl.multiple_of(shard(e, d) * height + first, 16), rows)
                    cols = pl.ds(pl.multiple_of(h * width, 128), width) if dst.shape[1] > width else slice(None)
                    started.append(pltpu.make_async_copy(block.at[:, pl.ds(start, width)], dst.at[at, cols], sem))
    for cp in started:
        cp.start()
    return started


def relative(idx_ref):
    return lambda e, d: lax.bitwise_xor(idx_ref[0], jnp.int32(d * 4 + e))


def by_top(idx_ref):
    return lambda e, d: lax.bitwise_xor(idx_ref[0] % 4, jnp.int32(e)) + d * 4


def load_qkv(idx_ref, pieces, w_ref, sem, vec_ref=None):
    def find(e, d):
        if len(pieces) == 8:
            return pieces[e].at[d], pieces[4 + e].at[d]
        return pieces[e].at[d], pieces[5].at[e - 1, d] if e else pieces[4].at[d]

    where = relative(idx_ref)
    rows, half = pieces[0].shape[1], w_ref.shape[1] // 2
    if vec_ref is not None:
        return load_pieces(idx_ref, [(lambda e, d: find(e, d)[:1], where, half, 128, vec_ref, rows, 0)], sem)
    return load_pieces(idx_ref, [(find, where, 0, half, w_ref, rows, 0)], sem)


def load_mlp(idx_ref, pieces, w1_ref, w2_ref, sem):
    where = by_top(idx_ref)

    def find1(e, d):
        return pieces[e // 2].at[e % 2, d], pieces[2 + e // 2].at[e % 2, d]

    def find2(e, d):
        return pieces[4 + e % 2].at[e // 2, d], pieces[6 + e % 2].at[e // 2, d]

    rows = pieces[0].shape[2]
    w = w2_ref.shape[1] // 2
    plan = [(find1, where, 0, w1_ref.shape[1] // 2, w1_ref, rows, 0)]
    plan += [(find2, where, j * w, w, w2_ref, 4 * rows, j * rows) for j in range(4)]
    return load_pieces(idx_ref, plan, sem.at[0])


def qkv_kernel(idx_ref, x_ref, *refs):
    pieces = refs[:-9]
    q_ref, k_ref, v_ref, h_ref, vt_ref, bu_ref, w_ref, vec_ref, sem = refs[-9:]
    d = x_ref.shape[1]

    @pl.when(pl.program_id(0) == 0)
    def _():
        rows = pieces[0].shape[1]
        vecs = load_qkv(idx_ref, pieces, w_ref, sem.at[1], vec_ref)
        going = load_qkv(idx_ref, pieces, w_ref, sem.at[0])
        for cp in vecs:
            cp.wait()
        table = vec_ref[...].astype(F32).T[:VECS]
        vt_ref[...] = table
        bu_ref[...] = jnp.concatenate(
            [table[8 + j : 9 + j, s * rows : (s + 1) * rows] for s in range(d // rows) for j in range(4)], axis=1
        )
        for cp in going:
            cp.wait()

    c, r = norm_stats(x_ref[...].astype(F32))
    h = (c * r * vt_ref[0:1, :] + vt_ref[1:2, :]).astype(BF)
    h_ref[...] = h
    q = dg(h, w_ref[:, :d], NN)
    q_ref[...] = ((q + vt_ref[2:3, :]) * (0.125 * LOG2E)).astype(BF)
    k_ref[...] = dg(h, w_ref[:, d : 2 * d], NN).astype(BF)
    v_ref[...] = (dg(h, w_ref[:, 2 * d :], NN) + vt_ref[3:4, :]).astype(BF)


def qkv(idx, x, pieces, tb=512):
    t, d = x.shape
    return pl.pallas_call(
        qkv_kernel,
        grid_spec=pltpu.PrefetchScalarGridSpec(
            num_scalar_prefetch=1,
            grid=(t // tb,),
            in_specs=[rows_of(tb, d)] + [ANY] * len(pieces),
            out_specs=[rows_of(tb, d)] * 4 + [fixed((VECS, d)), fixed((1, 4 * d))],
            scratch_shapes=[
                pltpu.VMEM((d, 3 * d), BF),
                pltpu.VMEM((d, 128), BF),
                pltpu.SemaphoreType.DMA((2,)),
            ],
        ),
        out_shape=[SDS((t, d), BF)] * 4 + [SDS((VECS, d), F32), SDS((1, 4 * d), F32)],
        compiler_params=params(),
        cost_estimate=cost(6 * t * d * d, t * d * 8 + d * d * 6),
        name="qkv",
    )(idx, x, *pieces)


def attend_kernel(tag_ref, q_ref, k_ref, v_ref, *refs, qb):
    o_ref, l_ref = refs[-2:]
    r = pl.program_id(0)
    length = q_ref.shape[0]
    low = lax.broadcasted_iota(jnp.int32, (1, 128), 1) < 64

    def block(qs, qn, ks, kn):
        q = q_ref[pl.ds(qs, qn), :]
        k = k_ref[pl.ds(ks, kn), :]
        v = v_ref[pl.ds(ks, kn), :]
        outs = []
        for h in range(2):
            sel = low if h == 0 else jnp.logical_not(low)
            qm = jnp.where(sel, q, jnp.asarray(0, BF))
            vm = jnp.where(sel, v, jnp.asarray(1, BF))
            s = dg(qm, k, NT)
            m = jnp.max(s, axis=1, keepdims=True)
            outs.append((dg(jnp.exp2(s - m).astype(BF), vm, NN), m))
        (a, ma), (b, mb) = outs
        acc = jnp.where(low, a, b)
        total = pltpu.roll(jnp.where(low, b, a), 64, 1)
        o_ref[pl.ds(qs, qn), :] = (acc / total).astype(o_ref.dtype)
        lse = (jnp.where(low, ma, mb) + jnp.log2(total)).T
        l_ref[0, 0, 0:1, pl.ds(qs, qn)] = lse[0:1]
        l_ref[0, 0, 1:2, pl.ds(qs, qn)] = lse[64:65]

    @pl.when(tag_ref[r] == 0)
    def _():
        for i in range(length // qb):
            block(i * qb, qb, 0, length)

    @pl.when(tag_ref[r] != 0)
    def _():
        c = length // 4
        for i in range(4):
            block(i * c, c, i * c, c)


def attend(tag, q, k, v, first, pairs, before=(), qb=512):
    t, d = q.shape
    rows = tag.shape[0]
    length = t // rows
    blk = pl.BlockSpec((length, 128), lambda r, p, _: (r, p + first))
    lse = pl.BlockSpec((1, 1, 2, length), lambda r, p, _: (r, p + first, 0, 0))
    return pl.pallas_call(
        functools.partial(attend_kernel, qb=qb),
        grid_spec=pltpu.PrefetchScalarGridSpec(
            num_scalar_prefetch=1,
            grid=(rows, pairs),
            in_specs=[blk] * 3 + [ANY] * len(before),
            out_specs=[blk, lse],
        ),
        out_shape=[SDS((t, d), BF), SDS((rows, d // 128, 2, length), F32)],
        input_output_aliases={4: 0, 5: 1} if before else {},
        compiler_params=params(2),
        cost_estimate=cost(2048 * t * length * pairs, t * d * 8, t * length * 12),
        name="attend",
    )(tag, q, k, v, *before)


ODDS = (2.3021649, 1.05007451e-1, -2.545477e-4, -1.0560537e-4, 4.093017e-6)


def gelu_both(u):
    z = u * u
    odds = ODDS[3] + z * ODDS[4]
    odds = ODDS[2] + z * odds
    odds = ODDS[1] + z * odds
    odds = ODDS[0] + z * odds
    phi = pltpu.reciprocal(1.0 + jnp.exp2(-u * odds), approx=True)
    density = jnp.exp2(z * (-0.5 * LOG2E) - 0.5 * math.log2(2.0 * math.pi))
    return u * phi, phi + u * density


def mlp_kernel(idx_ref, x_ref, o_ref, vt_ref, bu_ref, *refs, fc):
    pieces = refs[:8]
    x2_ref, gl_ref, gp_ref, y_ref, w1_ref, w2_ref, sem = refs[8:]
    d = x_ref.shape[1]
    ff = w2_ref.shape[0]

    @pl.when(pl.program_id(0) == 0)
    def _():
        going = load_mlp(idx_ref, pieces, w1_ref, w2_ref, sem)
        for cp in going:
            cp.wait()

    x2 = x_ref[...].astype(F32) + dg(o_ref[...], w1_ref[:, :d], NN) + vt_ref[4:5, :]
    x2_ref[...] = x2
    c, r = norm_stats(x2)
    h = (c * r * vt_ref[5:6, :] + vt_ref[6:7, :]).astype(BF)
    y = x2 + vt_ref[7:8, :]
    for f in range(0, ff, fc):
        u = dg(h, w1_ref[:, d + f : d + f + fc], NN) + bu_ref[:, f : f + fc]
        g, gp = gelu_both(u)
        g = g.astype(BF)
        gl_ref[:, f : f + fc] = g
        gp_ref[:, f : f + fc] = gp.astype(BF)
        y = y + dg(g, w2_ref[f : f + fc, :], NN)
    y_ref[...] = y.astype(BF)


def mlp(idx, x, o, vt, bu, pieces, tb=256, fc=768):
    t, d = x.shape
    ff = bu.shape[1]
    return pl.pallas_call(
        functools.partial(mlp_kernel, fc=fc),
        grid_spec=pltpu.PrefetchScalarGridSpec(
            num_scalar_prefetch=1,
            grid=(t // tb,),
            in_specs=[rows_of(tb, d)] * 2 + [whole(vt.shape), whole(bu.shape)] + [ANY] * 8,
            out_specs=[rows_of(tb, d), rows_of(tb, ff), rows_of(tb, ff), rows_of(tb, d)],
            scratch_shapes=[
                pltpu.VMEM((d, d + ff), BF),
                pltpu.VMEM((ff, d), BF),
                pltpu.SemaphoreType.DMA((2,)),
            ],
        ),
        out_shape=[SDS((t, d), F32), SDS((t, ff), BF), SDS((t, ff), BF), SDS((t, d), BF)],
        compiler_params=params(),
        cost_estimate=cost(4 * t * d * (d + 2 * ff), t * (10 * d + 4 * ff) + 4 * d * ff, 2 * t * ff),
        name="mlp",
    )(idx, x, o, vt, bu, *pieces)


def permute_kernel(ord_ref, y_ref, o_ref):
    jb = o_ref.shape[0]
    t = y_ref.shape[0]
    order = jnp.broadcast_to(ord_ref[...].astype(F32), (8, jb)).T[:, 0:1]
    hot = jnp.where(order == lax.broadcasted_iota(jnp.int32, (jb, t), 1).astype(F32), 1.0, 0.0)
    o_ref[...] = dg(hot.astype(BF), y_ref[...], NN).astype(BF)


def permute(order, y, jb=512):
    t, d = y.shape
    return pl.pallas_call(
        permute_kernel,
        grid=(t // jb,),
        in_specs=[pl.BlockSpec((1, jb), lambda i: (0, i)), whole((t, d))],
        out_specs=rows_of(jb, d),
        out_shape=SDS((t, d), BF),
        compiler_params=params(),
        cost_estimate=cost(2 * t * t * d, t * d * 4),
        name="permute",
    )(order, y)


def split_halves(c, r, mine_ref, theirs_ref):
    h = r.shape[1] // 2
    left, right = r[:, :h], r[:, h:]
    mine_ref[...] = jnp.where(c == 0, left, right)
    theirs_ref[...] = jnp.where(c == 0, right, left)


def mlp_back_kernel(idx_ref, ord_ref, ret_ref, gp_ref, x2_ref, o_ref, vt_ref, *refs, fc):
    pieces = refs[:8]
    (dm_ref, du_ref, dx2_ref, do_ref, h2_ref, sums_ref, gbu_ref, mine_ref, theirs_ref) = refs[8:17]
    w1_ref, w2_ref, acc_ref, sem = refs[17:]
    i = pl.program_id(0)
    tb, ff = gp_ref.shape
    t, d = ret_ref.shape

    @pl.when(i == 0)
    def _():
        going = load_mlp(idx_ref, pieces, w1_ref, w2_ref, sem)
        sums_ref[...] = jnp.zeros_like(sums_ref)
        gbu_ref[...] = jnp.zeros_like(gbu_ref)
        acc_ref[...] = jnp.zeros_like(acc_ref)
        for cp in going:
            cp.wait()

    at = lax.broadcasted_iota(jnp.int32, (tb, t), 0) + i * tb
    hot = jnp.where(ord_ref[...] == at, 1.0, 0.0).astype(BF)
    dy = dg(hot, ret_ref[...], NN)
    dm = dy.astype(BF)
    dm_ref[...] = dm
    sums_ref[0:1, :] += jnp.sum(dy, axis=0, keepdims=True)
    dh = jnp.zeros((tb, d), F32)
    for f in range(0, ff, fc):
        du = dg(dm, w2_ref[f : f + fc, :], NT) * gp_ref[:, f : f + fc].astype(F32)
        gbu_ref[:, f : f + fc] += jnp.sum(du, axis=0, keepdims=True)
        du = du.astype(BF)
        du_ref[:, f : f + fc] = du
        dh = dh + dg(du, w1_ref[:, d + f : d + f + fc], NT)
    c, r = norm_stats(x2_ref[...])
    xh = c * r
    gain = vt_ref[5:6, :]
    h2_ref[...] = (xh * gain + vt_ref[6:7, :]).astype(BF)
    sums_ref[1:2, :] += jnp.sum(dh * xh, axis=0, keepdims=True)
    sums_ref[2:3, :] += jnp.sum(dh, axis=0, keepdims=True)
    dz = dh * gain
    m1 = jnp.sum(dz, axis=-1, keepdims=True) * (1.0 / d)
    m2 = jnp.sum(dz * xh, axis=-1, keepdims=True) * (1.0 / d)
    dx2 = dy + r * (dz - m1 - xh * m2)
    dx2_ref[...] = dx2
    da = dx2.astype(BF)
    sums_ref[3:4, :] += jnp.sum(da.astype(F32), axis=0, keepdims=True)
    do_ref[...] = dg(da, w1_ref[:, :d], NT).astype(BF)
    acc_ref[...] += dg(o_ref[...], da, TN)

    @pl.when(i == pl.num_programs(0) - 1)
    def _():
        split_halves(idx_ref[1], acc_ref[...].astype(BF), mine_ref, theirs_ref)


def mlp_back(idx, order_row, ret, gp, x2, o, vt, pieces, tb=256, fc=768):
    t, d = x2.shape
    ff = gp.shape[1]
    return pl.pallas_call(
        functools.partial(mlp_back_kernel, fc=fc),
        grid_spec=pltpu.PrefetchScalarGridSpec(
            num_scalar_prefetch=1,
            grid=(t // tb,),
            in_specs=[whole((1, t)), whole((t, d)), rows_of(tb, ff), rows_of(tb, d), rows_of(tb, d), whole(vt.shape)]
            + [ANY] * 8,
            out_specs=[rows_of(tb, d), rows_of(tb, ff)]
            + [rows_of(tb, d)] * 3
            + [fixed((8, d)), fixed((1, ff))]
            + [fixed((d, d // 2))] * 2,
            scratch_shapes=[
                pltpu.VMEM((d, d + ff), BF),
                pltpu.VMEM((ff, d), BF),
                pltpu.VMEM((d, d), F32),
                pltpu.SemaphoreType.DMA((2,)),
            ],
        ),
        out_shape=[
            SDS((t, d), BF),
            SDS((t, ff), BF),
            SDS((t, d), F32),
            SDS((t, d), BF),
            SDS((t, d), BF),
            SDS((8, d), F32),
            SDS((1, ff), F32),
            SDS((d, d // 2), BF),
            SDS((d, d // 2), BF),
        ],
        compiler_params=params(),
        cost_estimate=cost(2 * t * d * (d + 2 * ff + t) * 1.5, t * (20 * d + 4 * ff)),
        name="mlp_back",
    )(idx, order_row, ret, gp, x2, o, vt, *pieces)


def grad_down_kernel(idx_ref, g_ref, dm_ref, mine_ref, theirs_ref):
    split_halves(idx_ref[1], dg(g_ref[...], dm_ref[...], TN).astype(BF), mine_ref, theirs_ref)


def grad_down(idx, g, dm, mb=768):
    t, ff = g.shape
    d = dm.shape[1]
    return pl.pallas_call(
        grad_down_kernel,
        grid_spec=pltpu.PrefetchScalarGridSpec(
            num_scalar_prefetch=1,
            grid=(ff // mb,),
            in_specs=[pl.BlockSpec((t, mb), lambda i, _: (0, i)), whole((t, d))],
            out_specs=[rows_of(mb, d // 2)] * 2,
        ),
        out_shape=[SDS((ff, d // 2), BF)] * 2,
        compiler_params=params(),
        cost_estimate=cost(3 * t * ff * d, 2 * t * (ff + d) + 2 * ff * d),
        name="grad_down",
    )(idx, g, dm)


def grad_wide_kernel(idx_ref, a_ref, b_ref, mine_ref, theirs_ref):
    split_halves(idx_ref[1], dg(a_ref[...], b_ref[...], TN).astype(BF), mine_ref, theirs_ref)


def grad_wide(idx, a, b, name):
    t, d = a.shape
    width = b.shape[1]
    return pl.pallas_call(
        grad_wide_kernel,
        grid_spec=pltpu.PrefetchScalarGridSpec(
            num_scalar_prefetch=1,
            grid=(width // d,),
            in_specs=[whole((t, d)), pl.BlockSpec((t, d), lambda i, _: (0, i))],
            out_specs=[pl.BlockSpec((d, d // 2), lambda i, _: (0, i))] * 2,
        ),
        out_shape=[SDS((d, width // 2), BF)] * 2,
        compiler_params=params(),
        cost_estimate=cost(3 * t * width * d, 2 * t * (width + d) + 2 * width * d),
        name=name,
    )(idx, a, b)


def attend_back_kernel(
    tag_ref, q_ref, k_ref, v_ref, do_ref, o_ref, l_ref, dq_ref, dk_ref, dv_ref, dl_ref, dqt_ref, *, kb, qb
):
    r = pl.program_id(0)
    length = q_ref.shape[0]
    low = lax.broadcasted_iota(jnp.int32, (1, 128), 1) < 64
    prod = (do_ref[...].astype(F32) * o_ref[...].astype(F32)).T
    dl_ref[0:1, :] = jnp.sum(prod[0:64], axis=0, keepdims=True)
    dl_ref[1:2, :] = jnp.sum(prod[64:128], axis=0, keepdims=True)

    def block(ks, kn, qs, qn):
        k = k_ref[pl.ds(ks, kn), :]
        v = v_ref[pl.ds(ks, kn), :]
        q = q_ref[pl.ds(qs, qn), :]
        do = do_ref[pl.ds(qs, qn), :]
        dks = []
        dvs = []
        dqs = []
        for h in range(2):
            sel = low if h == 0 else jnp.logical_not(low)
            km = jnp.where(sel, k, jnp.asarray(0, BF))
            vm = jnp.where(sel, v, jnp.asarray(0, BF))
            pt = jnp.exp2(dg(km, q, NT) - l_ref[0, 0, h : h + 1, pl.ds(qs, qn)])
            dst = (pt * (dg(vm, do, NT) - dl_ref[h : h + 1, pl.ds(qs, qn)])).astype(BF)
            dvs.append(dg(pt.astype(BF), do, NN))
            dks.append(dg(dst, q, NN))
            dqs.append(dg(km.T, dst, NN))
        return jnp.where(low, dks[0], dks[1]), jnp.where(low, dvs[0], dvs[1]), dqs[0] + dqs[1]

    def run(kn, qn, plan):
        seen = set()
        for ks, starts in plan:
            dk = dv = None
            for qs in starts:
                a, b, dq = block(ks, kn, qs, qn)
                dk = a if dk is None else dk + a
                dv = b if dv is None else dv + b
                if qs in seen:
                    dqt_ref[:, pl.ds(qs, qn)] += dq
                else:
                    dqt_ref[:, pl.ds(qs, qn)] = dq
                seen.add(qs)
            dk_ref[pl.ds(ks, kn), :] = (dk * LN2).astype(BF)
            dv_ref[pl.ds(ks, kn), :] = dv.astype(BF)
        dq_ref[...] = (dqt_ref[...].T * 0.125).astype(BF)

    @pl.when(tag_ref[r] == 0)
    def _():
        run(kb, qb, [(ks, range(0, length, qb)) for ks in range(0, length, kb)])

    @pl.when(tag_ref[r] != 0)
    def _():
        c = length // 4
        run(c, c, [(ks, [ks]) for ks in range(0, length, c)])


def attend_back(tag, q, k, v, do, o, lse, first, pairs, kb=512, qb=512):
    t = q.shape[0]
    d = pairs * 128
    rows = tag.shape[0]
    length = t // rows
    blk = pl.BlockSpec((length, 128), lambda r, p, _: (r, p + first))
    out = pl.BlockSpec((length, 128), lambda r, p, _: (r, p))
    lse_spec = pl.BlockSpec((1, 1, 2, length), lambda r, p, _: (r, p + first, 0, 0))
    return pl.pallas_call(
        functools.partial(attend_back_kernel, kb=kb, qb=qb),
        grid_spec=pltpu.PrefetchScalarGridSpec(
            num_scalar_prefetch=1,
            grid=(rows, pairs),
            in_specs=[blk] * 5 + [lse_spec],
            out_specs=[out] * 3,
            scratch_shapes=[pltpu.VMEM((2, length), F32), pltpu.VMEM((128, length), F32)],
        ),
        out_shape=[SDS((t, d), BF)] * 3,
        compiler_params=params(2),
        cost_estimate=cost(40 * t * length * d, t * d * 16, t * length * 12),
        name="attend_back",
    )(tag, q, k, v, do, o, lse)


def grad_qkv_kernel(idx_ref, h_ref, dq_ref, dk_ref, dv_ref, *refs, rows):
    w = dq_ref.shape[1]
    for m, ref in enumerate((dq_ref, dk_ref, dv_ref)):
        at = slice(m * w, (m + 1) * w)
        part = dg(h_ref[...], ref[...], TN)
        if rows is None:
            refs[0][:, at] = part.astype(BF)
        else:
            outs, sum_ref = refs[1:-1], refs[-1]
            q = len(outs)
            sum_ref[...] = part + refs[0][:, at].astype(F32)
            for e in range(q):
                for z in range(4):
                    s = z * q + lax.bitwise_xor(idx_ref[0] % q, jnp.int32(e))
                    outs[e][z, :, at] = sum_ref[pl.ds(pl.multiple_of(s * rows, 8), rows), :].astype(BF)


def grad_qkv(idx, h1, dq, dk, dv, recv=None, n=None):
    t, d = h1.shape
    w = d // 2
    own = recv is not None
    half = pl.BlockSpec((t, w), lambda i, ix: (0, lax.bitwise_xor(ix[1], jnp.int32(0 if own else 1))))
    outs = [(4, d // n, 3 * w)] * (n // 4) if own else [(d, 3 * w)]
    return pl.pallas_call(
        functools.partial(grad_qkv_kernel, rows=d // n if own else None),
        grid_spec=pltpu.PrefetchScalarGridSpec(
            num_scalar_prefetch=1,
            grid=(1,),
            in_specs=[whole((t, d)), half, half, half] + [whole((d, 3 * w))] * own,
            out_specs=[fixed(o) for o in outs],
            scratch_shapes=[pltpu.VMEM((d, w), F32)] * own,
        ),
        out_shape=[SDS(o, BF) for o in outs],
        compiler_params=params(),
        cost_estimate=cost(6 * t * d * w, t * d * 6),
        name="grad_qkv_own" if own else "grad_qkv_other",
    )(idx, h1, dq, dk, dv, *([recv] * own))


def tokens_back_kernel(idx_ref, x_ref, vt_ref, dx2_ref, dq_ref, dk_ref, dv_ref, *refs):
    pieces = refs[:-4]
    tg_ref, s_ref, w_ref, sem = refs[-4:]
    d = x_ref.shape[1]

    @pl.when(pl.program_id(0) == 0)
    def _():
        going = load_qkv(idx_ref, pieces, w_ref, sem)
        s_ref[...] = jnp.zeros_like(s_ref)
        for cp in going:
            cp.wait()

    dh = dg(dq_ref[...], w_ref[:, :d], NT)
    dh = dh + dg(dk_ref[...], w_ref[:, d : 2 * d], NT)
    dh = dh + dg(dv_ref[...], w_ref[:, 2 * d :], NT)
    s_ref[2:3, :] += jnp.sum(dq_ref[...].astype(F32), axis=0, keepdims=True)
    s_ref[3:4, :] += jnp.sum(dv_ref[...].astype(F32), axis=0, keepdims=True)
    c, r = norm_stats(x_ref[...].astype(F32))
    xh = c * r
    s_ref[0:1, :] += jnp.sum(dh * xh, axis=0, keepdims=True)
    s_ref[1:2, :] += jnp.sum(dh, axis=0, keepdims=True)
    dz = dh * vt_ref[0:1, :]
    m1 = jnp.sum(dz, axis=-1, keepdims=True) * (1.0 / d)
    m2 = jnp.sum(dz * xh, axis=-1, keepdims=True) * (1.0 / d)
    tg_ref[...] = dx2_ref[...] + r * (dz - m1 - xh * m2)


def tokens_back(idx, dq, dk, dv, x, vt, dx2, pieces, tb=512):
    t, d = x.shape
    return pl.pallas_call(
        tokens_back_kernel,
        grid_spec=pltpu.PrefetchScalarGridSpec(
            num_scalar_prefetch=1,
            grid=(t // tb,),
            in_specs=[rows_of(tb, d), whole(vt.shape)] + [rows_of(tb, d)] * 4 + [ANY] * len(pieces),
            out_specs=[rows_of(tb, d), fixed((8, d))],
            scratch_shapes=[pltpu.VMEM((d, 3 * d), BF), pltpu.SemaphoreType.DMA],
        ),
        out_shape=[SDS((t, d), F32), SDS((8, d), F32)],
        compiler_params=params(),
        cost_estimate=cost(9 * t * d * d, t * d * 16 + d * d * 6),
        name="tokens_back",
    )(idx, x, vt, dx2, dq, dk, dv, *pieces)


def hop(x, groups):
    return lax.all_to_all(x, "fsdp", split_axis=0, concat_axis=0, tiled=True, axis_index_groups=groups)


def sum_cores_kernel(idx_ref, *refs, q):
    outs = refs[-q:]
    rows = outs[0].shape[1]
    for e in range(q):
        at = lax.bitwise_xor(idx_ref[0] % q, jnp.int32(e))
        start = 0
        for a_ref, b_ref in zip(refs[:-q:2], refs[1:-q:2], strict=True):
            total = (a_ref[at].astype(F32) + b_ref[at].astype(F32)).astype(BF)
            w = total.shape[1]
            for j in range(total.shape[0] // rows):
                outs[e][0, :, start : start + w] = total[j * rows : (j + 1) * rows]
                start += w


def sum_cores(idx, pairs, rows, n):
    q = n // 4
    ops, specs, width = [], [], 0
    for pair in pairs:
        shape = (pair[0].shape[0] // n, pair[0].shape[1])
        width += shape[0] // rows * shape[1]
        ops += [x.reshape((n,) + shape) for x in pair]
        specs += [pl.BlockSpec((q,) + shape, lambda z, _: (z, 0, 0))] * 2
    return pl.pallas_call(
        functools.partial(sum_cores_kernel, q=q),
        grid_spec=pltpu.PrefetchScalarGridSpec(
            num_scalar_prefetch=1,
            grid=(4,),
            in_specs=specs,
            out_specs=[pl.BlockSpec((1, rows, width), lambda z, _: (z, 0, 0))] * q,
        ),
        out_shape=[SDS((4, rows, width), BF)] * q,
        compiler_params=params(),
        cost_estimate=cost(n * rows * width, n * rows * width * 6),
        name="sum_cores",
    )(idx, *ops)


def spread(parts, n):
    return [parts[0]] + [xor_pp(parts[e], e, n) for e in range(1, n // 4)]


def sum_parts_kernel(*refs):
    total = refs[0][...].astype(F32)
    for x in refs[1:-1]:
        total = total + x[...].astype(F32)
    refs[-1][...] = total.astype(BF)


def sum_parts(parts):
    shape = (1,) + parts[0].shape[1:]
    spec = pl.BlockSpec(shape, lambda i: (i, 0, 0))
    return pl.pallas_call(
        sum_parts_kernel,
        grid=(4,),
        in_specs=[spec] * len(parts),
        out_specs=spec,
        out_shape=SDS(parts[0].shape, BF),
        compiler_params=params(),
        cost_estimate=cost(4 * len(parts) * math.prod(shape), 8 * len(parts) * math.prod(shape)),
        name="sum_parts",
    )(*parts)


def sum_qkv_kernel(idx_ref, *refs, q):
    for d in range(4):
        at = lax.bitwise_xor(idx_ref[0] // q, jnp.int32(d))
        start = 0
        for parts in (refs[:q], refs[q : 2 * q]):
            total = parts[0][at].astype(F32)
            for x in parts[1:]:
                total = total + x[at].astype(F32)
            w = total.shape[1]
            refs[2 * q + d][:, start : start + w] = total.astype(BF)
            start += w


def sum_qkv(idx, far, vecs, n):
    _, rows, w = far[0].shape
    width = w + vecs[0].shape[2]
    ops = list(far) + list(vecs)
    near = pl.pallas_call(
        functools.partial(sum_qkv_kernel, q=n // 4),
        grid_spec=pltpu.PrefetchScalarGridSpec(
            num_scalar_prefetch=1,
            grid=(1,),
            in_specs=[whole(x.shape) for x in ops],
            out_specs=[fixed((rows, width))] * 4,
        ),
        out_shape=[SDS((rows, width), BF)] * 4,
        compiler_params=params(),
        cost_estimate=cost(n * rows * width, n * rows * width * 3),
        name="sum_qkv",
    )(idx, *ops)
    return near


def reduce_last(near, n, m):
    total = near[0].astype(F32)
    for x in near[1:]:
        total = total + x.astype(F32)
    return over_pairs(total, m)


def over_pairs(total, m):
    b = 2
    while b < m:
        total = total + lax.ppermute(total.astype(BF), "dp", [(i, i ^ b) for i in range(m)]).astype(F32)
        b *= 2
    return total


def vec_table_kernel(idx_ref, a, c, u, *refs, q):
    table_ref = refs[q]
    d = a.shape[1]
    rows = refs[0].shape[1]
    wide = u.shape[1] // d
    bias = [
        jnp.concatenate(
            [u[:, (s * wide + j) * rows : (s * wide + j + 1) * rows] for s in range(4 * q)], axis=1
        )
        for j in range(wide)
    ]
    lines = [c[0:4, :], a[3:4, :], a[1:3, :], a[0:1, :]] + bias + [jnp.zeros((120 - wide, d), F32)]
    table_ref[...] = jnp.concatenate(lines, axis=0).T
    for e in range(q):
        for z in range(4):
            s = z * q + lax.bitwise_xor(idx_ref[0] % q, jnp.int32(e))
            refs[e][z] = table_ref[pl.ds(pl.multiple_of(s * rows, 8), rows), :].astype(BF)


def vec_table(idx, s_mlp, s_tok, gbu, n):
    d = s_mlp.shape[1]
    q = n // 4
    return pl.pallas_call(
        functools.partial(vec_table_kernel, q=q),
        grid_spec=pltpu.PrefetchScalarGridSpec(
            num_scalar_prefetch=1,
            grid=(1,),
            in_specs=[whole(s_mlp.shape), whole(s_tok.shape), whole(gbu.shape)],
            out_specs=[fixed((4, d // n, 128))] * q,
            scratch_shapes=[pltpu.VMEM((d, 128), F32)],
        ),
        out_shape=[SDS((4, d // n, 128), BF)] * q,
        compiler_params=params(),
        cost_estimate=cost(d * 128, d * 1024),
        name="vec_table",
    )(idx, s_mlp, s_tok, gbu)


def local(
    tokens,
    sensor_tag,
    owner_order,
    ln1_gain,
    ln1_bias,
    w_qkv,
    b_query,
    b_value,
    w_out,
    b_out,
    ln2_gain,
    ln2_bias,
    w_up,
    b_up,
    w_down,
    b_down,
    out_grad,
    *,
    n,
    m,
):
    t, d = tokens.shape
    ff = w_up.shape[1]
    rows = d // n
    wide = ff // d
    f = lax.axis_index("fsdp")
    c = lax.axis_index("dp") % 2
    idx = jnp.stack([f, c]).astype(jnp.int32)
    use = idx if fits(rows, n) else jnp.zeros_like(idx)

    def core_half(x):
        h = x.shape[1] // 2
        return jnp.where(c == 0, x[:, :h], x[:, h:])

    vec = jnp.stack([ln1_gain, ln1_bias, b_query, b_value, b_out, ln2_gain, ln2_bias, b_down], axis=1)
    vec = jnp.concatenate([vec, b_up.reshape(wide, rows).T], axis=1)
    vec = jnp.pad(vec, ((0, 0), (0, 128 - vec.shape[1])))
    shard_a = jnp.concatenate([core_half(w_qkv), vec], axis=1)
    shard_b = jnp.concatenate(
        [core_half(jnp.concatenate([w_out, w_up], axis=1))]
        + [core_half(w_down[j * rows : (j + 1) * rows]) for j in range(wide)],
        axis=1,
    )
    q = n // 4
    everyone = jnp.arange(n)

    near_a = gather_near(shard_a, n)
    near_b = hop(jnp.broadcast_to(after(shard_b, near_a)[None], (4,) + shard_b.shape), tops(n))
    own_a = gather_far(near_a, n)
    cast = after(out_grad, near_a).astype(BF)
    own_a[1:] = after(own_a[1:], cast)
    swap_a = [core_swap(near_a, m), core_swap(jnp.stack(own_a[1:]), m)]
    if fits(rows, n):
        pieces_a = own_a + swap_a
    else:
        pieces_a = settle(own_a + swap_a[:1] + [swap_a[1][e] for e in range(q - 1)], f ^ everyone, c, n)
    near_b = after(near_b, own_a[1:])
    qh, kh, vh, h1, vt, bu = qkv(use, after(tokens, near_b), pieces_a)
    pairs = d // 128
    early = pairs * 2 // 3
    if fits(rows, n):
        first = [near_b[..., : (d + ff) // 2], near_b[..., (d + ff) // 2 :]]
        bits = (1, 2)
        second = [xor_pp(x, b, n) for x, b in zip(first, bits, strict=True)]
        both_b = [jnp.stack([x, y]) for x, y in zip(first, after(second, vt), strict=True)]
        far_b = [xor_pp(x, b, n) for x, b in zip(both_b, bits[::-1], strict=True)]
        part = attend(sensor_tag, after(qh, both_b), kh, vh, 0, early)
        far_b = after(far_b, part[0])
        pieces_b = []
        for x, y in zip(both_b, far_b, strict=True):
            pieces_b += [x, y, core_swap(x, m), core_swap(y, m)]
    else:
        far_b = gather_far(near_b, n)
        side = settle(
            far_b + [core_swap(x, m) for x in far_b], everyone // q * q + (everyone ^ f) % q, c, n, wide
        )
        part = attend(sensor_tag, qh, kh, vh, 0, early)
        cut = (d + ff) // 2
        one = [x[..., :cut] for x in side]
        two = [x[..., cut:] for x in side]
        pieces_b = [jnp.stack(one[i : i + 2]) for i in (0, 2, 4, 6)]
        pieces_b += [jnp.stack([two[i], two[i + 2]]) for i in (0, 1, 4, 5)]
    returned = lax.all_to_all(after(cast, far_b), "fsdp", split_axis=0, concat_axis=0, tiled=True)
    mixed, lse = attend(sensor_tag, qh, kh, vh, early, pairs - early, part)

    x2, active, slope, y = mlp(use, tokens, mixed, vt, bu, pieces_b)
    sent = permute(owner_order, y)
    encoded = lax.all_to_all(sent, "fsdp", split_axis=0, concat_axis=0, tiled=True)

    returned = after(returned, sent)
    dm, du, dx2, do, h2, s_mlp, gbu, out_own, out_other = mlp_back(
        use, owner_order, returned, slope, x2, mixed, vt, pieces_b
    )
    out_recv = core_swap(out_other, m)
    down_own, down_other = grad_down(idx, active, dm)
    down_recv = core_swap(down_other, m)
    up_own, up_other = grad_wide(idx, after(h2, down_own), du, "grad_up")
    up_recv = core_swap(up_other, m)
    encoded = after(encoded, up_own).astype(F32)
    out_recv, down_recv, up_recv = after((out_recv, down_recv, up_recv), encoded)
    pairs = [(up_own, up_recv), (out_own, out_recv), (down_own, down_recv)]
    far_b = sum_cores(idx, pairs, rows, n)
    do = after(do, far_b[0])
    far_b = spread(far_b, n)
    dj = attend_back(sensor_tag, qh, kh, vh, do, mixed, lse, 0, d // 128)
    (qkv_other,) = grad_qkv(idx, h1, *dj)
    qkv_recv = core_swap(qkv_other, m)
    far_b = after(far_b, dj[0])
    near_b = sum_parts([after(far_b[0], qkv_other)] + far_b[1:])
    total_b = hop(near_b, tops(n))
    far_a = grad_qkv(idx, after(h1, near_b), *dj, qkv_recv, n)
    dj = after(dj, far_a[0])
    far_a = spread(far_a, n)
    tokens_grad, s_tok = tokens_back(use, *dj, tokens, vt, dx2, pieces_a)
    far_a, total_b = after((far_a, total_b), tokens_grad)
    total_b = over_pairs(jnp.sum(total_b.astype(F32), axis=0), m).astype(BF)
    other_b = core_swap(total_b, m)
    far_v = spread(vec_table(idx, s_mlp, s_tok, after(gbu, far_a), n), n)

    near_a = sum_qkv(idx, after(far_a, total_b), far_v, n)
    near_a = [near_a[0]] + [xor_pp(near_a[i], i * q, n) for i in range(1, 4)]
    def both(mine, other):
        first = c == 0
        return jnp.where(first, mine, other).astype(F32), jnp.where(first, other, mine).astype(F32)

    def join(pair, start, width, parts, axis=1):
        out = []
        for p in range(parts):
            at = slice(start + p * width, start + (p + 1) * width)
            out.append(jnp.concatenate([pair[0][:, at], pair[1][:, at]], axis=1))
        return jnp.concatenate(out, axis=axis)

    h = d // 2
    g_mlp = both(total_b, other_b)
    grad_up_out = join(g_mlp, 0, h, wide)
    grad_out_out = join(g_mlp, ff // 2, h, 1)
    grad_down_out = join(g_mlp, (d + ff) // 2, h, wide, 0)
    near_a = after(near_a, grad_up_out, grad_out_out, grad_down_out)
    total_a = reduce_last(near_a, n, m)
    other_a = core_swap(total_a.astype(BF), m)
    cut = 3 * d // 2
    vecs = (total_a[:, cut:] + other_a[:, cut:].astype(F32)).T
    total_a, other_a = total_a[:, :cut].astype(BF), other_a[:, :cut]

    grad_qkv_out = join(both(total_a, other_a), 0, h, 3)
    return (
        encoded,
        tokens_grad,
        vecs[0],
        vecs[1],
        grad_qkv_out,
        vecs[2],
        vecs[3],
        grad_out_out,
        vecs[4],
        vecs[5],
        vecs[6],
        grad_up_out,
        vecs[8 : 8 + wide].reshape(ff // n),
        grad_down_out,
        vecs[7],
    )


def solution(mesh):
    n = mesh.shape["fsdp"]
    m = mesh.shape["dp"]
    both = P(("dp", "fsdp"), None)
    vec = P("fsdp")
    mat = P("fsdp", None)
    in_specs = (both, P(("dp", "fsdp")), both, vec, vec, mat, vec, vec, mat, vec, vec, vec, mat, vec, mat, vec, both)
    out_specs = (both, both, vec, vec, mat, vec, vec, mat, vec, vec, vec, mat, vec, mat, vec)
    return jax.shard_map(
        functools.partial(local, n=n, m=m), mesh=mesh, in_specs=in_specs, out_specs=out_specs, check_vma=False
    )
```

time: 479 us -> 469 us (0.979)
  Pallas kernels: 302 us -> 269 us
  starting transfers between devices: 69 us -> 95.1 us
    pallas_call x1, Pallas kernels: 49.8 us -> 31.2 us  [attend_back(): pl.pallas_call(functools.partial(attend_back_kernel, kb=kb, qb=qb), grid_...]
    ppermute x21 -> x22, starting transfers between devices: 30.3 us -> 46.6 us  [xor_pp(): return lax.ppermute(x, 'fsdp', [(i, i ^ b) for i in range(n)])]
    pallas_call x8 -> x7, Pallas kernels: 68 us -> 60.2 us  [the longest x2 21.1 us: grad_qkv(): pl.pallas_call(functools.partial(grad_qkv_kernel, rows=d // n if own else...]
    ppermute x10 -> x12, starting transfers between devices: 13.4 us -> 20.2 us  [core_swap(): return lax.ppermute(x, 'dp', [(i, i ^ 1) for i in range(m)])]
    pallas_call x1, Pallas kernels: 50.3 us -> 44.4 us  [mlp(): pl.pallas_call(functools.partial(mlp_kernel, fc=fc), grid_spec=pltpu.Pref...]
    pallas_call x1 -> x2, Pallas kernels: 34 us -> 28.8 us  [attend(): pl.pallas_call(functools.partial(attend_kernel, qb=qb), grid_spec=pltpu.P...]
    all_to_all x1, starting transfers between devices: 7.25 us -> 12.3 us  [local(): lax.all_to_all(sent, 'fsdp', split_axis=0, concat_axis=0, tiled=True)]
    unnamed x47 -> x67, local copies, waits for them, and re-layouts: 6.65 us -> 10 us
  transfers between devices with their start and end apart: 35 -> 38, of which waited for: 16 -> 16; matrix products, arithmetic and copies ran while one was open for 5% -> 4% of each run, Pallas kernels for 61% -> 57%
where the time goes in v3:
time: 469 us; the launch traced here: 463 us
  Pallas kernels  269 us (57%)
  starting transfers between devices  95.1 us (20%)
  waiting for transfers between devices  61.9 us (13%)
  other arithmetic  18.2 us (4%)
  local copies, waits for them, and re-layouts  17 us (4%)
    pallas_call x1, Pallas kernels, mlp_back(): pl.pallas_call(functools.partial(mlp_back_kernel, fc=fc), grid_spec=pltpu...  51.9 us
    ppermute x22, waiting for transfers between devices, xor_pp(): return lax.ppermute(x, 'fsdp', [(i, i ^ b) for i in range(n)])  47.8 us
    ppermute x22, starting transfers between devices, xor_pp(): return lax.ppermute(x, 'fsdp', [(i, i ^ b) for i in range(n)])  46.6 us
    pallas_call x1, Pallas kernels, mlp(): pl.pallas_call(functools.partial(mlp_kernel, fc=fc), grid_spec=pltpu.Pref...  44.4 us
    pallas_call x1, Pallas kernels, attend_back(): pl.pallas_call(functools.partial(attend_back_kernel, kb=kb, qb=qb), grid_...  31.2 us
    pallas_call x2, Pallas kernels, attend(): pl.pallas_call(functools.partial(attend_kernel, qb=qb), grid_spec=pltpu.P...  28.8 us
    pallas_call x2, Pallas kernels, grad_qkv(): pl.pallas_call(functools.partial(grad_qkv_kernel, rows=d // n if own else...  21.1 us
    ppermute x12, starting transfers between devices, core_swap(): return lax.ppermute(x, 'dp', [(i, i ^ 1) for i in range(m)])  20.2 us
  transfers between devices with their start and end apart: 38, of which 16 were waited for; matrix products, arithmetic and copies ran while one was open for 4% of the time, Pallas kernels for 57%

profile of v3, /device:TPU:0, one launch (start us, length us, event | category | flops | bytes accessed | tf_op | source)
XLA Modules:
  0.0 462.5 jit_solution(828595457961642279)
XLA Ops:
  18.5 5.4 %all-to-all-start = ((bf16[4,48,3456]{2,1,0:T(8,128)(2,1)}), bf16[4,48,3456]{2,1,0:T(8,128)(2,1)S(1)}, u32[]{:S(2)}, u32[]{:S(2)}) async-start(bf16[4,48,3456]{2,1,0:T(8,128)(2,1)} %broadcast_in_dim.2), calls=%async_computation | async-start | bytes 2654208 | tf_op jit(solution)/shard_map/all_to_all | solution.py:665
  32.1 6.8 %collective-permute-done.5.refs_3_ = bf16[4,48,1280]{2,1,0:T(8,128)(2,1)S(1)} collective-permute-done((bf16[4,48,1280]{2,1,0:T(8,128)(2,1)S(1)}, bf16[4,48,1280]{2,1,0:T(8,128)(2,1)S(1)}, u32[]{:S(2)}, u32[]{:S(2)}) %collective-permute-start.5) | collective-permute-done | bytes 491552 | tf_op jit(solution)/shard_map/ppermute | solution.py:64
  39.0 9.2 %collective-permute-done.4.refs_2_ = bf16[4,48,1280]{2,1,0:T(8,128)(2,1)S(1)} collective-permute-done((bf16[4,48,1280]{2,1,0:T(8,128)(2,1)S(1)}, bf16[4,48,1280]{2,1,0:T(8,128)(2,1)S(1)}, u32[]{:S(2)}, u32[]{:S(2)}) %collective-permute-start.4) | collective-permute-done | bytes 491552 | tf_op jit(solution)/shard_map/ppermute | solution.py:64
  49.7 6.1 %all-to-all-done = bf16[4,48,3456]{2,1,0:T(8,128)(2,1)S(1)} async-done(((bf16[4,48,3456]{2,1,0:T(8,128)(2,1)}), bf16[4,48,3456]{2,1,0:T(8,128)(2,1)S(1)}, u32[]{:S(2)}, u32[]{:S(2)}) %all-to-all-start) | async-done | bytes 1327136 | tf_op jit(solution)/shard_map/all_to_all | solution.py:665
  64.9 14.6 %qkv.1 = (bf16[2048,768]{1,0:T(8,128)(2,1)}, bf16[2048,768]{1,0:T(8,128)(2,1)}, bf16[2048,768]{1,0:T(8,128)(2,1)}, bf16[2048,768]{1,0:T(8,128)(2,1)}, f32[16,768]{1,0:T(8,128)}, /*index=5*/f32[1,3072]{1,0:T(1,128)}) custom-call(s32[2]{0:T(128)} %pad_add_fusion.idx_ref, bf16[2048,768]{1,0:T(8,128)(2,1)} %x_ref.4, bf16[4,48,1280]{2,1,0:T(8,128)(2,1)} %copy-done.7, ...), custom_call_target="tpu_custom_call" | custom-call | flops 7077888 | bytes 15744 | tf_op jit(solution)/shard_map/qkv/pallas_call | solution.py:194
  83.3 18.3 %attend.2 = (bf16[2048,768]{1,0:T(8,128)(2,1)}, f32[2,6,2,1024]{3,2,1,0:T(2,128)}) custom-call(s32[2]{0:T(128)} %tag_ref.5, bf16[2048,768]{1,0:T(8,128)(2,1)} %get-tuple-element.119.q_ref, bf16[2048,768]{1,0:T(8,128)(2,1)} %get-tuple-element.114.k_ref, bf16[2048,768]{1,0:T(8,128)(2,1)} %get-tuple-element.115.v_ref), custom_call_target="tpu_custom_call" | custom-call | flops 16777216 | bytes 12288 | tf_op jit(solution)/shard_map/attend/pallas_call | solution.py:258
  101.6 9.1 %collective-permute-done.11.refs_5_ = bf16[2,4,48,1536]{3,2,1,0:T(8,128)(2,1)S(1)} collective-permute-done((bf16[2,4,48,1536]{3,2,1,0:T(8,128)(2,1)S(1)}, bf16[2,4,48,1536]{3,2,1,0:T(8,128)(2,1)S(1)}, u32[]{:S(2)}, u32[]{:S(2)}) %collective-permute-start.11) | collective-permute-done | bytes 1179680 | tf_op jit(solution)/shard_map/ppermute | solution.py:64
  122.5 10.4 %attend.3 = (bf16[2048,768]{1,0:T(8,128)(2,1)}, f32[2,6,2,1024]{3,2,1,0:T(2,128)}) custom-call(s32[2]{0:T(128)} %tag_ref.5, bf16[2048,768]{1,0:T(8,128)(2,1)} %get-tuple-element.119.q_ref, bf16[2048,768]{1,0:T(8,128)(2,1)} %get-tuple-element.114.k_ref, bf16[2048,768]{1,0:T(8,128)(2,1)} %get-tuple-element.115.v_ref, ...), custom_call_target="tpu_custom_call", output_to_operand_aliasing={{0}: (4, {}), {1}: (5, {})} | custom-call | flops 8388608 | bytes 12288 | tf_op jit(solution)/shard_map/attend/pallas_call | solution.py:258
  134.6 44.4 %mlp.1 = (f32[2048,768]{1,0:T(8,128)}, bf16[2048,3072]{1,0:T(8,128)(2,1)}, bf16[2048,3072]{1,0:T(8,128)(2,1)}, bf16[2048,768]{1,0:T(8,128)(2,1)}) custom-call(s32[2]{0:T(128)} %pad_add_fusion.idx_ref, bf16[2048,768]{1,0:T(8,128)(2,1)} %x_ref.4, bf16[2048,768]{1,0:T(8,128)(2,1)} %get-tuple-element.122.o_ref, f32[16,768]{1,0:T(8,128)} %get-tuple-element.116.vt_ref, ...), custom_call_target="tpu_custom_call" | custom-call | flops 42467328 | bytes 49152 | tf_op jit(solution)/shard_map/mlp/pallas_call | solution.py:318
  179.0 11.0 %permute.1 = bf16[2048,768]{1,0:T(8,128)(2,1)} custom-call(s32[1,2048]{1,0:T(1,128)} %ord_ref.3, bf16[2048,768]{1,0:T(8,128)(2,1)} %get-tuple-element.126.y_ref), custom_call_target="tpu_custom_call" | custom-call | flops 6291456 | bytes 6144 | tf_op jit(solution)/shard_map/permute/pallas_call | solution.py:348
  190.0 12.3 %all-to-all-start.1 = ((bf16[16,128,768]{2,1,0:T(8,128)(2,1)}), bf16[16,128,768]{2,1,0:T(8,128)(2,1)S(1)}, u32[]{:S(2)}, u32[]{:S(2)}) async-start(bf16[16,128,768]{2,1,0:T(8,128)(2,1)} %bitcast.37), calls=%async_computation.1 | async-start | bytes 6291456 | tf_op jit(solution)/shard_map/all_to_all | solution.py:905
  202.3 51.9 %mlp_back.1 = (bf16[2048,768]{1,0:T(8,128)(2,1)}, bf16[2048,3072]{1,0:T(8,128)(2,1)}, f32[2048,768]{1,0:T(8,128)}, bf16[2048,768]{1,0:T(8,128)(2,1)}, bf16[2048,...) custom-call(s32[2]{0:T(128)} %pad_add_fusion.idx_ref, ...), custom_call_target="tpu_custom_call" | custom-call | flops 41287680 | bytes 55296 | tf_op jit(solution)/shard_map/mlp_back/pallas_call | solution.py:421
  254.3 15.2 %grad_down.1 = (bf16[3072,384]{1,0:T(8,128)(2,1)}, bf16[3072,384]{1,0:T(8,128)(2,1)}) custom-call(s32[2]{0:T(128)} %pad_add_fusion.idx_ref, bf16[2048,3072]{1,0:T(8,128)(2,1)} %get-tuple-element.132.g_ref, bf16[2048,768]{1,0:T(8,128)(2,1)} %get-tuple-element.133.dm_ref), custom_call_target="tpu_custom_call" | custom-call | flops 14155776 | bytes 19968 | tf_op jit(solution)/shard_map/grad_down/pallas_call | solution.py:463
  269.5 15.3 %grad_up.1 = (bf16[768,1536]{1,0:T(8,128)(2,1)}, bf16[768,1536]{1,0:T(8,128)(2,1)}) custom-call(s32[2]{0:T(128)} %pad_add_fusion.idx_ref, bf16[2048,768]{1,0:T(8,128)(2,1)} %get-tuple-element.135.a_ref, bf16[2048,3072]{1,0:T(8,128)(2,1)} %get-tuple-element.136.b_ref), custom_call_target="tpu_custom_call" | custom-call | flops 14155776 | bytes 19968 | tf_op jit(solution)/shard_map/grad_up/pallas_call | solution.py:485
  288.5 5.4 %collective-permute-done.16 = bf16[768,384]{1,0:T(8,128)(2,1)} collective-permute-done((bf16[768,384]{1,0:T(8,128)(2,1)}, bf16[768,384]{1,0:T(8,128)(2,1)}, u32[]{:S(2)}, u32[]{:S(2)}) %collective-permute-start.16) | collective-permute-done | bytes 589856 | tf_op jit(solution)/shard_map/ppermute | solution.py:68
  293.9 7.3 %sum_cores.1 = (bf16[4,48,3456]{2,1,0:T(8,128)(2,1)}, bf16[4,48,3456]{2,1,0:T(8,128)(2,1)}, bf16[4,48,3456]{2,1,0:T(8,128)(2,1)}, bf16[4,48,3456]{2,1,0:T(8,128)(2,1)}) custom-call(s32[2]{0:T(128)} %pad_add_fusion.idx_ref, bf16[16,48,1536]{2,1,0:T(8,128)(2,1)} %bitcast.44, bf16[16,48,1536]{2,1,0:T(8,128)(2,1)} %bitcast.27.refs_1_, ...), custom_call_target="tpu_custom_call" | custom-call | flops 2592 | bytes 15552 | tf_op jit(solution)/shard_map/sum_cores/pallas_call | solution.py:690
  304.8 31.2 %attend_back.1 = (bf16[2048,768]{1,0:T(8,128)(2,1)}, bf16[2048,768]{1,0:T(8,128)(2,1)}, bf16[2048,768]{1,0:T(8,128)(2,1)}) custom-call(s32[2]{0:T(128)} %tag_ref.5, bf16[2048,768]{1,0:T(8,128)(2,1)} %get-tuple-element.119.q_ref, bf16[2048,768]{1,0:T(8,128)(2,1)} %get-tuple-element.114.k_ref, bf16[2048,768]{1,0:T(8,128)(2,1)} %get-tuple-element.115.v_ref, ...), custom_call_target="tpu_custom_call" | custom-call | flops 62914560 | bytes 24576 | tf_op jit(solution)/shard_map/attend_back/pallas_call | solution.py:564
  335.9 10.2 %grad_qkv_other.1 = bf16[768,1152]{1,0:T(8,128)(2,1)} custom-call(s32[2]{0:T(128)} %pad_add_fusion.idx_ref, bf16[2048,768]{1,0:T(8,128)(2,1)} %get-tuple-element.163.h_ref, bf16[2048,768]{1,0:T(8,128)(2,1)} %get-tuple-element.165.dq_ref, bf16[2048,768]{1,0:T(8,128)(2,1)} %get-tuple-element.166.dk_ref, bf16[2048,768]{1,0:T(8,128)(2,1)} %get-tuple-element.167.dv_ref), custom_call_target="tpu_custom_call" | custom-call | flops 3538944 | bytes 9216 | tf_op jit(solution)/shard_map/grad_qkv_other/pallas_call | solution.py:603
  346.2 18.4 %collective-permute-start.22 = (bf16[768,1152]{1,0:T(8,128)(2,1)}, bf16[768,1152]{1,0:T(8,128)(2,1)S(1)}, u32[]{:S(2)}, u32[]{:S(2)}) collective-permute-start(bf16[768,1152]{1,0:T(8,128)(2,1)} %grad_qkv_other.1), channel_id=1, source_target_pairs={{0,16},{16,0},{1,17},{17,1},{2,18},{18,2},{3,19},{19,3},{4,20},{20... | collective-permute-start | bytes 5308424 | tf_op jit(solution)/shard_map/ppermute | solution.py:68
  371.7 5.7 %all-to-all-start.3 = ((bf16[4,48,3456]{2,1,0:T(8,128)(2,1)}), bf16[4,48,3456]{2,1,0:T(8,128)(2,1)S(1)}, u32[]{:S(2)}, u32[]{:S(2)}) async-start(bf16[4,48,3456]{2,1,0:T(8,128)(2,1)} %sum_parts.1), calls=%async_computation.3 | async-start | bytes 2654208 | tf_op jit(solution)/shard_map/all_to_all | solution.py:665
  378.6 10.8 %grad_qkv_own.1 = (bf16[4,48,1152]{2,1,0:T(8,128)(2,1)}, bf16[4,48,1152]{2,1,0:T(8,128)(2,1)}, bf16[4,48,1152]{2,1,0:T(8,128)(2,1)}, bf16[4,48,1152]{2,1,0:T(8,128)(2,1)}) custom-call(s32[2]{0:T(128)} %pad_add_fusion.idx_ref, bf16[2048,768]{1,0:T(8,128)(2,1)} %get-tuple-element.163.h_ref, bf16[2048,768]{1,0:T(8,128)(2,1)} %get-tuple-element.165.dq_ref, ...), custom_call_target="tpu_custom_call" | custom-call | flops 3538944 | bytes 9216 | tf_op jit(solution)/shard_map/grad_qkv_own/pallas_call | solution.py:603
  389.5 20.3 %collective-permute-start.23 = (bf16[4,48,1152]{2,1,0:T(8,128)(2,1)}, bf16[4,48,1152]{2,1,0:T(8,128)(2,1)S(1)}, u32[]{:S(2)}, u32[]{:S(2)}) collective-permute-start(bf16[4,48,1152]{2,1,0:T(8,128)(2,1)} %get-tuple-element.169), channel_id=1, source_target_pairs={{0,1},{1,0},{2,3},{3,2},{4,5},{5,4},{6,7},{7,6},{8,9},{9,8},{10,11... | collective-permute-start | bytes 1327112 | tf_op jit(solution)/shard_map/ppermute | solution.py:64
  411.3 18.1 %tokens_back.1 = (f32[2048,768]{1,0:T(8,128)}, f32[8,768]{1,0:T(8,128)}) custom-call(s32[2]{0:T(128)} %pad_add_fusion.idx_ref, bf16[2048,768]{1,0:T(8,128)(2,1)} %x_ref.4, f32[16,768]{1,0:T(8,128)} %get-tuple-element.116.vt_ref, f32[2048,768]{1,0:T(8,128)} %get-tuple-element.139.dx2_ref, bf16[2048,768]{1,0:T(8,128)(2,1)} %get-tuple-element.165.dq_ref, ...), custom_call_target="tpu_custom_call" | custom-call | flops 10616832 | bytes 28032 | tf_op jit(solution)/shard_map/tokens_back/pallas_call | solution.py:648
  451.1 7.0 %collective-permute-done.30 = bf16[48,1280]{1,0:T(8,128)(2,1)S(1)} collective-permute-done((bf16[48,1280]{1,0:T(8,128)(2,1)}, bf16[48,1280]{1,0:T(8,128)(2,1)S(1)}, u32[]{:S(2)}, u32[]{:S(2)}) %collective-permute-start.30) | collective-permute-done | bytes 122912 | tf_op jit(solution)/shard_map/ppermute | solution.py:64
  (169 shorter events, 96.3 us)
Async XLA Ops:
  3.4 11.7 %collective-permute-start.1 = (bf16[48,1280]{1,0:T(8,128)(2,1)S(1)}, bf16[48,1280]{1,0:T(8,128)(2,1)S(1)}, u32[]{:S(2)}, u32[]{:S(2)}) collective-permute-start(bf16[48,1280]{1,0:T(8,128)(2,1)S(1)} %get-tuple-element.228), channel_id=1, source_target_pairs={{0,8},{1,9},{2,10},{3,11},{4,12},{5,13},{6,14},{7,15},{8,0},{9,1},... | collective-permute-start | bytes 368648 | tf_op jit(solution)/shard_map/ppermute | solution.py:64
  18.5 37.3 %all-to-all-start = ((bf16[4,48,3456]{2,1,0:T(8,128)(2,1)}), bf16[4,48,3456]{2,1,0:T(8,128)(2,1)S(1)}, u32[]{:S(2)}, u32[]{:S(2)}) async-start(bf16[4,48,3456]{2,1,0:T(8,128)(2,1)} %broadcast_in_dim.2), calls=%async_computation | async-start | bytes 2654208 | tf_op jit(solution)/shard_map/all_to_all | solution.py:665
  23.9 15.1 %collective-permute-start.5 = (bf16[4,48,1280]{2,1,0:T(8,128)(2,1)S(1)}, bf16[4,48,1280]{2,1,0:T(8,128)(2,1)S(1)}, u32[]{:S(2)}, u32[]{:S(2)}) collective-permute-start(bf16[4,48,1280]{2,1,0:T(8,128)(2,1)S(1)} %pad_maximum_fusion.3.refs_0_), channel_id=1, source_target_pairs={{0,3},{1,2},{2,1},{3,0},{4,7},{5,6},{6,5},{7,4},{8,11},{9,10},{10,... | collective-permute-start | bytes 1474568 | tf_op jit(solution)/shard_map/ppermute | solution.py:64
  26.3 21.8 %collective-permute-start.4 = (bf16[4,48,1280]{2,1,0:T(8,128)(2,1)S(1)}, bf16[4,48,1280]{2,1,0:T(8,128)(2,1)S(1)}, u32[]{:S(2)}, u32[]{:S(2)}) collective-permute-start(bf16[4,48,1280]{2,1,0:T(8,128)(2,1)S(1)} %pad_maximum_fusion.3.refs_0_), channel_id=1, source_target_pairs={{0,2},{1,3},{2,0},{3,1},{4,6},{5,7},{6,4},{7,5},{8,10},{9,11},{10,... | collective-permute-start | bytes 1474568 | tf_op jit(solution)/shard_map/ppermute | solution.py:64
  26.9 21.4 %collective-permute-start.3 = (bf16[4,48,1280]{2,1,0:T(8,128)(2,1)S(1)}, bf16[4,48,1280]{2,1,0:T(8,128)(2,1)S(1)}, u32[]{:S(2)}, u32[]{:S(2)}) collective-permute-start(bf16[4,48,1280]{2,1,0:T(8,128)(2,1)S(1)} %pad_maximum_fusion.3.refs_0_), channel_id=1, source_target_pairs={{0,1},{1,0},{2,3},{3,2},{4,5},{5,4},{6,7},{7,6},{8,9},{9,8},{10,11... | collective-permute-start | bytes 1474568 | tf_op jit(solution)/shard_map/ppermute | solution.py:64
  49.6 13.3 %collective-permute-start.7 = (bf16[3,4,48,1280]{3,2,1,0:T(8,128)(2,1)}, bf16[3,4,48,1280]{3,2,1,0:T(8,128)(2,1)S(1)}, u32[]{:S(2)}, u32[]{:S(2)}) collective-permute-start(bf16[3,4,48,1280]{3,2,1,0:T(8,128)(2,1)} %pad_maximum_fusion), channel_id=1, source_target_pairs={{0,16},{16,0},{1,17},{17,1},{2,18},{18,2},{3,19},{19,3},{4,20},{20... | collective-permute-start | bytes 4423688 | tf_op jit(solution)/shard_map/ppermute | solution.py:68
  57.0 22.6 %collective-permute-start.8 = (bf16[4,48,1920]{2,1,0:T(8,128)(2,1)}, bf16[4,48,1920]{2,1,0:T(8,128)(2,1)}, u32[]{:S(2)}, u32[]{:S(2)}) collective-permute-start(bf16[4,48,1920]{2,1,0:T(8,128)(2,1)} %get-tuple-element.210), channel_id=1, source_target_pairs={{0,1},{1,0},{2,3},{3,2},{4,5},{5,4},{6,7},{7,6},{8,9},{9,8},{10,11... | collective-permute-start | bytes 2211848 | tf_op jit(solution)/shard_map/ppermute | solution.py:64
  59.6 20.0 %collective-permute-start.9 = (bf16[4,48,1536]{2,1,0:T(8,128)(2,1)}, bf16[4,48,1536]{2,1,0:T(8,128)(2,1)}, u32[]{:S(2)}, u32[]{:S(2)}) collective-permute-start(bf16[4,48,1536]{2,1,0:T(8,128)(2,1)} %get-tuple-element.208), channel_id=1, source_target_pairs={{0,2},{1,3},{2,0},{3,1},{4,6},{5,7},{6,4},{7,5},{8,10},{9,11},{10,... | collective-permute-start | bytes 1769480 | tf_op jit(solution)/shard_map/ppermute | solution.py:64
  80.9 34.4 %collective-permute-start.10 = (bf16[2,4,48,1920]{3,2,1,0:T(8,128)(2,1)S(1)}, bf16[2,4,48,1920]{3,2,1,0:T(8,128)(2,1)S(1)}, u32[]{:S(2)}, u32[]{:S(2)}) collective-permute-start(bf16[2,4,48,1920]{3,2,1,0:T(8,128)(2,1)S(1)} %pad_maximum_fusion.1.refs_0_), channel_id=1, source_target_pairs={{0,2},{1,3},{2,0},{3,1},{4,6},{5,7},{6,4},{7,5},{8,10},{9,11},{10,... | collective-permute-start | bytes 4423688 | tf_op jit(solution)/shard_map/ppermute | solution.py:64
  82.7 28.0 %collective-permute-start.11 = (bf16[2,4,48,1536]{3,2,1,0:T(8,128)(2,1)S(1)}, bf16[2,4,48,1536]{3,2,1,0:T(8,128)(2,1)S(1)}, u32[]{:S(2)}, u32[]{:S(2)}) collective-permute-start(bf16[2,4,48,1536]{3,2,1,0:T(8,128)(2,1)S(1)} %pad_maximum_fusion.2.refs_4_), channel_id=1, source_target_pairs={{0,1},{1,0},{2,3},{3,2},{4,5},{5,4},{6,7},{7,6},{8,9},{9,8},{10,11... | collective-permute-start | bytes 3538952 | tf_op jit(solution)/shard_map/ppermute | solution.py:64
  116.4 73.6 %all-to-all-start.2 = ((bf16[16,128,768]{2,1,0:T(8,128)(2,1)}), bf16[16,128,768]{2,1,0:T(8,128)(2,1)}, u32[]{:S(2)}, u32[]{:S(2)}) async-start(bf16[16,128,768]{2,1,0:T(8,128)(2,1)} %bitcast.38), calls=%async_computation.2 | async-start | bytes 6291456 | tf_op jit(solution)/shard_map/all_to_all | solution.py:900
  121.4 11.5 %collective-permute-start.12 = (bf16[2,4,48,1920]{3,2,1,0:T(8,128)(2,1)S(1)}, bf16[2,4,48,1920]{3,2,1,0:T(8,128)(2,1)S(1)}, u32[]{:S(2)}, u32[]{:S(2)}) collective-permute-start(bf16[2,4,48,1920]{3,2,1,0:T(8,128)(2,1)S(1)} %pad_maximum_fusion.1.refs_0_), channel_id=1, source_target_pairs={{0,16},{16,0},{1,17},{17,1},{2,18},{18,2},{3,19},{19,3},{4,20},{20... | collective-permute-start | bytes 4423688 | tf_op jit(solution)/shard_map/ppermute | solution.py:68
  121.5 11.5 %collective-permute-start.13 = (bf16[2,4,48,1920]{3,2,1,0:T(8,128)(2,1)}, bf16[2,4,48,1920]{3,2,1,0:T(8,128)(2,1)}, u32[]{:S(2)}, u32[]{:S(2)}) collective-permute-start(bf16[2,4,48,1920]{3,2,1,0:T(8,128)(2,1)} %copy-done.3), channel_id=1, source_target_pairs={{0,16},{16,0},{1,17},{17,1},{2,18},{18,2},{3,19},{19,3},{4,20},{20... | collective-permute-start | bytes 4423688 | tf_op jit(solution)/shard_map/ppermute | solution.py:68
  190.0 95.3 %all-to-all-start.1 = ((bf16[16,128,768]{2,1,0:T(8,128)(2,1)}), bf16[16,128,768]{2,1,0:T(8,128)(2,1)S(1)}, u32[]{:S(2)}, u32[]{:S(2)}) async-start(bf16[16,128,768]{2,1,0:T(8,128)(2,1)} %bitcast.37), calls=%async_computation.1 | async-start | bytes 6291456 | tf_op jit(solution)/shard_map/all_to_all | solution.py:905
  301.2 63.3 %collective-permute-start.19 = (bf16[4,48,3456]{2,1,0:T(8,128)(2,1)}, bf16[4,48,3456]{2,1,0:T(8,128)(2,1)S(1)}, u32[]{:S(2)}, u32[]{:S(2)}) collective-permute-start(bf16[4,48,3456]{2,1,0:T(8,128)(2,1)} %get-tuple-element.155), channel_id=1, source_target_pairs={{0,1},{1,0},{2,3},{3,2},{4,5},{5,4},{6,7},{7,6},{8,9},{9,8},{10,11... | collective-permute-start | bytes 3981320 | tf_op jit(solution)/shard_map/ppermute | solution.py:64
  303.2 61.3 %collective-permute-start.20 = (bf16[4,48,3456]{2,1,0:T(8,128)(2,1)}, bf16[4,48,3456]{2,1,0:T(8,128)(2,1)S(1)}, u32[]{:S(2)}, u32[]{:S(2)}) collective-permute-start(bf16[4,48,3456]{2,1,0:T(8,128)(2,1)} %get-tuple-element.156), channel_id=1, source_target_pairs={{0,2},{1,3},{2,0},{3,1},{4,6},{5,7},{6,4},{7,5},{8,10},{9,11},{10,... | collective-permute-start | bytes 3981320 | tf_op jit(solution)/shard_map/ppermute | solution.py:64
  304.7 59.9 %collective-permute-start.21 = (bf16[4,48,3456]{2,1,0:T(8,128)(2,1)}, bf16[4,48,3456]{2,1,0:T(8,128)(2,1)S(1)}, u32[]{:S(2)}, u32[]{:S(2)}) collective-permute-start(bf16[4,48,3456]{2,1,0:T(8,128)(2,1)} %get-tuple-element.157), channel_id=1, source_target_pairs={{0,3},{1,2},{2,1},{3,0},{4,7},{5,6},{6,5},{7,4},{8,11},{9,10},{10,... | collective-permute-start | bytes 3981320 | tf_op jit(solution)/shard_map/ppermute | solution.py:64
  346.2 31.3 %collective-permute-start.22 = (bf16[768,1152]{1,0:T(8,128)(2,1)}, bf16[768,1152]{1,0:T(8,128)(2,1)S(1)}, u32[]{:S(2)}, u32[]{:S(2)}) collective-permute-start(bf16[768,1152]{1,0:T(8,128)(2,1)} %grad_qkv_other.1), channel_id=1, source_target_pairs={{0,16},{16,0},{1,17},{17,1},{2,18},{18,2},{3,19},{19,3},{4,20},{20... | collective-permute-start | bytes 5308424 | tf_op jit(solution)/shard_map/ppermute | solution.py:68
  371.7 59.8 %all-to-all-start.3 = ((bf16[4,48,3456]{2,1,0:T(8,128)(2,1)}), bf16[4,48,3456]{2,1,0:T(8,128)(2,1)S(1)}, u32[]{:S(2)}, u32[]{:S(2)}) async-start(bf16[4,48,3456]{2,1,0:T(8,128)(2,1)} %sum_parts.1), calls=%async_computation.3 | async-start | bytes 2654208 | tf_op jit(solution)/shard_map/all_to_all | solution.py:665
  389.5 39.8 %collective-permute-start.23 = (bf16[4,48,1152]{2,1,0:T(8,128)(2,1)}, bf16[4,48,1152]{2,1,0:T(8,128)(2,1)S(1)}, u32[]{:S(2)}, u32[]{:S(2)}) collective-permute-start(bf16[4,48,1152]{2,1,0:T(8,128)(2,1)} %get-tuple-element.169), channel_id=1, source_target_pairs={{0,1},{1,0},{2,3},{3,2},{4,5},{5,4},{6,7},{7,6},{8,9},{9,8},{10,11... | collective-permute-start | bytes 1327112 | tf_op jit(solution)/shard_map/ppermute | solution.py:64
  409.8 21.7 %collective-permute-start.24 = (bf16[4,48,1152]{2,1,0:T(8,128)(2,1)}, bf16[4,48,1152]{2,1,0:T(8,128)(2,1)S(1)}, u32[]{:S(2)}, u32[]{:S(2)}) collective-permute-start(bf16[4,48,1152]{2,1,0:T(8,128)(2,1)} %get-tuple-element.170), channel_id=1, source_target_pairs={{0,2},{1,3},{2,0},{3,1},{4,6},{5,7},{6,4},{7,5},{8,10},{9,11},{10,... | collective-permute-start | bytes 1327112 | tf_op jit(solution)/shard_map/ppermute | solution.py:64
  411.2 20.2 %collective-permute-start.25 = (bf16[4,48,1152]{2,1,0:T(8,128)(2,1)}, bf16[4,48,1152]{2,1,0:T(8,128)(2,1)S(1)}, u32[]{:S(2)}, u32[]{:S(2)}) collective-permute-start(bf16[4,48,1152]{2,1,0:T(8,128)(2,1)} %get-tuple-element.171), channel_id=1, source_target_pairs={{0,3},{1,2},{2,1},{3,0},{4,7},{5,6},{6,5},{7,4},{8,11},{9,10},{10,... | collective-permute-start | bytes 1327112 | tf_op jit(solution)/shard_map/ppermute | solution.py:64
  431.7 17.5 %collective-permute-start.32 = (bf16[48,3456]{1,0:T(8,128)(2,1)S(1)}, bf16[48,3456]{1,0:T(8,128)(2,1)S(1)}, u32[]{:S(2)}, u32[]{:S(2)}) collective-permute-start(bf16[48,3456]{1,0:T(8,128)(2,1)S(1)} %reduce_sum.12), channel_id=1, source_target_pairs={{0,16},{16,0},{1,17},{17,1},{2,18},{18,2},{3,19},{19,3},{4,20},{20... | collective-permute-start | bytes 995336 | tf_op jit(solution)/shard_map/ppermute | solution.py:68
  446.5 11.5 %collective-permute-start.30 = (bf16[48,1280]{1,0:T(8,128)(2,1)}, bf16[48,1280]{1,0:T(8,128)(2,1)S(1)}, u32[]{:S(2)}, u32[]{:S(2)}) collective-permute-start(bf16[48,1280]{1,0:T(8,128)(2,1)} %get-tuple-element.191), channel_id=1, source_target_pairs={{0,8},{1,9},{2,10},{3,11},{4,12},{5,13},{6,14},{7,15},{8,0},{9,1},... | collective-permute-start | bytes 368648 | tf_op jit(solution)/shard_map/ppermute | solution.py:64
  (42 other events, 338.6 us)

commit v4 on v3

--- a/solution.py
+++ b/solution.py
@@ -350,7 +350,7 @@
         grid=(t // jb,),
         in_specs=[pl.BlockSpec((1, jb), lambda i: (0, i)), whole((t, d))],
         out_specs=rows_of(jb, d),
-        out_shape=SDS((t, d), BF),
+        out_shape=pltpu.HBM((t, d), BF),
         compiler_params=params(),
         cost_estimate=cost(2 * t * t * d, t * d * 4),
         name="permute",
@@ -444,8 +444,8 @@
             SDS((t, d), BF),
             SDS((8, d), F32),
             SDS((1, ff), F32),
-            SDS((d, d // 2), BF),
-            SDS((d, d // 2), BF),
+            pltpu.HBM((d, d // 2), BF),
+            pltpu.HBM((d, d // 2), BF),
         ],
         compiler_params=params(),
         cost_estimate=cost(2 * t * d * (d + 2 * ff + t) * 1.5, t * (20 * d + 4 * ff)),
@@ -468,7 +468,7 @@
             in_specs=[pl.BlockSpec((t, mb), lambda i, _: (0, i)), whole((t, d))],
             out_specs=[rows_of(mb, d // 2)] * 2,
         ),
-        out_shape=[SDS((ff, d // 2), BF)] * 2,
+        out_shape=[pltpu.HBM((ff, d // 2), BF)] * 2,
         compiler_params=params(),
         cost_estimate=cost(3 * t * ff * d, 2 * t * (ff + d) + 2 * ff * d),
         name="grad_down",
@@ -490,7 +490,7 @@
             in_specs=[whole((t, d)), pl.BlockSpec((t, d), lambda i, _: (0, i))],
             out_specs=[pl.BlockSpec((d, d // 2), lambda i, _: (0, i))] * 2,
         ),
-        out_shape=[SDS((d, width // 2), BF)] * 2,
+        out_shape=[pltpu.HBM((d, width // 2), BF)] * 2,
         compiler_params=params(),
         cost_estimate=cost(3 * t * width * d, 2 * t * (width + d) + 2 * width * d),
         name=name,
@@ -498,8 +498,9 @@
 
 
 def attend_back_kernel(
-    tag_ref, q_ref, k_ref, v_ref, do_ref, o_ref, l_ref, dq_ref, dk_ref, dv_ref, dl_ref, dqt_ref, *, kb, qb
+    tag_ref, q_ref, k_ref, v_ref, do_ref, o_ref, l_ref, *refs, kb, qb
 ):
+    dq_ref, dk_ref, dv_ref, dl_ref, dqt_ref = refs[-5:]
     r = pl.program_id(0)
     length = q_ref.shape[0]
     low = lax.broadcasted_iota(jnp.int32, (1, 128), 1) < 64
@@ -553,28 +554,27 @@
         run(c, c, [(ks, [ks]) for ks in range(0, length, c)])
 
 
-def attend_back(tag, q, k, v, do, o, lse, first, pairs, kb=512, qb=512):
-    t = q.shape[0]
-    d = pairs * 128
+def attend_back(tag, q, k, v, do, o, lse, first, pairs, before=(), kb=512, qb=512):
+    t, d = q.shape
     rows = tag.shape[0]
     length = t // rows
     blk = pl.BlockSpec((length, 128), lambda r, p, _: (r, p + first))
-    out = pl.BlockSpec((length, 128), lambda r, p, _: (r, p))
     lse_spec = pl.BlockSpec((1, 1, 2, length), lambda r, p, _: (r, p + first, 0, 0))
     return pl.pallas_call(
         functools.partial(attend_back_kernel, kb=kb, qb=qb),
         grid_spec=pltpu.PrefetchScalarGridSpec(
             num_scalar_prefetch=1,
             grid=(rows, pairs),
-            in_specs=[blk] * 5 + [lse_spec],
-            out_specs=[out] * 3,
+            in_specs=[blk] * 5 + [lse_spec] + [ANY] * len(before),
+            out_specs=[blk] * 3,
             scratch_shapes=[pltpu.VMEM((2, length), F32), pltpu.VMEM((128, length), F32)],
         ),
         out_shape=[SDS((t, d), BF)] * 3,
+        input_output_aliases={7: 0, 8: 1, 9: 2} if before else {},
         compiler_params=params(2),
-        cost_estimate=cost(40 * t * length * d, t * d * 16, t * length * 12),
+        cost_estimate=cost(5120 * t * length * pairs, t * d * 16, t * length * 12),
         name="attend_back",
-    )(tag, q, k, v, do, o, lse)
+    )(tag, q, k, v, do, o, lse, *before)
 
 
 def grad_qkv_kernel(idx_ref, h_ref, dq_ref, dk_ref, dv_ref, *refs, rows):
@@ -609,7 +609,7 @@
             out_specs=[fixed(o) for o in outs],
             scratch_shapes=[pltpu.VMEM((d, w), F32)] * own,
         ),
-        out_shape=[SDS(o, BF) for o in outs],
+        out_shape=[pltpu.HBM(o, BF) for o in outs],
         compiler_params=params(),
         cost_estimate=cost(6 * t * d * w, t * d * 6),
         name="grad_qkv_own" if own else "grad_qkv_other",
@@ -672,7 +672,7 @@
         at = lax.bitwise_xor(idx_ref[0] % q, jnp.int32(e))
         start = 0
         for a_ref, b_ref in zip(refs[:-q:2], refs[1:-q:2], strict=True):
-            total = (a_ref[at].astype(F32) + b_ref[at].astype(F32)).astype(BF)
+            total = a_ref[at] + b_ref[at]
             w = total.shape[1]
             for j in range(total.shape[0] // rows):
                 outs[e][0, :, start : start + w] = total[j * rows : (j + 1) * rows]
@@ -695,7 +695,7 @@
             in_specs=specs,
             out_specs=[pl.BlockSpec((1, rows, width), lambda z, _: (z, 0, 0))] * q,
         ),
-        out_shape=[SDS((4, rows, width), BF)] * q,
+        out_shape=[pltpu.HBM((4, rows, width), BF)] * q,
         compiler_params=params(),
         cost_estimate=cost(n * rows * width, n * rows * width * 6),
         name="sum_cores",
@@ -721,7 +721,7 @@
         grid=(4,),
         in_specs=[spec] * len(parts),
         out_specs=spec,
-        out_shape=SDS(parts[0].shape, BF),
+        out_shape=pltpu.HBM(parts[0].shape, BF),
         compiler_params=params(),
         cost_estimate=cost(4 * len(parts) * math.prod(shape), 8 * len(parts) * math.prod(shape)),
         name="sum_parts",
@@ -753,7 +753,7 @@
             in_specs=[whole(x.shape) for x in ops],
             out_specs=[fixed((rows, width))] * 4,
         ),
-        out_shape=[SDS((rows, width), BF)] * 4,
+        out_shape=[pltpu.HBM((rows, width), BF)] * 4,
         compiler_params=params(),
         cost_estimate=cost(n * rows * width, n * rows * width * 3),
         name="sum_qkv",
@@ -913,13 +913,13 @@
     down_recv = core_swap(down_other, m)
     up_own, up_other = grad_wide(idx, after(h2, down_own), du, "grad_up")
     up_recv = core_swap(up_other, m)
-    encoded = after(encoded, up_own).astype(F32)
-    out_recv, down_recv, up_recv = after((out_recv, down_recv, up_recv), encoded)
-    pairs = [(up_own, up_recv), (out_own, out_recv), (down_own, down_recv)]
-    far_b = sum_cores(idx, pairs, rows, n)
+    part = attend_back(sensor_tag, qh, kh, vh, after(do, up_own, encoded), mixed, lse, 0, 1)
+    out_recv, down_recv, up_recv = after((out_recv, down_recv, up_recv), part[0])
+    pairs_b = [(up_own, up_recv), (out_own, out_recv), (down_own, down_recv)]
+    far_b = sum_cores(idx, pairs_b, rows, n)
     do = after(do, far_b[0])
     far_b = spread(far_b, n)
-    dj = attend_back(sensor_tag, qh, kh, vh, do, mixed, lse, 0, d // 128)
+    dj = attend_back(sensor_tag, qh, kh, vh, do, mixed, lse, 1, pairs - 1, part)
     (qkv_other,) = grad_qkv(idx, h1, *dj)
     qkv_recv = core_swap(qkv_other, m)
     far_b = after(far_b, dj[0])
@@ -935,6 +935,7 @@
     far_v = spread(vec_table(idx, s_mlp, s_tok, after(gbu, far_a), n), n)
 
     near_a = sum_qkv(idx, after(far_a, total_b), far_v, n)
+    encoded = after(encoded, near_a[0]).astype(F32)
     near_a = [near_a[0]] + [xor_pp(near_a[i], i * q, n) for i in range(1, 4)]
     def both(mine, other):
         first = c == 0
@@ -952,7 +953,7 @@
     grad_up_out = join(g_mlp, 0, h, wide)
     grad_out_out = join(g_mlp, ff // 2, h, 1)
     grad_down_out = join(g_mlp, (d + ff) // 2, h, wide, 0)
-    near_a = after(near_a, grad_up_out, grad_out_out, grad_down_out)
+    near_a = after(near_a, grad_up_out, grad_out_out, grad_down_out, encoded)
     total_a = reduce_last(near_a, n, m)
     other_a = core_swap(total_a.astype(BF), m)
     cut = 3 * d // 2

time: 469 us -> 464 us (0.989)
  Pallas kernels: 269 us -> 299 us
  starting transfers between devices: 95.1 us -> 72.8 us
  waiting for transfers between devices: 61.9 us -> 48.6 us
    pallas_call x1 -> x2, Pallas kernels: 31.2 us -> 53.1 us  [attend_back(): pl.pallas_call(functools.partial(attend_back_kernel, kb=kb, qb=qb), grid_...]
    ppermute x22, starting transfers between devices: 46.6 us -> 31.5 us  [xor_pp(): return lax.ppermute(x, 'fsdp', [(i, i ^ b) for i in range(n)])]
    ppermute x22, waiting for transfers between devices: 47.8 us -> 39.9 us  [xor_pp(): return lax.ppermute(x, 'fsdp', [(i, i ^ b) for i in range(n)])]
    pallas_call x2, Pallas kernels: 28.8 us -> 36.5 us  [attend(): pl.pallas_call(functools.partial(attend_kernel, qb=qb), grid_spec=pltpu.P...]
    ppermute x12, waiting for transfers between devices: 8.01 us -> 2.62 us  [core_swap(): return lax.ppermute(x, 'dp', [(i, i ^ 1) for i in range(m)])]
    unnamed x67 -> x57, local copies, waits for them, and re-layouts: 10 us -> 7.45 us
  transfers between devices with their start and end apart: 38 -> 38, of which waited for: 16 -> 16; matrix products, arithmetic and copies ran while one was open for 4% -> 4% of each run, Pallas kernels for 57% -> 64%
where the time goes in v4:
time: 464 us; the launch traced here: 455 us
  Pallas kernels  299 us (64%)
  starting transfers between devices  72.8 us (16%)
  waiting for transfers between devices  48.6 us (10%)
  other arithmetic  19.4 us (4%)
  local copies, waits for them, and re-layouts  14.4 us (3%)
    pallas_call x2, Pallas kernels, attend_back(): pl.pallas_call(functools.partial(attend_back_kernel, kb=kb, qb=qb), grid_...  53.1 us
    pallas_call x1, Pallas kernels, mlp_back(): pl.pallas_call(functools.partial(mlp_back_kernel, fc=fc), grid_spec=pltpu...  51.9 us
    pallas_call x1, Pallas kernels, mlp(): pl.pallas_call(functools.partial(mlp_kernel, fc=fc), grid_spec=pltpu.Pref...  44.4 us
    ppermute x22, waiting for transfers between devices, xor_pp(): return lax.ppermute(x, 'fsdp', [(i, i ^ b) for i in range(n)])  39.9 us
    pallas_call x2, Pallas kernels, attend(): pl.pallas_call(functools.partial(attend_kernel, qb=qb), grid_spec=pltpu.P...  36.5 us
    ppermute x22, starting transfers between devices, xor_pp(): return lax.ppermute(x, 'fsdp', [(i, i ^ b) for i in range(n)])  31.5 us
    pallas_call x2, Pallas kernels, grad_qkv(): pl.pallas_call(functools.partial(grad_qkv_kernel, rows=d // n if own else...  21 us
    pallas_call x1, Pallas kernels, tokens_back(): pl.pallas_call(tokens_back_kernel, grid_spec=pltpu.PrefetchScalarGridSpec...  18.1 us
  transfers between devices with their start and end apart: 38, of which 16 were waited for; matrix products, arithmetic and copies ran while one was open for 4% of the time, Pallas kernels for 64%

profile of v4, /device:TPU:0, one launch (start us, length us, event | category | flops | bytes accessed | tf_op | source)
XLA Modules:
  0.0 455.4 jit_solution(12342405299250734445)
XLA Ops:
  18.5 5.4 %all-to-all-start = ((bf16[4,48,3456]{2,1,0:T(8,128)(2,1)}), bf16[4,48,3456]{2,1,0:T(8,128)(2,1)S(1)}, u32[]{:S(2)}, u32[]{:S(2)}) async-start(bf16[4,48,3456]{2,1,0:T(8,128)(2,1)} %broadcast_in_dim.2), calls=%async_computation | async-start | bytes 2654208 | tf_op jit(solution)/shard_map/all_to_all | solution.py:665
  27.4 4.7 %convert_element_type.41 = bf16[2048,768]{1,0:T(8,128)(2,1)} convert(f32[2048,768]{1,0:T(8,128)} %param.33) | non-fusion elementwise | flops 1572864 | bytes 9437184 | tf_op jit(solution)/shard_map/convert_element_type | solution.py:867
  32.1 6.8 %collective-permute-done.5.refs_3_ = bf16[4,48,1280]{2,1,0:T(8,128)(2,1)S(1)} collective-permute-done((bf16[4,48,1280]{2,1,0:T(8,128)(2,1)S(1)}, bf16[4,48,1280]{2,1,0:T(8,128)(2,1)S(1)}, u32[]{:S(2)}, u32[]{:S(2)}) %collective-permute-start.5) | collective-permute-done | bytes 491552 | tf_op jit(solution)/shard_map/ppermute | solution.py:64
  39.0 9.2 %collective-permute-done.4.refs_2_ = bf16[4,48,1280]{2,1,0:T(8,128)(2,1)S(1)} collective-permute-done((bf16[4,48,1280]{2,1,0:T(8,128)(2,1)S(1)}, bf16[4,48,1280]{2,1,0:T(8,128)(2,1)S(1)}, u32[]{:S(2)}, u32[]{:S(2)}) %collective-permute-start.4) | collective-permute-done | bytes 491552 | tf_op jit(solution)/shard_map/ppermute | solution.py:64
  49.7 6.1 %all-to-all-done = bf16[4,48,3456]{2,1,0:T(8,128)(2,1)S(1)} async-done(((bf16[4,48,3456]{2,1,0:T(8,128)(2,1)}), bf16[4,48,3456]{2,1,0:T(8,128)(2,1)S(1)}, u32[]{:S(2)}, u32[]{:S(2)}) %all-to-all-start) | async-done | bytes 1327136 | tf_op jit(solution)/shard_map/all_to_all | solution.py:665
  64.9 14.6 %qkv.1 = (bf16[2048,768]{1,0:T(8,128)(2,1)}, bf16[2048,768]{1,0:T(8,128)(2,1)}, bf16[2048,768]{1,0:T(8,128)(2,1)}, bf16[2048,768]{1,0:T(8,128)(2,1)}, f32[16,768]{1,0:T(8,128)}, /*index=5*/f32[1,3072]{1,0:T(1,128)}) custom-call(s32[2]{0:T(128)} %pad_add_fusion.idx_ref, bf16[2048,768]{1,0:T(8,128)(2,1)} %x_ref.4, bf16[4,48,1280]{2,1,0:T(8,128)(2,1)} %copy-done.7, ...), custom_call_target="tpu_custom_call" | custom-call | flops 7077888 | bytes 15744 | tf_op jit(solution)/shard_map/qkv/pallas_call | solution.py:194
  83.2 23.5 %attend.2 = (bf16[2048,768]{1,0:T(8,128)(2,1)}, f32[2,6,2,1024]{3,2,1,0:T(2,128)}) custom-call(s32[2]{0:T(128)} %tag_ref.7, bf16[2048,768]{1,0:T(8,128)(2,1)} %get-tuple-element.123.q_ref, bf16[2048,768]{1,0:T(8,128)(2,1)} %get-tuple-element.118.k_ref, bf16[2048,768]{1,0:T(8,128)(2,1)} %get-tuple-element.119.v_ref), custom_call_target="tpu_custom_call" | custom-call | flops 16777216 | bytes 12288 | tf_op jit(solution)/shard_map/attend/pallas_call | solution.py:258
  110.6 4.6 %collective-permute-done.10.refs_1_ = bf16[2,4,48,1920]{3,2,1,0:T(8,128)(2,1)S(1)} collective-permute-done((bf16[2,4,48,1920]{3,2,1,0:T(8,128)(2,1)S(1)}, bf16[2,4,48,1920]{3,2,1,0:T(8,128)(2,1)S(1)}, u32[]{:S(2)}, u32[]{:S(2)}) %collective-permute-start.10) | collective-permute-done | bytes 1474592 | tf_op jit(solution)/shard_map/ppermute | solution.py:64
  116.4 4.7 %all-to-all-start.2 = ((bf16[16,128,768]{2,1,0:T(8,128)(2,1)}), bf16[16,128,768]{2,1,0:T(8,128)(2,1)}, u32[]{:S(2)}, u32[]{:S(2)}) async-start(bf16[16,128,768]{2,1,0:T(8,128)(2,1)} %bitcast.39), calls=%async_computation.2 | async-start | bytes 6291456 | tf_op jit(solution)/shard_map/all_to_all | solution.py:900
  122.2 13.0 %attend.3 = (bf16[2048,768]{1,0:T(8,128)(2,1)}, f32[2,6,2,1024]{3,2,1,0:T(2,128)}) custom-call(s32[2]{0:T(128)} %tag_ref.7, bf16[2048,768]{1,0:T(8,128)(2,1)} %get-tuple-element.123.q_ref, bf16[2048,768]{1,0:T(8,128)(2,1)} %get-tuple-element.118.k_ref, bf16[2048,768]{1,0:T(8,128)(2,1)} %get-tuple-element.119.v_ref, ...), custom_call_target="tpu_custom_call", output_to_operand_aliasing={{0}: (4, {}), {1}: (5, {})} | custom-call | flops 8388608 | bytes 12288 | tf_op jit(solution)/shard_map/attend/pallas_call | solution.py:258
  136.7 44.4 %mlp.1 = (f32[2048,768]{1,0:T(8,128)}, bf16[2048,3072]{1,0:T(8,128)(2,1)}, bf16[2048,3072]{1,0:T(8,128)(2,1)}, bf16[2048,768]{1,0:T(8,128)(2,1)}) custom-call(s32[2]{0:T(128)} %pad_add_fusion.idx_ref, bf16[2048,768]{1,0:T(8,128)(2,1)} %x_ref.4, bf16[2048,768]{1,0:T(8,128)(2,1)} %get-tuple-element.126.o_ref, f32[16,768]{1,0:T(8,128)} %get-tuple-element.120.vt_ref, ...), custom_call_target="tpu_custom_call" | custom-call | flops 42467328 | bytes 49152 | tf_op jit(solution)/shard_map/mlp/pallas_call | solution.py:318
  181.1 11.1 %permute.1 = bf16[2048,768]{1,0:T(8,128)(2,1)} custom-call(s32[1,2048]{1,0:T(1,128)} %ord_ref.3, bf16[2048,768]{1,0:T(8,128)(2,1)} %get-tuple-element.130.y_ref), custom_call_target="tpu_custom_call" | custom-call | flops 6291456 | bytes 6144 | tf_op jit(solution)/shard_map/permute/pallas_call | solution.py:348
  192.2 9.0 %all-to-all-start.1 = ((bf16[16,128,768]{2,1,0:T(8,128)(2,1)}), bf16[16,128,768]{2,1,0:T(8,128)(2,1)S(1)}, u32[]{:S(2)}, u32[]{:S(2)}) async-start(bf16[16,128,768]{2,1,0:T(8,128)(2,1)} %bitcast.37), calls=%async_computation.1 | async-start | bytes 6291456 | tf_op jit(solution)/shard_map/all_to_all | solution.py:905
  201.2 51.9 %mlp_back.1 = (bf16[2048,768]{1,0:T(8,128)(2,1)}, bf16[2048,3072]{1,0:T(8,128)(2,1)}, f32[2048,768]{1,0:T(8,128)}, bf16[2048,768]{1,0:T(8,128)(2,1)}, bf16[2048,...) custom-call(s32[2]{0:T(128)} %pad_add_fusion.idx_ref, ...), custom_call_target="tpu_custom_call" | custom-call | flops 41287680 | bytes 55296 | tf_op jit(solution)/shard_map/mlp_back/pallas_call | solution.py:421
  253.2 15.2 %grad_down.1 = (bf16[3072,384]{1,0:T(8,128)(2,1)}, bf16[3072,384]{1,0:T(8,128)(2,1)}) custom-call(s32[2]{0:T(128)} %pad_add_fusion.idx_ref, bf16[2048,3072]{1,0:T(8,128)(2,1)} %get-tuple-element.137.g_ref, bf16[2048,768]{1,0:T(8,128)(2,1)} %get-tuple-element.138.dm_ref), custom_call_target="tpu_custom_call" | custom-call | flops 14155776 | bytes 19968 | tf_op jit(solution)/shard_map/grad_down/pallas_call | solution.py:463
  268.4 15.4 %grad_up.1 = (bf16[768,1536]{1,0:T(8,128)(2,1)}, bf16[768,1536]{1,0:T(8,128)(2,1)}) custom-call(s32[2]{0:T(128)} %pad_add_fusion.idx_ref, bf16[2048,768]{1,0:T(8,128)(2,1)} %get-tuple-element.140.a_ref, bf16[2048,3072]{1,0:T(8,128)(2,1)} %get-tuple-element.141.b_ref), custom_call_target="tpu_custom_call" | custom-call | flops 14155776 | bytes 19968 | tf_op jit(solution)/shard_map/grad_up/pallas_call | solution.py:485
  284.3 10.9 %attend_back.2 = (bf16[2048,768]{1,0:T(8,128)(2,1)}, bf16[2048,768]{1,0:T(8,128)(2,1)}, bf16[2048,768]{1,0:T(8,128)(2,1)}) custom-call(s32[2]{0:T(128)} %tag_ref.7, bf16[2048,768]{1,0:T(8,128)(2,1)} %get-tuple-element.123.q_ref, bf16[2048,768]{1,0:T(8,128)(2,1)} %get-tuple-element.118.k_ref, bf16[2048,768]{1,0:T(8,128)(2,1)} %get-tuple-element.119.v_ref, ...), custom_call_target="tpu_custom_call" | custom-call | flops 10485760 | bytes 24576 | tf_op jit(solution)/shard_map/attend_back/pallas_call | solution.py:563
  295.2 7.3 %sum_cores.1 = (bf16[4,48,3456]{2,1,0:T(8,128)(2,1)}, bf16[4,48,3456]{2,1,0:T(8,128)(2,1)}, bf16[4,48,3456]{2,1,0:T(8,128)(2,1)}, bf16[4,48,3456]{2,1,0:T(8,128)(2,1)}) custom-call(s32[2]{0:T(128)} %pad_add_fusion.idx_ref, bf16[16,48,1536]{2,1,0:T(8,128)(2,1)} %bitcast.44, bf16[16,48,1536]{2,1,0:T(8,128)(2,1)} %bitcast.27.refs_1_, ...), custom_call_target="tpu_custom_call" | custom-call | flops 2592 | bytes 15552 | tf_op jit(solution)/shard_map/sum_cores/pallas_call | solution.py:690
  309.2 42.2 %attend_back.3 = (bf16[2048,768]{1,0:T(8,128)(2,1)}, bf16[2048,768]{1,0:T(8,128)(2,1)}, bf16[2048,768]{1,0:T(8,128)(2,1)}) custom-call(s32[2]{0:T(128)} %tag_ref.7, bf16[2048,768]{1,0:T(8,128)(2,1)} %get-tuple-element.123.q_ref, bf16[2048,768]{1,0:T(8,128)(2,1)} %get-tuple-element.118.k_ref, ...), custom_call_target="tpu_custom_call", output_to_operand_aliasing={{0}: (7, {}), {1}: (8, {}), {2}: (9, {})} | custom-call | flops 52428800 | bytes 24576 | tf_op jit(solution)/shard_map/attend_back/pallas_call | solution.py:563
  351.4 10.2 %grad_qkv_other.1 = bf16[768,1152]{1,0:T(8,128)(2,1)} custom-call(s32[2]{0:T(128)} %pad_add_fusion.idx_ref, bf16[2048,768]{1,0:T(8,128)(2,1)} %get-tuple-element.169.h_ref, bf16[2048,768]{1,0:T(8,128)(2,1)} %get-tuple-element.175.dq_ref, bf16[2048,768]{1,0:T(8,128)(2,1)} %get-tuple-element.176.dk_ref, bf16[2048,768]{1,0:T(8,128)(2,1)} %get-tuple-element.177.dv_ref), custom_call_target="tpu_custom_call" | custom-call | flops 3538944 | bytes 9216 | tf_op jit(solution)/shard_map/grad_qkv_other/pallas_call | solution.py:603
  361.6 15.8 %collective-permute-start.22 = (bf16[768,1152]{1,0:T(8,128)(2,1)}, bf16[768,1152]{1,0:T(8,128)(2,1)}, u32[]{:S(2)}, u32[]{:S(2)}) collective-permute-start(bf16[768,1152]{1,0:T(8,128)(2,1)} %grad_qkv_other.1), channel_id=1, source_target_pairs={{0,16},{16,0},{1,17},{17,1},{2,18},{18,2},{3,19},{19,3},{4,20},{20... | collective-permute-start | bytes 5308424 | tf_op jit(solution)/shard_map/ppermute | solution.py:68
  383.3 4.6 %all-to-all-start.3 = ((bf16[4,48,3456]{2,1,0:T(8,128)(2,1)}), bf16[4,48,3456]{2,1,0:T(8,128)(2,1)}, u32[]{:S(2)}, u32[]{:S(2)}) async-start(bf16[4,48,3456]{2,1,0:T(8,128)(2,1)} %sum_parts.1), calls=%async_computation.3 | async-start | bytes 2654208 | tf_op jit(solution)/shard_map/all_to_all | solution.py:665
  387.9 10.8 %grad_qkv_own.1 = (bf16[4,48,1152]{2,1,0:T(8,128)(2,1)}, bf16[4,48,1152]{2,1,0:T(8,128)(2,1)}, bf16[4,48,1152]{2,1,0:T(8,128)(2,1)}, bf16[4,48,1152]{2,1,0:T(8,128)(2,1)}) custom-call(s32[2]{0:T(128)} %pad_add_fusion.idx_ref, bf16[2048,768]{1,0:T(8,128)(2,1)} %get-tuple-element.169.h_ref, bf16[2048,768]{1,0:T(8,128)(2,1)} %get-tuple-element.175.dq_ref, ...), custom_call_target="tpu_custom_call" | custom-call | flops 3538944 | bytes 9216 | tf_op jit(solution)/shard_map/grad_qkv_own/pallas_call | solution.py:603
  402.3 18.1 %tokens_back.1 = (f32[2048,768]{1,0:T(8,128)}, f32[8,768]{1,0:T(8,128)}) custom-call(s32[2]{0:T(128)} %pad_add_fusion.idx_ref, bf16[2048,768]{1,0:T(8,128)(2,1)} %x_ref.4, f32[16,768]{1,0:T(8,128)} %get-tuple-element.120.vt_ref, f32[2048,768]{1,0:T(8,128)} %get-tuple-element.174.dx2_ref, bf16[2048,768]{1,0:T(8,128)(2,1)} %get-tuple-element.175.dq_ref, ...), custom_call_target="tpu_custom_call" | custom-call | flops 10616832 | bytes 28032 | tf_op jit(solution)/shard_map/tokens_back/pallas_call | solution.py:648
  (160 shorter events, 94.3 us)
Async XLA Ops:
  18.5 37.3 %all-to-all-start = ((bf16[4,48,3456]{2,1,0:T(8,128)(2,1)}), bf16[4,48,3456]{2,1,0:T(8,128)(2,1)S(1)}, u32[]{:S(2)}, u32[]{:S(2)}) async-start(bf16[4,48,3456]{2,1,0:T(8,128)(2,1)} %broadcast_in_dim.2), calls=%async_computation | async-start | bytes 2654208 | tf_op jit(solution)/shard_map/all_to_all | solution.py:665
  23.9 15.1 %collective-permute-start.5 = (bf16[4,48,1280]{2,1,0:T(8,128)(2,1)S(1)}, bf16[4,48,1280]{2,1,0:T(8,128)(2,1)S(1)}, u32[]{:S(2)}, u32[]{:S(2)}) collective-permute-start(bf16[4,48,1280]{2,1,0:T(8,128)(2,1)S(1)} %pad_maximum_fusion.3.refs_0_), channel_id=1, source_target_pairs={{0,3},{1,2},{2,1},{3,0},{4,7},{5,6},{6,5},{7,4},{8,11},{9,10},{10,... | collective-permute-start | bytes 1474568 | tf_op jit(solution)/shard_map/ppermute | solution.py:64
  26.3 21.8 %collective-permute-start.4 = (bf16[4,48,1280]{2,1,0:T(8,128)(2,1)S(1)}, bf16[4,48,1280]{2,1,0:T(8,128)(2,1)S(1)}, u32[]{:S(2)}, u32[]{:S(2)}) collective-permute-start(bf16[4,48,1280]{2,1,0:T(8,128)(2,1)S(1)} %pad_maximum_fusion.3.refs_0_), channel_id=1, source_target_pairs={{0,2},{1,3},{2,0},{3,1},{4,6},{5,7},{6,4},{7,5},{8,10},{9,11},{10,... | collective-permute-start | bytes 1474568 | tf_op jit(solution)/shard_map/ppermute | solution.py:64
  26.9 21.4 %collective-permute-start.3 = (bf16[4,48,1280]{2,1,0:T(8,128)(2,1)S(1)}, bf16[4,48,1280]{2,1,0:T(8,128)(2,1)S(1)}, u32[]{:S(2)}, u32[]{:S(2)}) collective-permute-start(bf16[4,48,1280]{2,1,0:T(8,128)(2,1)S(1)} %pad_maximum_fusion.3.refs_0_), channel_id=1, source_target_pairs={{0,1},{1,0},{2,3},{3,2},{4,5},{5,4},{6,7},{7,6},{8,9},{9,8},{10,11... | collective-permute-start | bytes 1474568 | tf_op jit(solution)/shard_map/ppermute | solution.py:64
  49.6 13.3 %collective-permute-start.7 = (bf16[3,4,48,1280]{3,2,1,0:T(8,128)(2,1)}, bf16[3,4,48,1280]{3,2,1,0:T(8,128)(2,1)S(1)}, u32[]{:S(2)}, u32[]{:S(2)}) collective-permute-start(bf16[3,4,48,1280]{3,2,1,0:T(8,128)(2,1)} %pad_maximum_fusion), channel_id=1, source_target_pairs={{0,16},{16,0},{1,17},{17,1},{2,18},{18,2},{3,19},{19,3},{4,20},{20... | collective-permute-start | bytes 4423688 | tf_op jit(solution)/shard_map/ppermute | solution.py:68
  57.0 22.5 %collective-permute-start.8 = (bf16[4,48,1920]{2,1,0:T(8,128)(2,1)}, bf16[4,48,1920]{2,1,0:T(8,128)(2,1)}, u32[]{:S(2)}, u32[]{:S(2)}) collective-permute-start(bf16[4,48,1920]{2,1,0:T(8,128)(2,1)} %get-tuple-element.218), channel_id=1, source_target_pairs={{0,1},{1,0},{2,3},{3,2},{4,5},{5,4},{6,7},{7,6},{8,9},{9,8},{10,11... | collective-permute-start | bytes 2211848 | tf_op jit(solution)/shard_map/ppermute | solution.py:64
  59.6 19.9 %collective-permute-start.9 = (bf16[4,48,1536]{2,1,0:T(8,128)(2,1)}, bf16[4,48,1536]{2,1,0:T(8,128)(2,1)}, u32[]{:S(2)}, u32[]{:S(2)}) collective-permute-start(bf16[4,48,1536]{2,1,0:T(8,128)(2,1)} %get-tuple-element.216), channel_id=1, source_target_pairs={{0,2},{1,3},{2,0},{3,1},{4,6},{5,7},{6,4},{7,5},{8,10},{9,11},{10,... | collective-permute-start | bytes 1769480 | tf_op jit(solution)/shard_map/ppermute | solution.py:64
  80.9 34.4 %collective-permute-start.10 = (bf16[2,4,48,1920]{3,2,1,0:T(8,128)(2,1)S(1)}, bf16[2,4,48,1920]{3,2,1,0:T(8,128)(2,1)S(1)}, u32[]{:S(2)}, u32[]{:S(2)}) collective-permute-start(bf16[2,4,48,1920]{3,2,1,0:T(8,128)(2,1)S(1)} %pad_maximum_fusion.1.refs_0_), channel_id=1, source_target_pairs={{0,2},{1,3},{2,0},{3,1},{4,6},{5,7},{6,4},{7,5},{8,10},{9,11},{10,... | collective-permute-start | bytes 4423688 | tf_op jit(solution)/shard_map/ppermute | solution.py:64
  82.6 28.0 %collective-permute-start.11 = (bf16[2,4,48,1536]{3,2,1,0:T(8,128)(2,1)S(1)}, bf16[2,4,48,1536]{3,2,1,0:T(8,128)(2,1)S(1)}, u32[]{:S(2)}, u32[]{:S(2)}) collective-permute-start(bf16[2,4,48,1536]{3,2,1,0:T(8,128)(2,1)S(1)} %pad_maximum_fusion.2.refs_4_), channel_id=1, source_target_pairs={{0,1},{1,0},{2,3},{3,2},{4,5},{5,4},{6,7},{7,6},{8,9},{9,8},{10,11... | collective-permute-start | bytes 3538952 | tf_op jit(solution)/shard_map/ppermute | solution.py:64
  116.4 75.8 %all-to-all-start.2 = ((bf16[16,128,768]{2,1,0:T(8,128)(2,1)}), bf16[16,128,768]{2,1,0:T(8,128)(2,1)}, u32[]{:S(2)}, u32[]{:S(2)}) async-start(bf16[16,128,768]{2,1,0:T(8,128)(2,1)} %bitcast.39), calls=%async_computation.2 | async-start | bytes 6291456 | tf_op jit(solution)/shard_map/all_to_all | solution.py:900
  121.1 14.1 %collective-permute-start.12 = (bf16[2,4,48,1920]{3,2,1,0:T(8,128)(2,1)S(1)}, bf16[2,4,48,1920]{3,2,1,0:T(8,128)(2,1)S(1)}, u32[]{:S(2)}, u32[]{:S(2)}) collective-permute-start(bf16[2,4,48,1920]{3,2,1,0:T(8,128)(2,1)S(1)} %pad_maximum_fusion.1.refs_0_), channel_id=1, source_target_pairs={{0,16},{16,0},{1,17},{17,1},{2,18},{18,2},{3,19},{19,3},{4,20},{20... | collective-permute-start | bytes 4423688 | tf_op jit(solution)/shard_map/ppermute | solution.py:68
  121.2 14.1 %collective-permute-start.13 = (bf16[2,4,48,1920]{3,2,1,0:T(8,128)(2,1)}, bf16[2,4,48,1920]{3,2,1,0:T(8,128)(2,1)}, u32[]{:S(2)}, u32[]{:S(2)}) collective-permute-start(bf16[2,4,48,1920]{3,2,1,0:T(8,128)(2,1)} %copy-done.3), channel_id=1, source_target_pairs={{0,16},{16,0},{1,17},{17,1},{2,18},{18,2},{3,19},{19,3},{4,20},{20... | collective-permute-start | bytes 4423688 | tf_op jit(solution)/shard_map/ppermute | solution.py:68
  121.7 13.5 %collective-permute-start.14 = (bf16[2,4,48,1536]{3,2,1,0:T(8,128)(2,1)S(1)}, bf16[2,4,48,1536]{3,2,1,0:T(8,128)(2,1)S(1)}, u32[]{:S(2)}, u32[]{:S(2)}) collective-permute-start(bf16[2,4,48,1536]{3,2,1,0:T(8,128)(2,1)S(1)} %pad_maximum_fusion.2.refs_4_), channel_id=1, source_target_pairs={{0,16},{16,0},{1,17},{17,1},{2,18},{18,2},{3,19},{19,3},{4,20},{20... | collective-permute-start | bytes 3538952 | tf_op jit(solution)/shard_map/ppermute | solution.py:68
  121.7 13.5 %collective-permute-start.15 = (bf16[2,4,48,1536]{3,2,1,0:T(8,128)(2,1)}, bf16[2,4,48,1536]{3,2,1,0:T(8,128)(2,1)}, u32[]{:S(2)}, u32[]{:S(2)}) collective-permute-start(bf16[2,4,48,1536]{3,2,1,0:T(8,128)(2,1)} %copy-done.5), channel_id=1, source_target_pairs={{0,16},{16,0},{1,17},{17,1},{2,18},{18,2},{3,19},{19,3},{4,20},{20... | collective-permute-start | bytes 3538952 | tf_op jit(solution)/shard_map/ppermute | solution.py:68
  192.2 92.1 %all-to-all-start.1 = ((bf16[16,128,768]{2,1,0:T(8,128)(2,1)}), bf16[16,128,768]{2,1,0:T(8,128)(2,1)S(1)}, u32[]{:S(2)}, u32[]{:S(2)}) async-start(bf16[16,128,768]{2,1,0:T(8,128)(2,1)} %bitcast.37), calls=%async_computation.1 | async-start | bytes 6291456 | tf_op jit(solution)/shard_map/all_to_all | solution.py:905
  302.5 74.9 %collective-permute-start.19 = (bf16[4,48,3456]{2,1,0:T(8,128)(2,1)}, bf16[4,48,3456]{2,1,0:T(8,128)(2,1)S(1)}, u32[]{:S(2)}, u32[]{:S(2)}) collective-permute-start(bf16[4,48,3456]{2,1,0:T(8,128)(2,1)} %get-tuple-element.155), channel_id=1, source_target_pairs={{0,1},{1,0},{2,3},{3,2},{4,5},{5,4},{6,7},{7,6},{8,9},{9,8},{10,11... | collective-permute-start | bytes 3981320 | tf_op jit(solution)/shard_map/ppermute | solution.py:64
  304.6 72.8 %collective-permute-start.20 = (bf16[4,48,3456]{2,1,0:T(8,128)(2,1)}, bf16[4,48,3456]{2,1,0:T(8,128)(2,1)S(1)}, u32[]{:S(2)}, u32[]{:S(2)}) collective-permute-start(bf16[4,48,3456]{2,1,0:T(8,128)(2,1)} %get-tuple-element.156), channel_id=1, source_target_pairs={{0,2},{1,3},{2,0},{3,1},{4,6},{5,7},{6,4},{7,5},{8,10},{9,11},{10,... | collective-permute-start | bytes 3981320 | tf_op jit(solution)/shard_map/ppermute | solution.py:64
  307.8 69.6 %collective-permute-start.21 = (bf16[4,48,3456]{2,1,0:T(8,128)(2,1)}, bf16[4,48,3456]{2,1,0:T(8,128)(2,1)}, u32[]{:S(2)}, u32[]{:S(2)}) collective-permute-start(bf16[4,48,3456]{2,1,0:T(8,128)(2,1)} %get-tuple-element.157), channel_id=1, source_target_pairs={{0,3},{1,2},{2,1},{3,0},{4,7},{5,6},{6,5},{7,4},{8,11},{9,10},{10,... | collective-permute-start | bytes 3981320 | tf_op jit(solution)/shard_map/ppermute | solution.py:64
  361.6 26.3 %collective-permute-start.22 = (bf16[768,1152]{1,0:T(8,128)(2,1)}, bf16[768,1152]{1,0:T(8,128)(2,1)}, u32[]{:S(2)}, u32[]{:S(2)}) collective-permute-start(bf16[768,1152]{1,0:T(8,128)(2,1)} %grad_qkv_other.1), channel_id=1, source_target_pairs={{0,16},{16,0},{1,17},{17,1},{2,18},{18,2},{3,19},{19,3},{4,20},{20... | collective-permute-start | bytes 5308424 | tf_op jit(solution)/shard_map/ppermute | solution.py:68
  383.3 39.1 %all-to-all-start.3 = ((bf16[4,48,3456]{2,1,0:T(8,128)(2,1)}), bf16[4,48,3456]{2,1,0:T(8,128)(2,1)}, u32[]{:S(2)}, u32[]{:S(2)}) async-start(bf16[4,48,3456]{2,1,0:T(8,128)(2,1)} %sum_parts.1), calls=%async_computation.3 | async-start | bytes 2654208 | tf_op jit(solution)/shard_map/all_to_all | solution.py:665
  398.7 21.7 %collective-permute-start.23 = (bf16[4,48,1152]{2,1,0:T(8,128)(2,1)}, bf16[4,48,1152]{2,1,0:T(8,128)(2,1)}, u32[]{:S(2)}, u32[]{:S(2)}) collective-permute-start(bf16[4,48,1152]{2,1,0:T(8,128)(2,1)} %get-tuple-element.171), channel_id=1, source_target_pairs={{0,1},{1,0},{2,3},{3,2},{4,5},{5,4},{6,7},{7,6},{8,9},{9,8},{10,11... | collective-permute-start | bytes 1327112 | tf_op jit(solution)/shard_map/ppermute | solution.py:64
  400.4 20.2 %collective-permute-start.24 = (bf16[4,48,1152]{2,1,0:T(8,128)(2,1)}, bf16[4,48,1152]{2,1,0:T(8,128)(2,1)}, u32[]{:S(2)}, u32[]{:S(2)}) collective-permute-start(bf16[4,48,1152]{2,1,0:T(8,128)(2,1)} %get-tuple-element.172), channel_id=1, source_target_pairs={{0,2},{1,3},{2,0},{3,1},{4,6},{5,7},{6,4},{7,5},{8,10},{9,11},{10,... | collective-permute-start | bytes 1327112 | tf_op jit(solution)/shard_map/ppermute | solution.py:64
  400.9 21.6 %collective-permute-start.25 = (bf16[4,48,1152]{2,1,0:T(8,128)(2,1)}, bf16[4,48,1152]{2,1,0:T(8,128)(2,1)}, u32[]{:S(2)}, u32[]{:S(2)}) collective-permute-start(bf16[4,48,1152]{2,1,0:T(8,128)(2,1)} %get-tuple-element.173), channel_id=1, source_target_pairs={{0,3},{1,2},{2,1},{3,0},{4,7},{5,6},{6,5},{7,4},{8,11},{9,10},{10,... | collective-permute-start | bytes 1327112 | tf_op jit(solution)/shard_map/ppermute | solution.py:64
  424.0 21.3 %collective-permute-start.32 = (bf16[48,3456]{1,0:T(8,128)(2,1)S(1)}, bf16[48,3456]{1,0:T(8,128)(2,1)S(1)}, u32[]{:S(2)}, u32[]{:S(2)}) collective-permute-start(bf16[48,3456]{1,0:T(8,128)(2,1)S(1)} %reduce_sum.12), channel_id=1, source_target_pairs={{0,16},{16,0},{1,17},{17,1},{2,18},{18,2},{3,19},{19,3},{4,20},{20... | collective-permute-start | bytes 995336 | tf_op jit(solution)/shard_map/ppermute | solution.py:68
  (37 other events, 310.7 us)
